TPU v7x, 32 devices: a whole 2x2x4 slice. The times are simulated.
32 devices in a mesh: group: 4 (over y, x), dom: 8 (over z, core).
Axes of the slice: x: 2, y: 2, z: 4, core: 2. Of those that a mesh axis runs over, the one named last changes fastest.
Arguments:
- features: bfloat16 [16384, 128], P(('group', 'dom')), may hold values from -6 to 6
- adj_local: bfloat16 [16384, 512], P(('group', 'dom')), as said below
- adj_bound: bfloat16 [16384, 256], P(('group', 'dom')), as said below
- w_self: bfloat16 [128, 128], replicated, may hold values from -0.5 to 0.5
- w_neigh: bfloat16 [128, 128], replicated, may hold values from -0.5 to 0.5
- pub_rows: int32 [32, 64], P(('group', 'dom')), may hold values from 0 to 511, as said below
- recv_pos: int32 [32, 256], P(('group', 'dom')), may hold values from 0 to 63, as said below
- recv_count: int32 [32, 8], P(('group', 'dom')), may hold values from 0 to 32, as said below
- target_mask: int32 [16384], P(('group', 'dom')), may hold values from 0 to 1, as said below
- cotangent: bfloat16 [16384, 128], P(('group', 'dom')), may hold values from -6 to 6
Outputs:
- hidden_out: bfloat16 [16384, 128], P(('group', 'dom'))
- grad_features: bfloat16 [16384, 128], P(('group', 'dom'))
- grad_w_self: float32 [128, 128], replicated
- grad_w_neigh: float32 [128, 128], replicated
Inputs may be any that keep to these rules, and one draw needn't show every extreme that they name: `pub_rows`: the 64 entries of a partition are distinct. `recv_pos`: for one partition and one peer the 32 positions are distinct. `recv_count`: A partition's count from itself is 0; in every group one partition receives 32 rows from every other partition of the group. `target_mask`: exactly 16 ones in every aligned block of 128 rows. `adj_local`: Nonnegative. `adj_bound`: Nonnegative.
All inputs are finite; a program needn't handle non-finite values.
Results may differ from a plain program's by a relative error of at most 0.0051.
Values may be sent and summed in bfloat16 or wider, within the bound.
No kernel may reach another device: no remote copies, remote signals or barrier semaphores. Data moves between devices by JAX's collectives and lax.ppermute only.
A program may use at most 64 MiB of HBM per device.

v0:
```python
import math

import jax
import jax.numpy as jnp
from jax import lax
from jax.sharding import PartitionSpec as P


def silu_slope(preact):
    sigma = jax.nn.sigmoid(preact)
    return sigma * (1.0 + preact * (1.0 - sigma))


def local(
    features,
    adj_local,
    adj_bound,
    w_self,
    w_neigh,
    pub_rows,
    recv_pos,
    recv_count,
    target_mask,
    cotangent,
):
    dom_size = lax.axis_size("dom")
    devices_all = lax.axis_size("group") * dom_size
    row_count, width = features.shape
    slot_rows = recv_pos.shape[1] // dom_size
    slot_ids = jnp.arange(slot_rows, dtype=jnp.int32)
    bf_zero = jnp.zeros((), jnp.bfloat16)
    use_grid = slot_ids[None, :] < recv_count[0][:, None]
    in_use = use_grid.reshape(-1)
    bound_tile = jnp.where(in_use[None, :], adj_bound, bf_zero)
    published = pub_rows[0]
    asked_pos, asked_use = (
        lax.all_to_all(
            recv_pos[0].reshape(dom_size, slot_rows), "dom", split_axis=0, concat_axis=0, tiled=True
        ),
        lax.all_to_all(use_grid.astype(jnp.int32), "dom", split_axis=0, concat_axis=0, tiled=True),
    )
    chosen_rows = published[asked_pos.reshape(-1)]
    sent_use = asked_use.reshape(-1) > 0
    outgoing = jnp.where(sent_use[:, None], features[chosen_rows], bf_zero).reshape(
        dom_size, slot_rows, width
    )
    received = lax.all_to_all(outgoing, "dom", split_axis=0, concat_axis=0, tiled=True).reshape(
        dom_size * slot_rows, width
    )
    weight_sum = jnp.sum(adj_local, axis=1, dtype=jnp.float32) + jnp.sum(
        bound_tile, axis=1, dtype=jnp.float32
    )
    inverse_degree = (1.0 / (1.0 + weight_sum))[:, None]
    summed = jnp.dot(adj_local, features, preferred_element_type=jnp.float32) + jnp.dot(
        bound_tile, received, preferred_element_type=jnp.float32
    )
    aggregate = (summed * inverse_degree).astype(jnp.bfloat16)
    preact = jnp.dot(features, w_self, preferred_element_type=jnp.float32) + jnp.dot(
        aggregate, w_neigh, preferred_element_type=jnp.float32
    )
    hidden_out = jax.nn.silu(preact).astype(jnp.bfloat16)
    chosen = target_mask.astype(jnp.float32)[:, None]
    grad_pre = (cotangent.astype(jnp.float32) * chosen * silu_slope(preact)).astype(jnp.bfloat16)
    grad_self = jnp.dot(features.T, grad_pre, preferred_element_type=jnp.float32)
    grad_neigh = jnp.dot(aggregate.T, grad_pre, preferred_element_type=jnp.float32)
    grad_aggregate = (
        jnp.dot(grad_pre, w_neigh.T, preferred_element_type=jnp.float32) * inverse_degree
    ).astype(jnp.bfloat16)
    grad_received = jnp.dot(bound_tile.T, grad_aggregate, preferred_element_type=jnp.float32)
    grad_local = jnp.dot(grad_pre, w_self.T, preferred_element_type=jnp.float32) + jnp.dot(
        adj_local.T, grad_aggregate, preferred_element_type=jnp.float32
    )
    returned = lax.all_to_all(
        grad_received.reshape(dom_size, slot_rows, width).astype(jnp.bfloat16),
        "dom",
        split_axis=0,
        concat_axis=0,
        tiled=True,
    ).astype(jnp.float32)
    peer_grads = (
        jnp.zeros((row_count, width), jnp.float32)
        .at[chosen_rows]
        .add(returned.reshape(dom_size * slot_rows, width))
    )
    grad_features = (grad_local + peer_grads).astype(jnp.bfloat16)
    total_self, total_neigh = lax.psum((grad_self, grad_neigh), ("group", "dom"))
    grad_scale = 1.0 / math.sqrt(row_count * devices_all // 8)
    return (hidden_out, grad_features, total_self * grad_scale, total_neigh * grad_scale)


def solution(mesh):
    in_specs = (
        P(("group", "dom"), None),
        P(("group", "dom"), None),
        P(("group", "dom"), None),
        P(),
        P(),
        P(("group", "dom"), None),
        P(("group", "dom"), None),
        P(("group", "dom"), None),
        P(("group", "dom")),
        P(("group", "dom"), None),
    )
    out_specs = (P(("group", "dom"), None), P(("group", "dom"), None), P(), P())
    return jax.shard_map(local, mesh=mesh, in_specs=in_specs, out_specs=out_specs, check_vma=False)
```

profile of v0, /device:TPU:0, one launch (start us, length us, event | category | flops | bytes accessed | tf_op | source)
XLA Modules:
  0.0 179.7 jit_solution(11584726352165659103)
XLA Ops:
  7.2 0.0 copy-start
  7.2 0.0 copy-start.2
  7.2 0.5 broadcast.110
  7.7 0.2 copy-done.7
  7.9 0.7 reduce.6
  8.6 0.7 all_to_all.17
  9.2 6.3 %all-to-all-start.1 = ((s32[8,1,32]{2,1,0:T(1,128)}), s32[8,1,32]{2,1,0:T(1,128)S(1)}, u32[]{:S(2)}, u32[]{:S(2)}) async-start(s32[8,1,32]{2,1,0:T(1,128)} %all_to_all.17), calls=%async_computation.1 | async-start | bytes 8192 | tf_op jit(solution)/shard_map/all_to_all | solution.py:37
  15.6 1.3 compare_convert_fusion
  16.9 0.7 iota_compare_fusion
  17.6 0.1 lt.60
  17.7 1.2 convert_reduce_fusion
  18.9 0.0 copy-start.4
  18.9 0.3 fusion.11
  19.2 0.4 copy-done.4
  19.7 0.2 fusion.10
  19.8 0.8 copy-done.3
  20.6 0.1 convert_reduce_fusion.1
  20.8 0.5 copy-done.6
  21.3 0.0 all-to-all-done.1
  21.3 5.1 %all-to-all-start = ((s32[8,1,32]{2,1,0:T(1,128)}), s32[8,1,32]{2,1,0:T(1,128)S(1)}, u32[]{:S(2)}, u32[]{:S(2)}) async-start(s32[8,1,32]{2,1,0:T(1,128)} %compare_convert_fusion), calls=%async_computation | async-start | bytes 8192 | tf_op jit(solution)/shard_map/all_to_all | solution.py:40
  26.4 0.7 reduce.7
  27.1 0.1 reshape.148
  27.2 0.6 copy-done.1
  27.8 1.9 %gather_fusion = s32[256]{0:T(256)S(1)} fusion(s32[64]{0:T(128)S(1)} %bitcast.37, s32[1024]{0:T(1024)S(1)} %pad_clamp_fusion.1), kind=kCustom, calls=%fused_computation | custom fusion | bytes 3072 | tf_op jit(solution)/shard_map/gather | solution.py:42
  29.7 0.9 gather_fusion.1
  30.6 1.3 all-to-all-done
  31.9 0.7 broadcast_select_fusion.3
  32.6 3.8 %all-to-all-start.2 = ((bf16[8,32,128]{2,1,0:T(8,128)(2,1)}), bf16[8,32,128]{2,1,0:T(8,128)(2,1)S(1)}, u32[]{:S(2)}, u32[]{:S(2)}) async-start(bf16[8,32,128]{2,1,0:T(8,128)(2,1)} %broadcast_select_fusion.3), calls=%async_computation.2 | async-start | bytes 131072 | tf_op jit(solution)/shard_map/all_to_all | solution.py:47
  36.4 0.0 all-reduce.3.cloned.1.call-start
  36.5 5.9 %all-to-all-done.2 = bf16[8,32,128]{2,1,0:T(8,128)(2,1)S(1)} async-done(((bf16[8,32,128]{2,1,0:T(8,128)(2,1)}), bf16[8,32,128]{2,1,0:T(8,128)(2,1)S(1)}, u32[]{:S(2)}, u32[]{:S(2)}) %all-to-all-start.2) | async-done | bytes 65568 | tf_op jit(solution)/shard_map/all_to_all | solution.py:47
  42.4 0.2 fusion.2
  42.6 0.5 copy-done.5
  43.1 0.2 copy-done.8
  43.3 0.9 multiply_convert_fusion
  44.2 0.9 fusion.13
  45.1 0.9 convolution_bitcast_fusion.1
  45.9 0.2 fusion.3
  46.1 0.2 fusion.12
  46.3 0.0 all-reduce.3.cloned.1.call-update
  46.3 0.3 fusion
  46.7 0.9 convolution_convert_fusion
  47.6 3.4 %all-to-all-start.3 = ((bf16[8,32,128]{2,1,0:T(8,128)(2,1)}), bf16[8,32,128]{2,1,0:T(8,128)(2,1)S(1)}, u32[]{:S(2)}, u32[]{:S(2)}) async-start(bf16[8,32,128]{2,1,0:T(8,128)(2,1)} %bitcast.10), calls=%async_computation.3 | async-start | bytes 131072 | tf_op jit(solution)/shard_map/all_to_all | solution.py:73
  51.0 116.8 %all-reduce.3.cloned.1.call-done = (f32[128,128]{0,1:T(8,128)}, f32[128,128]{0,1:T(8,128)}) async-done(((f32[128,128]{0,1:T(8,128)}, f32[128,128]{0,1:T(8,128)}), (f32[128,128]{0,1:T(8,128)}, f32[128,128]{0,1:T(8,128)})) %all-reduce.3.cloned.1.call-update) | async-done | bytes 131088 | tf_op jit(solution)/shard_map/psum | solution.py:86
  167.8 0.9 broadcast_multiply_fusion
  168.7 0.7 copy.29
  169.4 0.7 copy.30
  170.1 2.0 %scatter_custom_fusion = f32[512,128]{1,0:T(8,128)S(1)} fusion(f32[512,128]{1,0:T(8,128)S(1)} %fusion, s32[256]{0:T(256)S(1)} %bitcast.43, bf16[256,128]{1,0:T(8,128)(2,1)S(1)} %bitcast.38), kind=kCustom, calls=%fused_computation.19 | custom fusion | flops 65536 | bytes 327680 | tf_op jit(solution)/shard_map/scatter-add | solution.py:83
  172.2 0.7 convert_element_type.55
  (16 shorter events, 0.1 us)
Async XLA Ops:
  7.2 11.7 %copy-start = (bf16[512,128]{1,0:T(8,128)(2,1)S(1)}, bf16[512,128]{1,0:T(8,128)(2,1)}, u32[]{:S(2)}) copy-start(bf16[512,128]{1,0:T(8,128)(2,1)} %param.10) | copy-start | bytes 393220
  7.2 0.7 copy-start.7
  7.2 11.7 %copy-start.2 = (bf16[512,512]{1,0:T(8,128)(2,1)S(1)}, bf16[512,512]{1,0:T(8,128)(2,1)}, u32[]{:S(2)}) copy-start(bf16[512,512]{1,0:T(8,128)(2,1)} %param.11) | copy-start | bytes 1572868
  9.2 12.1 %all-to-all-start.1 = ((s32[8,1,32]{2,1,0:T(1,128)}), s32[8,1,32]{2,1,0:T(1,128)S(1)}, u32[]{:S(2)}, u32[]{:S(2)}) async-start(s32[8,1,32]{2,1,0:T(1,128)} %all_to_all.17), calls=%async_computation.1 | async-start | bytes 8192 | tf_op jit(solution)/shard_map/all_to_all | solution.py:37
  18.9 0.8 copy-start.4
  19.7 0.9 copy-start.3
  20.6 0.7 copy-start.6
  21.3 10.6 %all-to-all-start = ((s32[8,1,32]{2,1,0:T(1,128)}), s32[8,1,32]{2,1,0:T(1,128)S(1)}, u32[]{:S(2)}, u32[]{:S(2)}) async-start(s32[8,1,32]{2,1,0:T(1,128)} %compare_convert_fusion), calls=%async_computation | async-start | bytes 8192 | tf_op jit(solution)/shard_map/all_to_all | solution.py:40
  27.2 0.7 copy-start.1
  32.6 9.7 %all-to-all-start.2 = ((bf16[8,32,128]{2,1,0:T(8,128)(2,1)}), bf16[8,32,128]{2,1,0:T(8,128)(2,1)S(1)}, u32[]{:S(2)}, u32[]{:S(2)}) async-start(bf16[8,32,128]{2,1,0:T(8,128)(2,1)} %broadcast_select_fusion.3), calls=%async_computation.2 | async-start | bytes 131072 | tf_op jit(solution)/shard_map/all_to_all | solution.py:47
  36.4 131.3 %all-reduce.3.cloned.1.call-start = ((), (), s32[]{:S(2)}) async-start(), calls=%async_computation.4 | async-start | bytes 262144 | tf_op jit(solution)/shard_map/psum | solution.py:86
  42.4 0.8 copy-start.5
  42.4 0.9 copy-start.8
  47.6 122.5 %all-to-all-start.3 = ((bf16[8,32,128]{2,1,0:T(8,128)(2,1)}), bf16[8,32,128]{2,1,0:T(8,128)(2,1)S(1)}, u32[]{:S(2)}, u32[]{:S(2)}) async-start(bf16[8,32,128]{2,1,0:T(8,128)(2,1)} %bitcast.10), calls=%async_computation.3 | async-start | bytes 131072 | tf_op jit(solution)/shard_map/all_to_all | solution.py:73
Sparse Core Ops, SparseCore 0:
  46.5 121.2 all-reduce.2
where the time goes:
time: 180 us
  waiting for transfers between devices  124 us (69%)
  starting transfers between devices  18.6 us (10%)
  between operations  14.2 us (8%)
  other arithmetic  9.08 us (5%)
  local copies, waits for them, and re-layouts  8.84 us (5%)
  matrix products  4.96 us (3%)
    psum x1, waiting for transfers between devices, local(): lax.psum((grad_self, grad_neigh), ('group', 'dom'))  117 us
    all_to_all x1, starting transfers between devices, local(): lax.all_to_all(recv_pos[0].reshape(dom_size, slot_rows), 'dom', split_axi...  6.33 us
    all_to_all x1, waiting for transfers between devices, local(): lax.all_to_all(outgoing, 'dom', split_axis=0, concat_axis=0, tiled=True)  5.86 us
    unnamed x21, local copies, waits for them, and re-layouts  5.27 us
    all_to_all x1, starting transfers between devices, local(): lax.all_to_all(use_grid.astype(jnp.int32), 'dom', split_axis=0, concat_ax...  5.1 us
    all_to_all x1, starting transfers between devices, local(): lax.all_to_all(outgoing, 'dom', split_axis=0, concat_axis=0, tiled=True)  3.79 us
  transfers between devices with their start and end apart: 5, of which 3 were waited for; matrix products, arithmetic and copies ran while one was open for 6% of the time, Pallas kernels for 0%

commit v1 on v0

v1 whole, which is shorter than its diff:
```python
import functools
import math

import jax
import jax.numpy as jnp
from jax import lax
from jax.experimental import pallas as pl
from jax.experimental.pallas import tpu as pltpu
from jax.sharding import PartitionSpec as P

BF = jnp.bfloat16
F32 = jnp.float32
VMEM = pl.BlockSpec(memory_space=pltpu.VMEM)
SMEM = pl.BlockSpec(memory_space=pltpu.SMEM)
PARAMS = pltpu.CompilerParams(vmem_limit_bytes=48 * 1024 * 1024)


def dot(a, b):
    return jnp.dot(a, b, preferred_element_type=F32)


def dot_t(a, b):
    return lax.dot_general(a, b, (((0,), (0,)), ((), ())), preferred_element_type=F32)


def dot_nt(a, b):
    return lax.dot_general(a, b, (((1,), (1,)), ((), ())), preferred_element_type=F32)


def one_hot(rows, targets):
    row = lax.broadcasted_iota(jnp.int32, (rows, targets.shape[1]), 0)
    return jnp.where(row == targets, 1.0, 0.0).astype(BF)


def call(body, outs, *args, smem=()):
    return pl.pallas_call(
        body,
        out_shape=[jax.ShapeDtypeStruct(shape, dtype) for shape, dtype in outs],
        in_specs=[SMEM if i in smem else VMEM for i in range(len(args))],
        out_specs=[VMEM] * len(outs),
        compiler_params=PARAMS,
    )(*args)


def xor_swap(x, axis, size, k):
    return lax.ppermute(x, axis, [(a, a ^ k) for a in range(size)])


def publish_body(pub_ref, features_ref, out_ref):
    out_ref[...] = dot_t(one_hot(features_ref.shape[0], pub_ref[...]), features_ref[...]).astype(BF)


def prepare_body(
    dom_size,
    pub_count,
    features_ref,
    local_ref,
    bound_ref,
    pos_ref,
    count_ref,
    w_self_ref,
    adj_ref,
    part_ref,
    inv_ref,
    self_ref,
):
    me = lax.axis_index("dom")
    slots = pos_ref.shape[1]
    slot_rows = slots // dom_size
    lane = lax.broadcasted_iota(jnp.int32, (1, slots), 1)
    peer = lane // slot_rows
    limit = jnp.zeros((1, slots), jnp.int32)
    for j in range(dom_size):
        limit = jnp.where(peer == j, count_ref[0, j], limit)
    in_use = lane % slot_rows < limit
    target = jnp.where(in_use, (peer ^ me) * pub_count + pos_ref[...], -1)
    columns = dom_size * pub_count
    chunk = math.gcd(columns, 512)
    features = features_ref[...]
    ones = jnp.ones(features.shape, BF)

    def move(c, total):
        start = pl.multiple_of(c * chunk, chunk)
        block = dot_nt(bound_ref[...], one_hot(chunk, target - start)).astype(BF)
        adj_ref[:, pl.ds(start, chunk)] = block
        return total + dot(block, jnp.ones((chunk, features.shape[1]), BF))

    sums = lax.fori_loop(0, columns // chunk, move, dot(local_ref[...], ones))
    inv_ref[...] = 1.0 / (1.0 + sums)
    part_ref[...] = dot(local_ref[...], features)
    self_ref[...] = dot(features, w_self_ref[...])


def layer_body(
    blocks,
    features_ref,
    local_ref,
    adj_ref,
    part_ref,
    inv_ref,
    self_ref,
    w_self_ref,
    w_neigh_ref,
    cot_ref,
    *refs,
):
    gathered = refs[:blocks]
    hidden_ref, local_grad_ref, keep_w_ref, send_w_ref, keep_g_ref, send_g_ref, rows_ref = refs[blocks:]
    pub_count = gathered[0].shape[0]
    for k in range(blocks):
        rows_ref[k * pub_count : (k + 1) * pub_count, :] = gathered[k][...]
    inv = inv_ref[...]
    aggregate = ((part_ref[...] + dot(adj_ref[...], rows_ref[...])) * inv).astype(BF)
    preact = self_ref[...] + dot(aggregate, w_neigh_ref[...])
    sigma = jax.nn.sigmoid(preact)
    hidden_ref[...] = (preact * sigma).astype(BF)
    slope = sigma * (1.0 + preact * (1.0 - sigma))
    grad_pre = (cot_ref[...].astype(F32) * slope).astype(BF)
    grad_agg = (dot_nt(grad_pre, w_neigh_ref[...]) * inv).astype(BF)
    grad_self = dot_t(features_ref[...], grad_pre)
    grad_neigh = dot_t(aggregate, grad_pre)
    first = lax.axis_index("dom") % 2 == 0
    keep_w_ref[...] = jnp.where(first, grad_self, grad_neigh)
    send_w_ref[...] = jnp.where(first, grad_neigh, grad_self)
    grad_rows = dot_t(adj_ref[...], grad_agg)
    for z in range(blocks // 2):
        here = slice(z * pub_count, (z + 1) * pub_count)
        even = slice(2 * z * pub_count, (2 * z + 1) * pub_count)
        odd = slice((2 * z + 1) * pub_count, (2 * z + 2) * pub_count)
        keep_g_ref[here, :] = grad_rows[even]
        send_g_ref[here, :] = grad_rows[odd].astype(BF)
    local_grad_ref[...] = dot_nt(grad_pre, w_self_ref[...]) + dot_t(local_ref[...], grad_agg)


def chip_body(group_size, pub_count, keep_w_ref, got_w_ref, keep_g_ref, got_g_ref, own_ref, far_ref, total_ref, *parts):
    grads = keep_g_ref[...] + got_g_ref[...].astype(F32)
    own_ref[...] = grads[:pub_count]
    far_ref[...] = grads[pub_count:].astype(BF)
    me = lax.axis_index("group")
    total_ref[...] = keep_w_ref[...] + got_w_ref[...]
    rows = parts[0].shape[0]
    for k in range(group_size):
        parts[k][...] = total_ref[pl.ds(pl.multiple_of((me ^ k) * rows, rows), rows), :]


def group_body(count, far_ref, *refs):
    parts, (total_ref, *messages) = refs[:count], refs[count:]
    total = parts[0][...]
    for part in parts[1:]:
        total = total + part[...]
    total_ref[...] = total
    high = total.astype(BF).astype(F32)
    halves = jnp.concatenate([high, total - high], axis=0).astype(BF)
    pub_count = far_ref.shape[0] // len(messages)
    for z, message in enumerate(messages):
        message[:pub_count, :] = far_ref[z * pub_count : (z + 1) * pub_count, :]
        message[pub_count:, :] = halves


def weights_body(scale, pub_count, total_ref, *refs):
    messages, (out_ref,) = refs[:-1], refs[-1:]
    total = total_ref[...]
    rows = total.shape[0]
    for message in messages:
        halves = message[pub_count:, :].astype(F32)
        total = total + halves[:rows] + halves[rows:]
    out_ref[...] = total * scale


def features_body(pub_ref, local_grad_ref, own_ref, *refs):
    messages, (out_ref,) = refs[:-1], refs[-1:]
    total = own_ref[...]
    for message in messages:
        total = total + message[: total.shape[0], :].astype(F32)
    place = one_hot(local_grad_ref.shape[0], pub_ref[...])
    high = total.astype(BF)
    low = (total - high.astype(F32)).astype(BF)
    out_ref[...] = (local_grad_ref[...] + dot(place, high) + dot(place, low)).astype(BF)


def place_body(count, *refs):
    mine, theirs, (self_ref, neigh_ref) = refs[:count], refs[count : 2 * count], refs[2 * count :]
    me = lax.axis_index("group")
    first = lax.axis_index("dom") % 2 == 0
    rows = mine[0].shape[0]
    for k in range(count):
        here = pl.ds(pl.multiple_of((me ^ k) * rows, rows), rows)
        a, b = mine[k][...], theirs[k][...]
        self_ref[here, :] = jnp.where(first, a, b)
        neigh_ref[here, :] = jnp.where(first, b, a)


def local(
    features,
    adj_local,
    adj_bound,
    w_self,
    w_neigh,
    pub_rows,
    recv_pos,
    recv_count,
    target_mask,
    cotangent,
):
    dom_size, group_size = lax.axis_size("dom"), lax.axis_size("group")
    z_size = dom_size // 2
    row_count, width = features.shape
    pub_count = pub_rows.shape[1]
    wide = (row_count, width)
    over_z = lambda x, z: xor_swap(x, "dom", dom_size, 2 * z)
    over_core = lambda x: xor_swap(x, "dom", dom_size, 1)
    over_group = lambda x, k: xor_swap(x, "group", group_size, k)

    (published,) = call(publish_body, [((pub_count, width), BF)], pub_rows, features)
    near = [published] + [over_z(published, z) for z in range(1, z_size)]
    far = [over_core(x) for x in near]
    gathered = [x for pair in zip(near, far) for x in pair]

    adj_rows, part, inverse, own_part = call(
        functools.partial(prepare_body, dom_size, pub_count),
        [((row_count, dom_size * pub_count), BF), (wide, F32), (wide, F32), (wide, F32)],
        features,
        adj_local,
        adj_bound,
        recv_pos,
        recv_count,
        w_self,
        smem=(4,),
    )
    chosen = jnp.where(target_mask[:, None] > 0, cotangent, jnp.zeros((), BF))
    slots_z = z_size * pub_count
    hidden, local_grad, keep_w, send_w, keep_g, send_g = pl.pallas_call(
        functools.partial(layer_body, dom_size),
        out_shape=[
            jax.ShapeDtypeStruct(s, d)
            for s, d in [
                (wide, BF),
                (wide, F32),
                ((width, width), F32),
                ((width, width), F32),
                ((slots_z, width), F32),
                ((slots_z, width), BF),
            ]
        ],
        in_specs=[VMEM] * (9 + dom_size),
        out_specs=[VMEM] * 6,
        scratch_shapes=[pltpu.VMEM((dom_size * pub_count, width), BF)],
        compiler_params=PARAMS,
    )(features, adj_local, adj_rows, part, inverse, own_part, w_self, w_neigh, chosen, *gathered)

    got_w, got_g = over_core(send_w), over_core(send_g)
    quarter = (width // group_size, width)
    own_g, far_g, _, *parts = call(
        functools.partial(chip_body, group_size, pub_count),
        [((pub_count, width), F32), ((slots_z - pub_count, width), BF), ((width, width), F32)]
        + [(quarter, F32)] * group_size,
        keep_w,
        got_w,
        keep_g,
        got_g,
    )
    got_parts = [parts[0]] + [over_group(parts[k], k) for k in range(1, group_size)]
    message = ((pub_count + 2 * quarter[0], width), BF)
    group_total, *messages = call(
        functools.partial(group_body, group_size), [(quarter, F32)] + [message] * (z_size - 1), far_g, *got_parts
    )
    got = [over_z(messages[z - 1], z) for z in range(1, z_size)]
    scale = 1.0 / math.sqrt(row_count * group_size * dom_size // 8)
    (total,) = call(functools.partial(weights_body, scale, pub_count), [(quarter, F32)], group_total, *got)
    mine = [total] + [over_group(total, k) for k in range(1, group_size)]
    theirs = [over_core(x) for x in mine]
    (grad_features,) = call(features_body, [(wide, BF)], pub_rows, local_grad, own_g, *got)
    grad_self, grad_neigh = call(
        functools.partial(place_body, group_size), [((width, width), F32)] * 2, *mine, *theirs
    )
    return hidden, grad_features, grad_self, grad_neigh


def solution(mesh):
    rows = P(("group", "dom"), None)
    in_specs = (rows, rows, rows, P(), P(), rows, rows, rows, P(("group", "dom")), rows)
    return jax.shard_map(
        local, mesh=mesh, in_specs=in_specs, out_specs=(rows, rows, P(), P()), check_vma=False
    )
```

time: 180 us -> 43.4 us (0.24)
  waiting for transfers between devices: 124 us -> 13.2 us
  between operations: 14.2 us -> 0.79 us
  other arithmetic: 9.08 us -> 1.72 us
  local copies, waits for them, and re-layouts: 8.84 us -> 3.26 us
  Pallas kernels: 0 us -> 5.13 us
  matrix products: 4.96 us -> 0 us
    psum x1 -> x0, waiting for transfers between devices: 117 us -> none  [local(): lax.psum((grad_self, grad_neigh), ('group', 'dom'))]
    ppermute x0 -> x22, starting transfers between devices: none -> 19 us  [xor_swap(): return lax.ppermute(x, axis, [(a, a ^ k) for a in range(size)])]
    all_to_all x4 -> x0, starting transfers between devices: 18.6 us -> none  [the longest x1 6.33 us: local(): lax.all_to_all(recv_pos[0].reshape(dom_size, slot_rows), 'dom', split_axi...]
    ppermute x0 -> x22, waiting for transfers between devices: none -> 13.2 us  [xor_swap(): return lax.ppermute(x, axis, [(a, a ^ k) for a in range(size)])]
    all_to_all x4 -> x0, waiting for transfers between devices: 7.18 us -> none  [the longest x1 5.86 us: local(): lax.all_to_all(outgoing, 'dom', split_axis=0, concat_axis=0, tiled=True)]
    pallas_call x0 -> x8, Pallas kernels: none -> 5.13 us  [the longest x7 3.82 us: call(): pl.pallas_call(body, out_shape=[jax.ShapeDtypeStruct(shape, dtype) for sh...]
    dot_general x10 -> x0, matrix products: 4.96 us -> none  [the longest x1 0.92 us: local(): jnp.dot(aggregate, w_neigh, preferred_element_type=jnp.float32)]
    gather x2 -> x0, local copies, waits for them, and re-layouts: 2.72 us -> none  [the longest x1 1.87 us: local(): chosen_rows = published[asked_pos.reshape(-1)]]
  transfers between devices with their start and end apart: 5 -> 22, of which waited for: 3 -> 11; matrix products, arithmetic and copies ran while one was open for 6% -> 4% of each run, Pallas kernels for 0% -> 5%
where the time goes in v1:
time: 43.4 us; the launch traced here: 43.1 us
  starting transfers between devices  19 us (44%)
  waiting for transfers between devices  13.2 us (30%)
  Pallas kernels  5.13 us (12%)
  local copies, waits for them, and re-layouts  3.26 us (8%)
  other arithmetic  1.72 us (4%)
  between operations  0.79 us (2%)
    ppermute x22, starting transfers between devices, xor_swap(): return lax.ppermute(x, axis, [(a, a ^ k) for a in range(size)])  19 us
    ppermute x22, waiting for transfers between devices, xor_swap(): return lax.ppermute(x, axis, [(a, a ^ k) for a in range(size)])  13.2 us
    pallas_call x7, Pallas kernels, call(): pl.pallas_call(body, out_shape=[jax.ShapeDtypeStruct(shape, dtype) for sh...  3.82 us
    unnamed x18, local copies, waits for them, and re-layouts  3.26 us
    pallas_call x1, Pallas kernels, local(): pl.pallas_call(functools.partial(layer_body, dom_size), out_shape=[jax.Sh...  1.3 us
    select_n x1, other arithmetic, local(): chosen = jnp.where(target_mask[:, None] > 0, cotangent, jnp.zeros((), BF))  1.04 us
  transfers between devices with their start and end apart: 22, of which 11 were waited for; matrix products, arithmetic and copies ran while one was open for 4% of the time, Pallas kernels for 5%

profile of v1, /device:TPU:0, one launch (start us, length us, event | category | flops | bytes accessed | tf_op | source)
XLA Modules:
  0.0 43.1 jit_solution(7886482269176419491)
XLA Ops:
  0.6 0.9 %copy-done.1 = bf16[512,128]{1,0:T(8,128)(2,1)S(1)} copy-done((bf16[512,128]{1,0:T(8,128)(2,1)S(1)}, bf16[512,128]{1,0:T(8,128)(2,1)}, u32[]{:S(2)}) %copy-start.1) | copy-done | bytes 131096
  1.5 0.7 %copy-done.5 = s32[1,64]{1,0:T(1,128)S(1)} copy-done((s32[1,64]{1,0:T(1,128)S(1)}, s32[1,64]{1,0:T(1,128)}, u32[]{:S(2)}) %copy-start.5) | copy-done | bytes 280
  2.2 0.2 shard_map.130.refs_0_
  2.4 5.1 %collective-permute-start.5 = (bf16[64,128]{1,0:T(8,128)(2,1)S(1)}, bf16[64,128]{1,0:T(8,128)(2,1)S(1)}, u32[]{:S(2)}, u32[]{:S(2)}) collective-permute-start(bf16[64,128]{1,0:T(8,128)(2,1)S(1)} %shard_map.130.refs_0_), channel_id=1, source_target_pairs={{0,6},{1,7},{2,4},{3,5},{4,2},{5,3},{6,0},{7,1},{8,14},{9,15},{10,... | collective-permute-start | bytes 49160 | tf_op jit(solution)/shard_map/ppermute | solution.py:46
  7.5 0.0 collective-permute-start.3
  7.5 0.6 %collective-permute-start.1 = (bf16[64,128]{1,0:T(8,128)(2,1)S(1)}, bf16[64,128]{1,0:T(8,128)(2,1)S(1)}, u32[]{:S(2)}, u32[]{:S(2)}) collective-permute-start(bf16[64,128]{1,0:T(8,128)(2,1)S(1)} %shard_map.130.refs_0_), channel_id=1, source_target_pairs={{0,2},{1,3},{2,0},{3,1},{4,6},{5,7},{6,4},{7,5},{8,10},{9,11},{10,... | collective-permute-start | bytes 49160 | tf_op jit(solution)/shard_map/ppermute | solution.py:46
  8.2 0.0 collective-permute-start
  8.2 0.7 %broadcast_compare_fusion = pred[512]{0:T(512)(128)(4,1)S(1)} fusion(s32[512]{0:T(512)} %param.18), kind=kLoop, calls=%fused_computation.1 | loop fusion | flops 512 | bytes 2560 | tf_op jit(solution)/shard_map/gt | solution.py:230
  8.9 0.4 collective-permute-done.5.refs_6_
  9.2 0.2 collective-permute-start.6
  9.4 2.7 %collective-permute-done.3.refs_4_ = bf16[64,128]{1,0:T(8,128)(2,1)S(1)} collective-permute-done((bf16[64,128]{1,0:T(8,128)(2,1)S(1)}, bf16[64,128]{1,0:T(8,128)(2,1)S(1)}, u32[]{:S(2)}, u32[]{:S(2)}) %collective-permute-start.3) | collective-permute-done | bytes 16416 | tf_op jit(solution)/shard_map/ppermute | solution.py:46
  12.2 0.0 collective-permute-start.4
  12.2 0.0 collective-permute-done.1.refs_2_
  12.2 0.5 %collective-permute-start.2 = (bf16[64,128]{1,0:T(8,128)(2,1)S(1)}, bf16[64,128]{1,0:T(8,128)(2,1)S(1)}, u32[]{:S(2)}, u32[]{:S(2)}) collective-permute-start(bf16[64,128]{1,0:T(8,128)(2,1)S(1)} %collective-permute-done.1.refs_2_), channel_id=1, source_target_pairs={{0,1},{1,0},{2,3},{3,2},{4,5},{5,4},{6,7},{7,6},{8,9},{9,8},{10,11... | collective-permute-start | bytes 49160 | tf_op jit(solution)/shard_map/ppermute | solution.py:46
  12.7 1.0 %broadcast_select_fusion.cot_ref = bf16[512,128]{1,0:T(8,128)(2,1)S(1)} fusion(bf16[512,128]{1,0:T(8,128)(2,1)} %param.19, pred[512]{0:T(512)(128)(4,1)S(1)} %broadcast_compare_fusion), kind=kLoop, calls=%fused_computation | loop fusion | flops 65536 | bytes 262656 | tf_op jit(solution)/shard_map/jit(_where)/select_n | solution.py:230
  13.8 0.0 copy-start
  13.8 1.0 %copy-done = bf16[512,512]{1,0:T(8,128)(2,1)S(1)} copy-done((bf16[512,512]{1,0:T(8,128)(2,1)S(1)}, bf16[512,512]{1,0:T(8,128)(2,1)}, u32[]{:S(2)}) %copy-start) | copy-done | bytes 524312
  14.8 1.4 %shard_map.129 = (bf16[512,512]{1,0:T(8,128)(2,1)S(1)}, f32[512,128]{1,0:T(8,128)S(1)}, f32[512,128]{1,0:T(8,128)S(1)}, f32[512,128]{1,0:T(8,128)S(1)}) custom-call(bf16[512,128]{1,0:T(8,128)(2,1)S(1)} %copy-done.1, bf16[512,512]{1,0:T(8,128)(2,1)S(1)} %copy-done, bf16[512,256]{1,0:T(8,128)(2,1)S(1)} %copy-done.2, s32[1,256]{1,0:T(1,128)S(1)} %copy-done.7, ...), custom_call_target="tpu_custom_call" | custom-call | tf_op jit(solution)/shard_map/pallas_call | solution.py:36
  16.2 0.0 collective-permute-done.6.refs_7_
  16.2 0.0 collective-permute-done.4.refs_5_
  16.3 1.3 %shard_map.131 = (bf16[512,128]{1,0:T(8,128)(2,1)}, f32[512,128]{1,0:T(8,128)S(1)}, f32[128,128]{1,0:T(8,128)S(1)}, f32[128,128]{1,0:T(8,128)S(1)}, f32[256,128]...) custom-call(bf16[512,128]{1,0:T(8,128)(2,1)S(1)} %copy-done.1, bf16[512,512]{1,0:T(8,128)(2,1)S(1)} %copy-done, ...), custom_call_target="tpu_custom_call" | custom-call | tf_op jit(solution)/shard_map/pallas_call | solution.py:232
  17.6 0.0 collective-permute-start.7
  17.6 0.5 %collective-permute-start.8 = (bf16[256,128]{1,0:T(8,128)(2,1)S(1)}, bf16[256,128]{1,0:T(8,128)(2,1)S(1)}, u32[]{:S(2)}, u32[]{:S(2)}) collective-permute-start(bf16[256,128]{1,0:T(8,128)(2,1)S(1)} %get-tuple-element.35), channel_id=1, source_target_pairs={{0,1},{1,0},{2,3},{3,2},{4,5},{5,4},{6,7},{7,6},{8,9},{9,8},{10,11... | collective-permute-start | bytes 196616 | tf_op jit(solution)/shard_map/ppermute | solution.py:46
  18.1 0.7 %collective-permute-done.7.got_w_ref = f32[128,128]{1,0:T(8,128)S(1)} collective-permute-done((f32[128,128]{1,0:T(8,128)S(1)}, f32[128,128]{1,0:T(8,128)S(1)}, u32[]{:S(2)}, u32[]{:S(2)}) %collective-permute-start.7) | collective-permute-done | bytes 65568 | tf_op jit(solution)/shard_map/ppermute | solution.py:46
  18.8 0.2 collective-permute-done.8.got_g_ref
  19.0 0.6 %shard_map.132 = (f32[64,128]{1,0:T(8,128)S(1)}, bf16[192,128]{1,0:T(8,128)(2,1)S(1)}, f32[128,128]{1,0:T(8,128)}, f32[32,128]{1,0:T(8,128)S(1)}, f32[32,128]{1,...) custom-call(f32[128,128]{1,0:T(8,128)S(1)} %get-tuple-element.32.keep_w_ref, ...), custom_call_target="tpu_custom_call" | custom-call | tf_op jit(solution)/shard_map/pallas_call | solution.py:36
  19.6 1.5 %collective-permute-start.9 = (f32[32,128]{1,0:T(8,128)S(1)}, f32[32,128]{1,0:T(8,128)S(1)}, u32[]{:S(2)}, u32[]{:S(2)}) collective-permute-start(f32[32,128]{1,0:T(8,128)S(1)} %get-tuple-element.39), channel_id=1, source_target_pairs={{0,8},{8,0},{16,24},{24,16},{1,9},{9,1},{17,25},{25,17},{2,10},{10... | collective-permute-start | bytes 49160 | tf_op jit(solution)/shard_map/ppermute | solution.py:46
  21.1 1.5 %collective-permute-start.10 = (f32[32,128]{1,0:T(8,128)S(1)}, f32[32,128]{1,0:T(8,128)S(1)}, u32[]{:S(2)}, u32[]{:S(2)}) collective-permute-start(f32[32,128]{1,0:T(8,128)S(1)} %get-tuple-element.40), channel_id=1, source_target_pairs={{0,16},{8,24},{16,0},{24,8},{1,17},{9,25},{17,1},{25,9},{2,18},{10... | collective-permute-start | bytes 49160 | tf_op jit(solution)/shard_map/ppermute | solution.py:46
  22.6 0.5 %collective-permute-start.11 = (f32[32,128]{1,0:T(8,128)S(1)}, f32[32,128]{1,0:T(8,128)S(1)}, u32[]{:S(2)}, u32[]{:S(2)}) collective-permute-start(f32[32,128]{1,0:T(8,128)S(1)} %get-tuple-element.41), channel_id=1, source_target_pairs={{0,24},{8,16},{16,8},{24,0},{1,25},{9,17},{17,9},{25,1},{2,26},{10... | collective-permute-start | bytes 49160 | tf_op jit(solution)/shard_map/ppermute | solution.py:46
  23.1 0.2 collective-permute-done.9.refs_1_
  23.4 1.5 %collective-permute-done.10.refs_2_ = f32[32,128]{1,0:T(8,128)S(1)} collective-permute-done((f32[32,128]{1,0:T(8,128)S(1)}, f32[32,128]{1,0:T(8,128)S(1)}, u32[]{:S(2)}, u32[]{:S(2)}) %collective-permute-start.10) | collective-permute-done | bytes 16416 | tf_op jit(solution)/shard_map/ppermute | solution.py:46
  24.9 2.4 %collective-permute-done.11.refs_3_ = f32[32,128]{1,0:T(8,128)S(1)} collective-permute-done((f32[32,128]{1,0:T(8,128)S(1)}, f32[32,128]{1,0:T(8,128)S(1)}, u32[]{:S(2)}, u32[]{:S(2)}) %collective-permute-start.11) | collective-permute-done | bytes 16416 | tf_op jit(solution)/shard_map/ppermute | solution.py:46
  27.3 0.1 collective-permute-start.12
  27.4 1.9 %collective-permute-start.13 = (bf16[128,128]{1,0:T(8,128)(2,1)S(1)}, bf16[128,128]{1,0:T(8,128)(2,1)S(1)}, u32[]{:S(2)}, u32[]{:S(2)}) collective-permute-start(bf16[128,128]{1,0:T(8,128)(2,1)S(1)} %get-tuple-element.43), channel_id=1, source_target_pairs={{0,4},{1,5},{2,6},{3,7},{4,0},{5,1},{6,2},{7,3},{8,12},{9,13},{10,... | collective-permute-start | bytes 98312 | tf_op jit(solution)/shard_map/ppermute | solution.py:46
  29.3 2.4 %collective-permute-start.14 = (bf16[128,128]{1,0:T(8,128)(2,1)S(1)}, bf16[128,128]{1,0:T(8,128)(2,1)S(1)}, u32[]{:S(2)}, u32[]{:S(2)}) collective-permute-start(bf16[128,128]{1,0:T(8,128)(2,1)S(1)} %get-tuple-element.44), channel_id=1, source_target_pairs={{0,6},{1,7},{2,4},{3,5},{4,2},{5,3},{6,0},{7,1},{8,14},{9,15},{10,... | collective-permute-start | bytes 98312 | tf_op jit(solution)/shard_map/ppermute | solution.py:46
  31.7 0.0 collective-permute-done.12.refs_0_
  31.8 0.8 %collective-permute-done.13.refs_1_ = bf16[128,128]{1,0:T(8,128)(2,1)S(1)} collective-permute-done((bf16[128,128]{1,0:T(8,128)(2,1)S(1)}, bf16[128,128]{1,0:T(8,128)(2,1)S(1)}, u32[]{:S(2)}, u32[]{:S(2)}) %collective-permute-start.13) | collective-permute-done | bytes 32800 | tf_op jit(solution)/shard_map/ppermute | solution.py:46
  32.6 2.5 %collective-permute-done.14.refs_2_ = bf16[128,128]{1,0:T(8,128)(2,1)S(1)} collective-permute-done((bf16[128,128]{1,0:T(8,128)(2,1)S(1)}, bf16[128,128]{1,0:T(8,128)(2,1)S(1)}, u32[]{:S(2)}, u32[]{:S(2)}) %collective-permute-start.14) | collective-permute-done | bytes 32800 | tf_op jit(solution)/shard_map/ppermute | solution.py:46
  35.0 0.5 %collective-permute-start.17 = (f32[32,128]{1,0:T(8,128)S(1)}, f32[32,128]{1,0:T(8,128)S(1)}, u32[]{:S(2)}, u32[]{:S(2)}) collective-permute-start(f32[32,128]{1,0:T(8,128)S(1)} %shard_map.135.refs_0_), channel_id=1, source_target_pairs={{0,24},{8,16},{16,8},{24,0},{1,25},{9,17},{17,9},{25,1},{2,26},{10... | collective-permute-start | bytes 49160 | tf_op jit(solution)/shard_map/ppermute | solution.py:46
  35.6 1.5 %collective-permute-start.16 = (f32[32,128]{1,0:T(8,128)S(1)}, f32[32,128]{1,0:T(8,128)S(1)}, u32[]{:S(2)}, u32[]{:S(2)}) collective-permute-start(f32[32,128]{1,0:T(8,128)S(1)} %shard_map.135.refs_0_), channel_id=1, source_target_pairs={{0,16},{8,24},{16,0},{24,8},{1,17},{9,25},{17,1},{25,9},{2,18},{10... | collective-permute-start | bytes 49160 | tf_op jit(solution)/shard_map/ppermute | solution.py:46
  37.1 1.5 %collective-permute-start.15 = (f32[32,128]{1,0:T(8,128)S(1)}, f32[32,128]{1,0:T(8,128)S(1)}, u32[]{:S(2)}, u32[]{:S(2)}) collective-permute-start(f32[32,128]{1,0:T(8,128)S(1)} %shard_map.135.refs_0_), channel_id=1, source_target_pairs={{0,8},{8,0},{16,24},{24,16},{1,9},{9,1},{17,25},{25,17},{2,10},{10... | collective-permute-start | bytes 49160 | tf_op jit(solution)/shard_map/ppermute | solution.py:46
  38.6 1.1 %collective-permute-done.17.refs_3_ = f32[32,128]{1,0:T(8,128)S(1)} collective-permute-done((f32[32,128]{1,0:T(8,128)S(1)}, f32[32,128]{1,0:T(8,128)S(1)}, u32[]{:S(2)}, u32[]{:S(2)}) %collective-permute-start.17) | collective-permute-done | bytes 16416 | tf_op jit(solution)/shard_map/ppermute | solution.py:46
  39.7 0.5 %collective-permute-start.20 = (f32[32,128]{1,0:T(8,128)S(1)}, f32[32,128]{1,0:T(8,128)S(1)}, u32[]{:S(2)}, u32[]{:S(2)}) collective-permute-start(f32[32,128]{1,0:T(8,128)S(1)} %collective-permute-done.16.refs_2_), channel_id=1, source_target_pairs={{0,1},{1,0},{2,3},{3,2},{4,5},{5,4},{6,7},{7,6},{8,9},{9,8},{10,11... | collective-permute-start | bytes 49160 | tf_op jit(solution)/shard_map/ppermute | solution.py:46
  40.3 0.6 %collective-permute-done.15.refs_1_ = f32[32,128]{1,0:T(8,128)S(1)} collective-permute-done((f32[32,128]{1,0:T(8,128)S(1)}, f32[32,128]{1,0:T(8,128)S(1)}, u32[]{:S(2)}, u32[]{:S(2)}) %collective-permute-start.15) | collective-permute-done | bytes 16416 | tf_op jit(solution)/shard_map/ppermute | solution.py:46
  40.8 0.0 collective-permute-start.19
  40.8 0.7 %copy-done.6 = s32[1,64]{1,0:T(1,128)S(1)} copy-done((s32[1,64]{1,0:T(1,128)S(1)}, s32[1,64]{1,0:T(1,128)}, u32[]{:S(2)}) %copy-start.6) | copy-done | bytes 280
  41.5 0.9 %shard_map.134 = bf16[512,128]{1,0:T(8,128)(2,1)} custom-call(s32[1,64]{1,0:T(1,128)S(1)} %copy-done.6, f32[512,128]{1,0:T(8,128)S(1)} %get-tuple-element.31.local_grad_ref, f32[64,128]{1,0:T(8,128)S(1)} %get-tuple-element.36.own_ref, bf16[128,128]{1,0:T(8,128)(2,1)S(1)} %collective-permute-done.12.refs_0_, ...), custom_call_target="tpu_custom_call" | custom-call | tf_op jit(solution)/shard_map/pallas_call | solution.py:36
  42.4 0.7 %shard_map.136 = (f32[128,128]{1,0:T(8,128)}, f32[128,128]{1,0:T(8,128)}) custom-call(f32[32,128]{1,0:T(8,128)S(1)} %shard_map.135.refs_0_, f32[32,128]{1,0:T(8,128)S(1)} %collective-permute-done.15.refs_1_, f32[32,128]{1,0:T(8,128)S(1)} %collective-permute-done.16.refs_2_, f32[32,128]{1,0:T(8,128)S(1)} %collective-permute-done.17.refs_3_, ...), custom_call_target="tpu_custom_call" | custom-call | tf_op jit(solution)/shard_map/pallas_call | solution.py:36
  (24 shorter events, 0.1 us)
Async XLA Ops:
  0.6 0.9 %copy-start.1 = (bf16[512,128]{1,0:T(8,128)(2,1)S(1)}, bf16[512,128]{1,0:T(8,128)(2,1)}, u32[]{:S(2)}) copy-start(bf16[512,128]{1,0:T(8,128)(2,1)} %features_ref.5) | copy-start | bytes 393220
  1.5 0.7 %copy-start.5 = (s32[1,64]{1,0:T(1,128)S(1)}, s32[1,64]{1,0:T(1,128)}, u32[]{:S(2)}) copy-start(s32[1,64]{1,0:T(1,128)} %pub_ref.3) | copy-start | bytes 772
  2.2 11.5 %copy-start.2 = (bf16[512,256]{1,0:T(8,128)(2,1)S(1)}, bf16[512,256]{1,0:T(8,128)(2,1)}, u32[]{:S(2)}) copy-start(bf16[512,256]{1,0:T(8,128)(2,1)} %bound_ref.1) | copy-start | bytes 786436
  2.4 6.8 %collective-permute-start.5 = (bf16[64,128]{1,0:T(8,128)(2,1)S(1)}, bf16[64,128]{1,0:T(8,128)(2,1)S(1)}, u32[]{:S(2)}, u32[]{:S(2)}) collective-permute-start(bf16[64,128]{1,0:T(8,128)(2,1)S(1)} %shard_map.130.refs_0_), channel_id=1, source_target_pairs={{0,6},{1,7},{2,4},{3,5},{4,2},{5,3},{6,0},{7,1},{8,14},{9,15},{10,... | collective-permute-start | bytes 49160 | tf_op jit(solution)/shard_map/ppermute | solution.py:46
  7.5 4.6 %collective-permute-start.3 = (bf16[64,128]{1,0:T(8,128)(2,1)S(1)}, bf16[64,128]{1,0:T(8,128)(2,1)S(1)}, u32[]{:S(2)}, u32[]{:S(2)}) collective-permute-start(bf16[64,128]{1,0:T(8,128)(2,1)S(1)} %shard_map.130.refs_0_), channel_id=1, source_target_pairs={{0,4},{1,5},{2,6},{3,7},{4,0},{5,1},{6,2},{7,3},{8,12},{9,13},{10,... | collective-permute-start | bytes 49160 | tf_op jit(solution)/shard_map/ppermute | solution.py:46
  7.5 4.6 %collective-permute-start.1 = (bf16[64,128]{1,0:T(8,128)(2,1)S(1)}, bf16[64,128]{1,0:T(8,128)(2,1)S(1)}, u32[]{:S(2)}, u32[]{:S(2)}) collective-permute-start(bf16[64,128]{1,0:T(8,128)(2,1)S(1)} %shard_map.130.refs_0_), channel_id=1, source_target_pairs={{0,2},{1,3},{2,0},{3,1},{4,6},{5,7},{6,4},{7,5},{8,10},{9,11},{10,... | collective-permute-start | bytes 49160 | tf_op jit(solution)/shard_map/ppermute | solution.py:46
  8.2 8.1 %collective-permute-start = (bf16[64,128]{1,0:T(8,128)(2,1)S(1)}, bf16[64,128]{1,0:T(8,128)(2,1)S(1)}, u32[]{:S(2)}, u32[]{:S(2)}) collective-permute-start(bf16[64,128]{1,0:T(8,128)(2,1)S(1)} %shard_map.130.refs_0_), channel_id=1, source_target_pairs={{0,1},{1,0},{2,3},{3,2},{4,5},{5,4},{6,7},{7,6},{8,9},{9,8},{10,11... | collective-permute-start | bytes 49160 | tf_op jit(solution)/shard_map/ppermute | solution.py:46
  8.8 4.9 %copy-start.3 = (bf16[128,128]{1,0:T(8,128)(2,1)S(1)}, bf16[128,128]{1,0:T(8,128)(2,1)}, u32[]{:S(2)}) copy-start(bf16[128,128]{1,0:T(8,128)(2,1)} %w_self_ref.3) | copy-start | bytes 98308
  8.8 4.9 %copy-start.7 = (s32[1,256]{1,0:T(1,128)S(1)}, s32[1,256]{1,0:T(1,128)}, u32[]{:S(2)}) copy-start(s32[1,256]{1,0:T(1,128)} %pos_ref.1) | copy-start | bytes 3076
  8.9 4.9 %copy-start.8 = (s32[1,8]{1,0:T(1,128)S(1)}, s32[1,8]{1,0:T(1,128)}, u32[]{:S(2)}) copy-start(s32[1,8]{1,0:T(1,128)} %count_ref.1) | copy-start | bytes 100
  9.2 7.0 %collective-permute-start.6 = (bf16[64,128]{1,0:T(8,128)(2,1)S(1)}, bf16[64,128]{1,0:T(8,128)(2,1)S(1)}, u32[]{:S(2)}, u32[]{:S(2)}) collective-permute-start(bf16[64,128]{1,0:T(8,128)(2,1)S(1)} %collective-permute-done.5.refs_6_), channel_id=1, source_target_pairs={{0,1},{1,0},{2,3},{3,2},{4,5},{5,4},{6,7},{7,6},{8,9},{9,8},{10,11... | collective-permute-start | bytes 49160 | tf_op jit(solution)/shard_map/ppermute | solution.py:46
  12.2 4.1 %collective-permute-start.4 = (bf16[64,128]{1,0:T(8,128)(2,1)S(1)}, bf16[64,128]{1,0:T(8,128)(2,1)S(1)}, u32[]{:S(2)}, u32[]{:S(2)}) collective-permute-start(bf16[64,128]{1,0:T(8,128)(2,1)S(1)} %collective-permute-done.3.refs_4_), channel_id=1, source_target_pairs={{0,1},{1,0},{2,3},{3,2},{4,5},{5,4},{6,7},{7,6},{8,9},{9,8},{10,11... | collective-permute-start | bytes 49160 | tf_op jit(solution)/shard_map/ppermute | solution.py:46
  12.2 4.1 %collective-permute-start.2 = (bf16[64,128]{1,0:T(8,128)(2,1)S(1)}, bf16[64,128]{1,0:T(8,128)(2,1)S(1)}, u32[]{:S(2)}, u32[]{:S(2)}) collective-permute-start(bf16[64,128]{1,0:T(8,128)(2,1)S(1)} %collective-permute-done.1.refs_2_), channel_id=1, source_target_pairs={{0,1},{1,0},{2,3},{3,2},{4,5},{5,4},{6,7},{7,6},{8,9},{9,8},{10,11... | collective-permute-start | bytes 49160 | tf_op jit(solution)/shard_map/ppermute | solution.py:46
  13.8 1.0 %copy-start = (bf16[512,512]{1,0:T(8,128)(2,1)S(1)}, bf16[512,512]{1,0:T(8,128)(2,1)}, u32[]{:S(2)}) copy-start(bf16[512,512]{1,0:T(8,128)(2,1)} %local_ref.3) | copy-start | bytes 1572868
  14.8 1.5 %copy-start.4 = (bf16[128,128]{1,0:T(8,128)(2,1)S(1)}, bf16[128,128]{1,0:T(8,128)(2,1)}, u32[]{:S(2)}) copy-start(bf16[128,128]{1,0:T(8,128)(2,1)} %w_neigh_ref.1) | copy-start | bytes 98308
  17.6 1.3 %collective-permute-start.7 = (f32[128,128]{1,0:T(8,128)S(1)}, f32[128,128]{1,0:T(8,128)S(1)}, u32[]{:S(2)}, u32[]{:S(2)}) collective-permute-start(f32[128,128]{1,0:T(8,128)S(1)} %get-tuple-element.33), channel_id=1, source_target_pairs={{0,1},{1,0},{2,3},{3,2},{4,5},{5,4},{6,7},{7,6},{8,9},{9,8},{10,11... | collective-permute-start | bytes 196616 | tf_op jit(solution)/shard_map/ppermute | solution.py:46
  17.6 1.4 %collective-permute-start.8 = (bf16[256,128]{1,0:T(8,128)(2,1)S(1)}, bf16[256,128]{1,0:T(8,128)(2,1)S(1)}, u32[]{:S(2)}, u32[]{:S(2)}) collective-permute-start(bf16[256,128]{1,0:T(8,128)(2,1)S(1)} %get-tuple-element.35), channel_id=1, source_target_pairs={{0,1},{1,0},{2,3},{3,2},{4,5},{5,4},{6,7},{7,6},{8,9},{9,8},{10,11... | collective-permute-start | bytes 196616 | tf_op jit(solution)/shard_map/ppermute | solution.py:46
  19.6 3.7 %collective-permute-start.9 = (f32[32,128]{1,0:T(8,128)S(1)}, f32[32,128]{1,0:T(8,128)S(1)}, u32[]{:S(2)}, u32[]{:S(2)}) collective-permute-start(f32[32,128]{1,0:T(8,128)S(1)} %get-tuple-element.39), channel_id=1, source_target_pairs={{0,8},{8,0},{16,24},{24,16},{1,9},{9,1},{17,25},{25,17},{2,10},{10... | collective-permute-start | bytes 49160 | tf_op jit(solution)/shard_map/ppermute | solution.py:46
  21.1 3.7 %collective-permute-start.10 = (f32[32,128]{1,0:T(8,128)S(1)}, f32[32,128]{1,0:T(8,128)S(1)}, u32[]{:S(2)}, u32[]{:S(2)}) collective-permute-start(f32[32,128]{1,0:T(8,128)S(1)} %get-tuple-element.40), channel_id=1, source_target_pairs={{0,16},{8,24},{16,0},{24,8},{1,17},{9,25},{17,1},{25,9},{2,18},{10... | collective-permute-start | bytes 49160 | tf_op jit(solution)/shard_map/ppermute | solution.py:46
  22.6 4.6 %collective-permute-start.11 = (f32[32,128]{1,0:T(8,128)S(1)}, f32[32,128]{1,0:T(8,128)S(1)}, u32[]{:S(2)}, u32[]{:S(2)}) collective-permute-start(f32[32,128]{1,0:T(8,128)S(1)} %get-tuple-element.41), channel_id=1, source_target_pairs={{0,24},{8,16},{16,8},{24,0},{1,25},{9,17},{17,9},{25,1},{2,26},{10... | collective-permute-start | bytes 49160 | tf_op jit(solution)/shard_map/ppermute | solution.py:46
  27.3 4.5 %collective-permute-start.12 = (bf16[128,128]{1,0:T(8,128)(2,1)S(1)}, bf16[128,128]{1,0:T(8,128)(2,1)S(1)}, u32[]{:S(2)}, u32[]{:S(2)}) collective-permute-start(bf16[128,128]{1,0:T(8,128)(2,1)S(1)} %get-tuple-element.42), channel_id=1, source_target_pairs={{0,2},{1,3},{2,0},{3,1},{4,6},{5,7},{6,4},{7,5},{8,10},{9,11},{10,... | collective-permute-start | bytes 98312 | tf_op jit(solution)/shard_map/ppermute | solution.py:46
  27.4 5.2 %collective-permute-start.13 = (bf16[128,128]{1,0:T(8,128)(2,1)S(1)}, bf16[128,128]{1,0:T(8,128)(2,1)S(1)}, u32[]{:S(2)}, u32[]{:S(2)}) collective-permute-start(bf16[128,128]{1,0:T(8,128)(2,1)S(1)} %get-tuple-element.43), channel_id=1, source_target_pairs={{0,4},{1,5},{2,6},{3,7},{4,0},{5,1},{6,2},{7,3},{8,12},{9,13},{10,... | collective-permute-start | bytes 98312 | tf_op jit(solution)/shard_map/ppermute | solution.py:46
  29.3 5.7 %collective-permute-start.14 = (bf16[128,128]{1,0:T(8,128)(2,1)S(1)}, bf16[128,128]{1,0:T(8,128)(2,1)S(1)}, u32[]{:S(2)}, u32[]{:S(2)}) collective-permute-start(bf16[128,128]{1,0:T(8,128)(2,1)S(1)} %get-tuple-element.44), channel_id=1, source_target_pairs={{0,6},{1,7},{2,4},{3,5},{4,2},{5,3},{6,0},{7,1},{8,14},{9,15},{10,... | collective-permute-start | bytes 98312 | tf_op jit(solution)/shard_map/ppermute | solution.py:46
  35.0 4.7 %collective-permute-start.17 = (f32[32,128]{1,0:T(8,128)S(1)}, f32[32,128]{1,0:T(8,128)S(1)}, u32[]{:S(2)}, u32[]{:S(2)}) collective-permute-start(f32[32,128]{1,0:T(8,128)S(1)} %shard_map.135.refs_0_), channel_id=1, source_target_pairs={{0,24},{8,16},{16,8},{24,0},{1,25},{9,17},{17,9},{25,1},{2,26},{10... | collective-permute-start | bytes 49160 | tf_op jit(solution)/shard_map/ppermute | solution.py:46
  35.6 4.2 %collective-permute-start.16 = (f32[32,128]{1,0:T(8,128)S(1)}, f32[32,128]{1,0:T(8,128)S(1)}, u32[]{:S(2)}, u32[]{:S(2)}) collective-permute-start(f32[32,128]{1,0:T(8,128)S(1)} %shard_map.135.refs_0_), channel_id=1, source_target_pairs={{0,16},{8,24},{16,0},{24,8},{1,17},{9,25},{17,1},{25,9},{2,18},{10... | collective-permute-start | bytes 49160 | tf_op jit(solution)/shard_map/ppermute | solution.py:46
  37.1 3.7 %collective-permute-start.15 = (f32[32,128]{1,0:T(8,128)S(1)}, f32[32,128]{1,0:T(8,128)S(1)}, u32[]{:S(2)}, u32[]{:S(2)}) collective-permute-start(f32[32,128]{1,0:T(8,128)S(1)} %shard_map.135.refs_0_), channel_id=1, source_target_pairs={{0,8},{8,0},{16,24},{24,16},{1,9},{9,1},{17,25},{25,17},{2,10},{10... | collective-permute-start | bytes 49160 | tf_op jit(solution)/shard_map/ppermute | solution.py:46
  38.6 3.8 %collective-permute-start.18 = (f32[32,128]{1,0:T(8,128)S(1)}, f32[32,128]{1,0:T(8,128)S(1)}, u32[]{:S(2)}, u32[]{:S(2)}) collective-permute-start(f32[32,128]{1,0:T(8,128)S(1)} %shard_map.135.refs_0_), channel_id=1, source_target_pairs={{0,1},{1,0},{2,3},{3,2},{4,5},{5,4},{6,7},{7,6},{8,9},{9,8},{10,11... | collective-permute-start | bytes 49160 | tf_op jit(solution)/shard_map/ppermute | solution.py:46
  39.7 2.6 %collective-permute-start.21 = (f32[32,128]{1,0:T(8,128)S(1)}, f32[32,128]{1,0:T(8,128)S(1)}, u32[]{:S(2)}, u32[]{:S(2)}) collective-permute-start(f32[32,128]{1,0:T(8,128)S(1)} %collective-permute-done.17.refs_3_), channel_id=1, source_target_pairs={{0,1},{1,0},{2,3},{3,2},{4,5},{5,4},{6,7},{7,6},{8,9},{9,8},{10,11... | collective-permute-start | bytes 49160 | tf_op jit(solution)/shard_map/ppermute | solution.py:46
  39.7 2.6 %collective-permute-start.20 = (f32[32,128]{1,0:T(8,128)S(1)}, f32[32,128]{1,0:T(8,128)S(1)}, u32[]{:S(2)}, u32[]{:S(2)}) collective-permute-start(f32[32,128]{1,0:T(8,128)S(1)} %collective-permute-done.16.refs_2_), channel_id=1, source_target_pairs={{0,1},{1,0},{2,3},{3,2},{4,5},{5,4},{6,7},{7,6},{8,9},{9,8},{10,11... | collective-permute-start | bytes 49160 | tf_op jit(solution)/shard_map/ppermute | solution.py:46
  40.8 1.5 %collective-permute-start.19 = (f32[32,128]{1,0:T(8,128)S(1)}, f32[32,128]{1,0:T(8,128)S(1)}, u32[]{:S(2)}, u32[]{:S(2)}) collective-permute-start(f32[32,128]{1,0:T(8,128)S(1)} %collective-permute-done.15.refs_1_), channel_id=1, source_target_pairs={{0,1},{1,0},{2,3},{3,2},{4,5},{5,4},{6,7},{7,6},{8,9},{9,8},{10,11... | collective-permute-start | bytes 49160 | tf_op jit(solution)/shard_map/ppermute | solution.py:46
  40.8 0.7 %copy-start.6 = (s32[1,64]{1,0:T(1,128)S(1)}, s32[1,64]{1,0:T(1,128)}, u32[]{:S(2)}) copy-start(s32[1,64]{1,0:T(1,128)} %pub_ref.3) | copy-start | bytes 772

commit v2 on v1

v2 whole, which is shorter than its diff:
```python
import functools
import math

import jax
import jax.numpy as jnp
from jax import lax
from jax.experimental import pallas as pl
from jax.experimental.pallas import tpu as pltpu
from jax.sharding import PartitionSpec as P

BF = jnp.bfloat16
F32 = jnp.float32
VMEM = pl.BlockSpec(memory_space=pltpu.VMEM)
HBM = pl.BlockSpec(memory_space=pltpu.HBM)
PARAMS = pltpu.CompilerParams(vmem_limit_bytes=48 * 1024 * 1024)


def dot(a, b):
    return jnp.dot(a, b, preferred_element_type=F32)


def dot_t(a, b):
    return lax.dot_general(a, b, (((0,), (0,)), ((), ())), preferred_element_type=F32)


def dot_nt(a, b):
    return lax.dot_general(a, b, (((1,), (1,)), ((), ())), preferred_element_type=F32)


def one_hot(rows, targets):
    row = lax.broadcasted_iota(jnp.int32, (rows, targets.shape[1]), 0)
    return jnp.where(row == targets, 1.0, 0.0).astype(BF)


def in_hbm(x):
    return pltpu.with_memory_space_constraint(x, pltpu.HBM)


def call(body, outs, *args):
    return pl.pallas_call(
        body,
        out_shape=[jax.ShapeDtypeStruct(shape, dtype) for shape, dtype in outs],
        in_specs=[VMEM] * len(args),
        out_specs=[VMEM] * len(outs),
        compiler_params=PARAMS,
    )(*args)


def odd_core():
    return lax.axis_index("dom") % 2 == 1


def tree_sum(parts):
    while len(parts) > 1:
        parts = [a + b for a, b in zip(parts[::2], parts[1::2])]
    return parts[0]


def load(pairs, sems):
    copies = [pltpu.make_async_copy(a, b, sems.at[i]) for i, (a, b) in enumerate(pairs)]
    for copy in copies:
        copy.start()
    return copies


def publish_body(count, *refs):
    sources, (out_ref, *targets), sems = refs[:count], refs[count:-1], refs[-1]
    pub, rows, *rest = load(list(zip(sources, targets)), sems)
    pub_ref, features_ref = targets[:2]
    pub_count = pub_ref.shape[1]
    square = (pub_count, pub_count)
    pub.wait()
    diagonal = lax.broadcasted_iota(jnp.int32, square, 0) == lax.broadcasted_iota(jnp.int32, square, 1)
    column = jnp.sum(jnp.where(diagonal, pub_ref[...].astype(F32), 0.0), axis=1, keepdims=True)
    row = lax.broadcasted_iota(jnp.int32, (pub_count, features_ref.shape[0]), 1)
    pick = jnp.where(row == column.astype(jnp.int32), 1.0, 0.0).astype(BF)
    rows.wait()
    out_ref[...] = dot(pick, features_ref[...]).astype(BF)
    for copy in rest:
        copy.wait()


def pair_body(own_ref, other_ref, out_ref):
    rows = own_ref.shape[0]
    odd = odd_core()
    own, other = own_ref[...], other_ref[...]
    out_ref[:rows, :] = jnp.where(odd, other, own)
    out_ref[rows:, :] = jnp.where(odd, own, other)


def prepare_body(
    dom_size,
    pub_ref,
    features_ref,
    local_ref,
    bound_ref,
    w_self_ref,
    pos_ref,
    count_ref,
    mask_ref,
    cot_ref,
    place_ref,
    adj_ref,
    flip_ref,
    part_ref,
    inv_ref,
    self_ref,
    chosen_ref,
):
    pub_count = pub_ref.shape[1]
    place_ref[...] = one_hot(features_ref.shape[0], pub_ref[...])
    features = features_ref[...]
    self_ref[...] = dot(features, w_self_ref[...])
    me = lax.axis_index("dom")
    chip = me - me % 2
    slots = pos_ref.shape[1]
    slot_rows = slots // dom_size
    lane = lax.broadcasted_iota(jnp.int32, (1, slots), 1)
    peer = lane // slot_rows
    limit = jnp.zeros((1, slots), jnp.int32)
    for j in range(dom_size):
        limit = jnp.where(peer == j, count_ref[0:1, j : j + 1], limit)
    in_use = lane % slot_rows < limit
    target = jnp.where(in_use, (peer ^ chip) * pub_count + pos_ref[...], -1)
    columns = dom_size * pub_count
    chunk = math.gcd(columns, 512)

    def move(c, total):
        here = pl.ds(pl.multiple_of(c * chunk, chunk), chunk)
        moves = one_hot(chunk, target - c * chunk)
        block = dot_nt(bound_ref[...], moves).astype(BF)
        adj_ref[:, here] = block
        flip_ref[here, :] = dot_nt(moves, bound_ref[...]).astype(BF)
        return total + dot(block, jnp.ones((chunk, features.shape[1]), BF))

    sums = lax.fori_loop(0, columns // chunk, move, jnp.zeros(features.shape, F32))
    first = lax.broadcasted_iota(jnp.int32, (8, mask_ref.shape[1]), 0) == 0
    mask = jnp.where(first & (mask_ref[...] > 0), 1.0, 0.0).astype(BF)
    chosen = dot_t(mask, jnp.ones((8, features.shape[1]), BF))
    chosen_ref[...] = (cot_ref[...].astype(F32) * chosen).astype(BF)
    part_ref[...] = dot(local_ref[...], features)
    inv_ref[...] = 1.0 / (1.0 + sums + dot(local_ref[...], jnp.ones(features.shape, BF)))


def layer_body(
    z_size,
    features_ref,
    adj_ref,
    flip_ref,
    part_ref,
    inv_ref,
    self_ref,
    w_neigh_ref,
    cot_ref,
    *refs,
):
    pairs, refs = refs[:z_size], refs[z_size:]
    hidden_ref, pre_ref, agg_ref, weights_ref, grads_ref, rounded_ref, rows_ref = refs
    count = pairs[0].shape[0]
    for z, pair in enumerate(pairs):
        rows_ref[z * count : (z + 1) * count, :] = pair[...]
    inv = inv_ref[...]
    aggregate = ((part_ref[...] + dot(adj_ref[...], rows_ref[...])) * inv).astype(BF)
    preact = self_ref[...] + dot(aggregate, w_neigh_ref[...])
    sigma = jax.nn.sigmoid(preact)
    hidden_ref[...] = (preact * sigma).astype(BF)
    slope = sigma * (1.0 + preact * (1.0 - sigma))
    grad_pre = (cot_ref[...].astype(F32) * slope).astype(BF)
    grad_agg = (dot_nt(grad_pre, w_neigh_ref[...]) * inv).astype(BF)
    pre_ref[...] = grad_pre
    agg_ref[...] = grad_agg
    width = features_ref.shape[1]
    weights_ref[:width, :] = dot_t(features_ref[...], grad_pre)
    weights_ref[width:, :] = dot_t(aggregate, grad_pre)
    grads = dot(flip_ref[...], grad_agg)
    grads_ref[...] = grads
    rounded_ref[...] = grads.astype(BF)


def local_body(local_ref, w_self_ref, pre_ref, agg_ref, out_ref):
    out_ref[...] = dot_nt(pre_ref[...], w_self_ref[...]) + dot_t(local_ref[...], agg_ref[...])


def chip_body(weights_ref, got_w_ref, grads_ref, got_g_ref, own_ref, total_ref, *messages):
    grads = grads_ref[...] + got_g_ref[...].astype(F32)
    rows = own_ref.shape[0]
    own_ref[...] = grads[:rows]
    total = (weights_ref[...] + got_w_ref[...]).astype(BF)
    total_ref[...] = total
    for z, message in zip(range(len(messages), 0, -1), messages):
        message[:rows, :] = grads[z * rows : (z + 1) * rows].astype(BF)
        message[rows:, :] = total


def column_body(scale, total_ref, own_ref, *refs):
    messages, (out_ref, even_ref, odd_ref) = refs[:-3], refs[-3:]
    rows = own_ref.shape[0]
    parts = [total_ref[...]] + [message[rows:, :] for message in messages]
    out_ref[...] = (tree_sum([part.astype(F32) for part in parts]) * scale).astype(BF)
    grads = own_ref[...]
    for message in messages:
        grads = grads + message[:rows, :].astype(F32)
    even_ref[...] = grads[: rows // 2]
    odd_ref[...] = grads[rows // 2 :]


def features_body(hidden_ref, place_ref, local_grad_ref, odd_ref, even_ref, hidden_out, out_ref):
    hidden_out[...] = hidden_ref[...]
    total = jnp.where(odd_core(), odd_ref[...], even_ref[...])
    place = place_ref[...]
    high = total.astype(BF)
    low = (total - high.astype(F32)).astype(BF)
    out_ref[...] = (local_grad_ref[...] + dot(place, high) + dot(place, low)).astype(BF)


def sum_body(*refs):
    refs[-1][...] = tree_sum([part[...].astype(F32) for part in refs[:-1]])


def order_body(mine_ref, other_ref, self_ref, neigh_ref):
    total = jnp.where(odd_core(), mine_ref[...], other_ref[...])
    width = self_ref.shape[0]
    self_ref[...] = total[:width]
    neigh_ref[...] = total[width:]


def local(
    features,
    adj_local,
    adj_bound,
    w_self,
    w_neigh,
    pub_rows,
    recv_pos,
    recv_count,
    target_mask,
    cotangent,
):
    dom_size, group_size = lax.axis_size("dom"), lax.axis_size("group")
    z_size = dom_size // 2
    row_count, width = features.shape
    pub_count = pub_rows.shape[1]
    wide = (row_count, width)
    devices = range(group_size * dom_size)

    def exchange(x, odd_step, even_step):
        return lax.ppermute(x, ("group", "dom"), [(a, a ^ (odd_step if a % 2 else even_step)) for a in devices])

    def over_core(x):
        return exchange(x, 1, 1)

    fetched = (
        pub_rows,
        features,
        adj_local,
        adj_bound,
        w_self,
        w_neigh,
        recv_pos,
        recv_count,
        target_mask.reshape(1, row_count),
        cotangent,
    )
    published, *fetched = pl.pallas_call(
        functools.partial(publish_body, len(fetched)),
        out_shape=[jax.ShapeDtypeStruct((pub_count, width), BF)]
        + [jax.ShapeDtypeStruct(x.shape, x.dtype) for x in fetched],
        in_specs=[HBM] * len(fetched),
        out_specs=[VMEM] * (1 + len(fetched)),
        scratch_shapes=[pltpu.SemaphoreType.DMA((len(fetched),))],
        compiler_params=PARAMS,
    )(*(in_hbm(x) for x in fetched))
    pub_rows, features, adj_local, adj_bound, w_self, w_neigh, recv_pos, recv_count, mask, cotangent = fetched
    (pair,) = call(pair_body, [((2 * pub_count, width), BF)], published, over_core(published))
    pairs = [pair] + [exchange(pair, 2 * z, 2 * z) for z in range(1, z_size)]

    columns = dom_size * pub_count
    place, adj_rows, adj_flip, part, inverse, own_part, chosen = call(
        functools.partial(prepare_body, dom_size),
        [
            ((row_count, pub_count), BF),
            ((row_count, columns), BF),
            ((columns, row_count), BF),
            (wide, F32),
            (wide, F32),
            (wide, F32),
            (wide, BF),
        ],
        pub_rows,
        features,
        adj_local,
        adj_bound,
        w_self,
        recv_pos,
        recv_count,
        mask,
        cotangent,
    )
    square, both = (width, width), (2 * width, width)
    hidden, grad_pre, grad_agg, weights, grads, rounded = pl.pallas_call(
        functools.partial(layer_body, z_size),
        out_shape=[
            jax.ShapeDtypeStruct(s, d)
            for s, d in [
                (wide, BF),
                (wide, BF),
                (wide, BF),
                (both, F32),
                ((columns, width), F32),
                ((columns, width), BF),
            ]
        ],
        in_specs=[VMEM] * (8 + z_size),
        out_specs=[VMEM] * 6,
        scratch_shapes=[pltpu.VMEM((columns, width), BF)],
        compiler_params=PARAMS,
    )(features, adj_rows, adj_flip, part, inverse, own_part, w_neigh, chosen, *pairs)
    (local_grad,) = call(local_body, [(wide, F32)], adj_local, w_self, grad_pre, grad_agg)

    message = ((2 * pub_count + 2 * width, width), BF)
    own_g, chip_w, *messages = call(
        chip_body,
        [((2 * pub_count, width), F32), (both, BF)] + [message] * (z_size - 1),
        weights,
        over_core(weights),
        grads,
        over_core(rounded),
    )
    far = range(z_size - 1, 0, -1)
    arrived = [exchange(x, 2 * z, dom_size) for z, x in zip(far, messages)][::-1]
    scale = 1.0 / math.sqrt(row_count * group_size * dom_size // 8)
    column_w, even_g, odd_g = call(
        functools.partial(column_body, scale),
        [(both, BF)] + [((pub_count, width), F32)] * 2,
        chip_w,
        own_g,
        *arrived,
    )
    others = [exchange(column_w, dom_size * k, 2) for k in range(1, group_size)]
    *others, even_g, local_grad = lax.optimization_barrier((*others, over_core(even_g), local_grad))
    hidden, grad_features = call(features_body, [(wide, BF)] * 2, hidden, place, local_grad, odd_g, even_g)
    (mine,) = call(sum_body, [(both, F32)], column_w, *others)
    grad_self, grad_neigh = call(order_body, [(square, F32)] * 2, mine, over_core(mine))
    return hidden, grad_features, grad_self, grad_neigh


def solution(mesh):
    rows = P(("group", "dom"), None)
    in_specs = (rows, rows, rows, P(), P(), rows, rows, rows, P(("group", "dom")), rows)
    return jax.shard_map(
        local, mesh=mesh, in_specs=in_specs, out_specs=(rows, rows, P(), P()), check_vma=False
    )
```

time: 43.4 us -> 31.8 us (0.73)
  starting transfers between devices: 19 us -> 13.4 us
  local copies, waits for them, and re-layouts: 3.26 us -> 0 us
  other arithmetic: 1.72 us -> 0 us
  waiting for transfers between devices: 13.2 us -> 12 us
    ppermute x22 -> x14, starting transfers between devices: 19 us -> 13.4 us  [exchange(): lax.ppermute(x, ('group', 'dom'), [(a, a ^ (odd_step if a % 2 else even_s...]
    unnamed x18 -> x0, local copies, waits for them, and re-layouts: 3.26 us -> none
    ppermute x22 -> x14, waiting for transfers between devices: 13.2 us -> 12 us  [exchange(): lax.ppermute(x, ('group', 'dom'), [(a, a ^ (odd_step if a % 2 else even_s...]
    pallas_call x1 -> x2, Pallas kernels: 1.3 us -> 2.39 us  [the longest x1 1.39 us: local(): pl.pallas_call(functools.partial(publish_body, len(fetched)), out_shape=[...]
    select_n x1 -> x0, other arithmetic: 1.04 us -> none  [local(): chosen = jnp.where(target_mask[:, None] > 0, cotangent, jnp.zeros((), BF))]
    pallas_call x7 -> x8, Pallas kernels: 3.82 us -> 3.1 us  [call(): pl.pallas_call(body, out_shape=[jax.ShapeDtypeStruct(shape, dtype) for sh...]
    gt x1 -> x0, other arithmetic: 0.69 us -> none  [local(): chosen = jnp.where(target_mask[:, None] > 0, cotangent, jnp.zeros((), BF))]
  transfers between devices with their start and end apart: 22 -> 14, of which waited for: 11 -> 13; matrix products, arithmetic and copies ran while one was open for 4% -> 0% of each run, Pallas kernels for 5% -> 7%
where the time goes in v2:
time: 31.8 us; the launch traced here: 31.6 us
  starting transfers between devices  13.4 us (42%)
  waiting for transfers between devices  12 us (38%)
  Pallas kernels  5.49 us (17%)
  between operations  0.71 us (2%)
    ppermute x14, starting transfers between devices, exchange(): lax.ppermute(x, ('group', 'dom'), [(a, a ^ (odd_step if a % 2 else even_s...  13.4 us
    ppermute x14, waiting for transfers between devices, exchange(): lax.ppermute(x, ('group', 'dom'), [(a, a ^ (odd_step if a % 2 else even_s...  12 us
    pallas_call x8, Pallas kernels, call(): pl.pallas_call(body, out_shape=[jax.ShapeDtypeStruct(shape, dtype) for sh...  3.1 us
    pallas_call x1, Pallas kernels, local(): pl.pallas_call(functools.partial(publish_body, len(fetched)), out_shape=[...  1.39 us
    pallas_call x1, Pallas kernels, local(): pl.pallas_call(functools.partial(layer_body, z_size), out_shape=[jax.Shap...  1 us
  transfers between devices with their start and end apart: 14, of which 13 were waited for; matrix products, arithmetic and copies ran while one was open for 0% of the time, Pallas kernels for 7%

profile of v2, /device:TPU:0, one launch (start us, length us, event | category | flops | bytes accessed | tf_op | source)
XLA Modules:
  0.0 31.6 jit_solution(2661308339331000664)
XLA Ops:
  0.6 1.4 %shard_map.129 = (bf16[64,128]{1,0:T(8,128)(2,1)S(1)}, s32[1,64]{1,0:T(1,128)S(1)}, bf16[512,128]{1,0:T(8,128)(2,1)S(1)}, bf16[512,512]{1,0:T(8,128)(2,1)S(1)}, ...) custom-call(s32[1,64]{1,0:T(1,128)} %refs_0_.1, ...), custom_call_target="tpu_custom_call" | custom-call | tf_op jit(solution)/shard_map/pallas_call | solution.py:264
  2.0 0.5 %collective-permute-start = (bf16[64,128]{1,0:T(8,128)(2,1)S(1)}, bf16[64,128]{1,0:T(8,128)(2,1)S(1)}, u32[]{:S(2)}, u32[]{:S(2)}) collective-permute-start(bf16[64,128]{1,0:T(8,128)(2,1)S(1)} %get-tuple-element.61.own_ref), channel_id=1, source_target_pairs={{0,1},{1,0},{2,3},{3,2},{4,5},{5,4},{6,7},{7,6},{8,9},{9,8},{10,11... | collective-permute-start | bytes 49160 | tf_op jit(solution)/shard_map/ppermute | solution.py:247
  2.5 0.8 %collective-permute-done.other_ref = bf16[64,128]{1,0:T(8,128)(2,1)S(1)} collective-permute-done((bf16[64,128]{1,0:T(8,128)(2,1)S(1)}, bf16[64,128]{1,0:T(8,128)(2,1)S(1)}, u32[]{:S(2)}, u32[]{:S(2)}) %collective-permute-start) | collective-permute-done | bytes 16416 | tf_op jit(solution)/shard_map/ppermute | solution.py:247
  3.4 5.0 %collective-permute-start.3 = (bf16[128,128]{1,0:T(8,128)(2,1)S(1)}, bf16[128,128]{1,0:T(8,128)(2,1)S(1)}, u32[]{:S(2)}, u32[]{:S(2)}) collective-permute-start(bf16[128,128]{1,0:T(8,128)(2,1)S(1)} %shard_map.131.refs_0_), channel_id=1, source_target_pairs={{0,6},{1,7},{2,4},{3,5},{4,2},{5,3},{6,0},{7,1},{8,14},{9,15},{10,... | collective-permute-start | bytes 98312 | tf_op jit(solution)/shard_map/ppermute | solution.py:247
  8.4 0.0 collective-permute-start.2
  8.4 0.6 %collective-permute-start.1 = (bf16[128,128]{1,0:T(8,128)(2,1)S(1)}, bf16[128,128]{1,0:T(8,128)(2,1)S(1)}, u32[]{:S(2)}, u32[]{:S(2)}) collective-permute-start(bf16[128,128]{1,0:T(8,128)(2,1)S(1)} %shard_map.131.refs_0_), channel_id=1, source_target_pairs={{0,2},{1,3},{2,0},{3,1},{4,6},{5,7},{6,4},{7,5},{8,10},{9,11},{10,... | collective-permute-start | bytes 98312 | tf_op jit(solution)/shard_map/ppermute | solution.py:247
  9.0 1.0 %shard_map.130 = (bf16[512,64]{1,0:T(8,128)(2,1)S(1)}, bf16[512,512]{1,0:T(8,128)(2,1)S(1)}, bf16[512,512]{1,0:T(8,128)(2,1)S(1)}, f32[512,128]{1,0:T(8,128)S(1)...) custom-call(s32[1,64]{1,0:T(1,128)S(1)} %get-tuple-element.46.pub_ref, ...), custom_call_target="tpu_custom_call" | custom-call | tf_op jit(solution)/shard_map/pallas_call | solution.py:40
  10.1 0.2 collective-permute-done.3.refs_3_
  10.3 2.9 %collective-permute-done.2.refs_2_ = bf16[128,128]{1,0:T(8,128)(2,1)S(1)} collective-permute-done((bf16[128,128]{1,0:T(8,128)(2,1)S(1)}, bf16[128,128]{1,0:T(8,128)(2,1)S(1)}, u32[]{:S(2)}, u32[]{:S(2)}) %collective-permute-start.2) | collective-permute-done | bytes 32800 | tf_op jit(solution)/shard_map/ppermute | solution.py:247
  13.2 0.0 collective-permute-done.1.refs_1_
  13.2 1.0 %shard_map.132 = (bf16[512,128]{1,0:T(8,128)(2,1)S(1)}, bf16[512,128]{1,0:T(8,128)(2,1)S(1)}, bf16[512,128]{1,0:T(8,128)(2,1)S(1)}, f32[256,128]{1,0:T(8,128)S(1...) custom-call(bf16[512,128]{1,0:T(8,128)(2,1)S(1)} %get-tuple-element.45.features_ref, ...), custom_call_target="tpu_custom_call" | custom-call | tf_op jit(solution)/shard_map/pallas_call | solution.py:300
  14.2 0.1 collective-permute-start.5
  14.3 0.5 %collective-permute-start.4 = (f32[256,128]{1,0:T(8,128)S(1)}, f32[256,128]{1,0:T(8,128)S(1)}, u32[]{:S(2)}, u32[]{:S(2)}) collective-permute-start(f32[256,128]{1,0:T(8,128)S(1)} %get-tuple-element.64.weights_ref), channel_id=1, source_target_pairs={{0,1},{1,0},{2,3},{3,2},{4,5},{5,4},{6,7},{7,6},{8,9},{9,8},{10,11... | collective-permute-start | bytes 393224 | tf_op jit(solution)/shard_map/ppermute | solution.py:247
  14.8 0.8 %collective-permute-done.5.got_g_ref = bf16[512,128]{1,0:T(8,128)(2,1)S(1)} collective-permute-done((bf16[512,128]{1,0:T(8,128)(2,1)S(1)}, bf16[512,128]{1,0:T(8,128)(2,1)S(1)}, u32[]{:S(2)}, u32[]{:S(2)}) %collective-permute-start.5) | collective-permute-done | bytes 131104 | tf_op jit(solution)/shard_map/ppermute | solution.py:247
  15.6 0.2 collective-permute-done.4.got_w_ref
  15.9 1.6 %collective-permute-start.6 = (bf16[384,128]{1,0:T(8,128)(2,1)S(1)}, bf16[384,128]{1,0:T(8,128)(2,1)S(1)}, u32[]{:S(2)}, u32[]{:S(2)}) collective-permute-start(bf16[384,128]{1,0:T(8,128)(2,1)S(1)} %get-tuple-element.69), channel_id=1, source_target_pairs={{0,8},{1,3},{2,10},{3,1},{4,12},{5,7},{6,14},{7,5},{8,0},{9,11},{1... | collective-permute-start | bytes 294920 | tf_op jit(solution)/shard_map/ppermute | solution.py:247
  17.4 0.5 %collective-permute-start.7 = (bf16[384,128]{1,0:T(8,128)(2,1)S(1)}, bf16[384,128]{1,0:T(8,128)(2,1)S(1)}, u32[]{:S(2)}, u32[]{:S(2)}) collective-permute-start(bf16[384,128]{1,0:T(8,128)(2,1)S(1)} %get-tuple-element.70), channel_id=1, source_target_pairs={{0,8},{1,5},{2,10},{3,7},{4,12},{5,1},{6,14},{7,3},{8,0},{9,13},{1... | collective-permute-start | bytes 294920 | tf_op jit(solution)/shard_map/ppermute | solution.py:247
  18.0 1.5 %collective-permute-start.8 = (bf16[384,128]{1,0:T(8,128)(2,1)S(1)}, bf16[384,128]{1,0:T(8,128)(2,1)S(1)}, u32[]{:S(2)}, u32[]{:S(2)}) collective-permute-start(bf16[384,128]{1,0:T(8,128)(2,1)S(1)} %get-tuple-element.71), channel_id=1, source_target_pairs={{0,8},{1,7},{2,10},{3,5},{4,12},{5,3},{6,14},{7,1},{8,0},{9,15},{1... | collective-permute-start | bytes 294920 | tf_op jit(solution)/shard_map/ppermute | solution.py:247
  19.5 1.1 %collective-permute-done.6.refs_0_ = bf16[384,128]{1,0:T(8,128)(2,1)S(1)} collective-permute-done((bf16[384,128]{1,0:T(8,128)(2,1)S(1)}, bf16[384,128]{1,0:T(8,128)(2,1)S(1)}, u32[]{:S(2)}, u32[]{:S(2)}) %collective-permute-start.6) | collective-permute-done | bytes 98336 | tf_op jit(solution)/shard_map/ppermute | solution.py:247
  20.6 1.5 %collective-permute-done.7.refs_1_ = bf16[384,128]{1,0:T(8,128)(2,1)S(1)} collective-permute-done((bf16[384,128]{1,0:T(8,128)(2,1)S(1)}, bf16[384,128]{1,0:T(8,128)(2,1)S(1)}, u32[]{:S(2)}, u32[]{:S(2)}) %collective-permute-start.7) | collective-permute-done | bytes 98336 | tf_op jit(solution)/shard_map/ppermute | solution.py:247
  22.1 1.1 %collective-permute-done.8.refs_2_ = bf16[384,128]{1,0:T(8,128)(2,1)S(1)} collective-permute-done((bf16[384,128]{1,0:T(8,128)(2,1)S(1)}, bf16[384,128]{1,0:T(8,128)(2,1)S(1)}, u32[]{:S(2)}, u32[]{:S(2)}) %collective-permute-start.8) | collective-permute-done | bytes 98336 | tf_op jit(solution)/shard_map/ppermute | solution.py:247
  23.1 0.1 shard_map.134
  23.2 0.1 collective-permute-start.11
  23.3 2.0 %collective-permute-start.10 = (bf16[256,128]{1,0:T(8,128)(2,1)S(1)}, bf16[256,128]{1,0:T(8,128)(2,1)S(1)}, u32[]{:S(2)}, u32[]{:S(2)}) collective-permute-start(bf16[256,128]{1,0:T(8,128)(2,1)S(1)} %get-tuple-element.72.refs_0_), channel_id=1, source_target_pairs={{0,2},{1,17},{2,0},{3,19},{4,6},{5,21},{6,4},{7,23},{8,10},{9,25},... | collective-permute-start | bytes 196616 | tf_op jit(solution)/shard_map/ppermute | solution.py:247
  25.3 0.1 collective-permute-start.9
  25.3 0.8 %collective-permute-start.12 = (f32[64,128]{1,0:T(8,128)S(1)}, f32[64,128]{1,0:T(8,128)S(1)}, u32[]{:S(2)}, u32[]{:S(2)}) collective-permute-start(f32[64,128]{1,0:T(8,128)S(1)} %get-tuple-element.73), channel_id=1, source_target_pairs={{0,1},{1,0},{2,3},{3,2},{4,5},{5,4},{6,7},{7,6},{8,9},{9,8},{10,11... | collective-permute-start | bytes 98312 | tf_op jit(solution)/shard_map/ppermute | solution.py:247
  26.2 0.4 %shard_map.135.local_grad_ref = f32[512,128]{1,0:T(8,128)S(1)} custom-call(bf16[512,512]{1,0:T(8,128)(2,1)S(1)} %get-tuple-element.47.local_ref, bf16[128,128]{1,0:T(8,128)(2,1)S(1)} %get-tuple-element.49.w_self_ref, bf16[512,128]{1,0:T(8,128)(2,1)S(1)} %get-tuple-element.74.pre_ref, bf16[512,128]{1,0:T(8,128)(2,1)S(1)} %get-tuple-element.75.agg_ref), custom_call_target="tpu_custom_call" | custom-call | tf_op jit(solution)/shard_map/pallas_call | solution.py:40
  26.6 0.5 %collective-permute-done.12.even_ref = f32[64,128]{1,0:T(8,128)S(1)} collective-permute-done((f32[64,128]{1,0:T(8,128)S(1)}, f32[64,128]{1,0:T(8,128)S(1)}, u32[]{:S(2)}, u32[]{:S(2)}) %collective-permute-start.12) | collective-permute-done | bytes 32800 | tf_op jit(solution)/shard_map/ppermute | solution.py:247
  27.0 0.5 %collective-permute-done.11.refs_3_ = bf16[256,128]{1,0:T(8,128)(2,1)S(1)} collective-permute-done((bf16[256,128]{1,0:T(8,128)(2,1)S(1)}, bf16[256,128]{1,0:T(8,128)(2,1)S(1)}, u32[]{:S(2)}, u32[]{:S(2)}) %collective-permute-start.11) | collective-permute-done | bytes 65568 | tf_op jit(solution)/shard_map/ppermute | solution.py:247
  27.5 0.7 %collective-permute-done.10.refs_2_ = bf16[256,128]{1,0:T(8,128)(2,1)S(1)} collective-permute-done((bf16[256,128]{1,0:T(8,128)(2,1)S(1)}, bf16[256,128]{1,0:T(8,128)(2,1)S(1)}, u32[]{:S(2)}, u32[]{:S(2)}) %collective-permute-start.10) | collective-permute-done | bytes 65568 | tf_op jit(solution)/shard_map/ppermute | solution.py:247
  28.2 1.3 %collective-permute-done.9.refs_1_ = bf16[256,128]{1,0:T(8,128)(2,1)S(1)} collective-permute-done((bf16[256,128]{1,0:T(8,128)(2,1)S(1)}, bf16[256,128]{1,0:T(8,128)(2,1)S(1)}, u32[]{:S(2)}, u32[]{:S(2)}) %collective-permute-start.9) | collective-permute-done | bytes 65568 | tf_op jit(solution)/shard_map/ppermute | solution.py:247
  29.6 0.1 collective-permute-start.13
  29.6 0.9 %shard_map.136 = (bf16[512,128]{1,0:T(8,128)(2,1)}, bf16[512,128]{1,0:T(8,128)(2,1)}) custom-call(bf16[512,128]{1,0:T(8,128)(2,1)S(1)} %get-tuple-element.62.hidden_ref, bf16[512,64]{1,0:T(8,128)(2,1)S(1)} %get-tuple-element.63.place_ref, f32[512,128]{1,0:T(8,128)S(1)} %shard_map.135.local_grad_ref, f32[64,128]{1,0:T(8,128)S(1)} %get-tuple-element.77.odd_ref, ...), custom_call_target="tpu_custom_call" | custom-call | tf_op jit(solution)/shard_map/pallas_call | solution.py:40
  30.5 0.5 %collective-permute-done.13.other_ref = f32[256,128]{1,0:T(8,128)S(1)} collective-permute-done((f32[256,128]{1,0:T(8,128)S(1)}, f32[256,128]{1,0:T(8,128)S(1)}, u32[]{:S(2)}, u32[]{:S(2)}) %collective-permute-start.13) | collective-permute-done | bytes 131104 | tf_op jit(solution)/shard_map/ppermute | solution.py:247
  31.0 0.7 %shard_map.138 = (f32[128,128]{1,0:T(8,128)}, f32[128,128]{1,0:T(8,128)}) custom-call(f32[256,128]{1,0:T(8,128)S(1)} %shard_map.137.mine_ref, f32[256,128]{1,0:T(8,128)S(1)} %collective-permute-done.13.other_ref), custom_call_target="tpu_custom_call" | custom-call | tf_op jit(solution)/shard_map/pallas_call | solution.py:40
  (3 shorter events, 0.1 us)
Async XLA Ops:
  2.0 1.4 %collective-permute-start = (bf16[64,128]{1,0:T(8,128)(2,1)S(1)}, bf16[64,128]{1,0:T(8,128)(2,1)S(1)}, u32[]{:S(2)}, u32[]{:S(2)}) collective-permute-start(bf16[64,128]{1,0:T(8,128)(2,1)S(1)} %get-tuple-element.61.own_ref), channel_id=1, source_target_pairs={{0,1},{1,0},{2,3},{3,2},{4,5},{5,4},{6,7},{7,6},{8,9},{9,8},{10,11... | collective-permute-start | bytes 49160 | tf_op jit(solution)/shard_map/ppermute | solution.py:247
  3.4 6.9 %collective-permute-start.3 = (bf16[128,128]{1,0:T(8,128)(2,1)S(1)}, bf16[128,128]{1,0:T(8,128)(2,1)S(1)}, u32[]{:S(2)}, u32[]{:S(2)}) collective-permute-start(bf16[128,128]{1,0:T(8,128)(2,1)S(1)} %shard_map.131.refs_0_), channel_id=1, source_target_pairs={{0,6},{1,7},{2,4},{3,5},{4,2},{5,3},{6,0},{7,1},{8,14},{9,15},{10,... | collective-permute-start | bytes 98312 | tf_op jit(solution)/shard_map/ppermute | solution.py:247
  8.4 4.8 %collective-permute-start.2 = (bf16[128,128]{1,0:T(8,128)(2,1)S(1)}, bf16[128,128]{1,0:T(8,128)(2,1)S(1)}, u32[]{:S(2)}, u32[]{:S(2)}) collective-permute-start(bf16[128,128]{1,0:T(8,128)(2,1)S(1)} %shard_map.131.refs_0_), channel_id=1, source_target_pairs={{0,4},{1,5},{2,6},{3,7},{4,0},{5,1},{6,2},{7,3},{8,12},{9,13},{10,... | collective-permute-start | bytes 98312 | tf_op jit(solution)/shard_map/ppermute | solution.py:247
  8.4 4.8 %collective-permute-start.1 = (bf16[128,128]{1,0:T(8,128)(2,1)S(1)}, bf16[128,128]{1,0:T(8,128)(2,1)S(1)}, u32[]{:S(2)}, u32[]{:S(2)}) collective-permute-start(bf16[128,128]{1,0:T(8,128)(2,1)S(1)} %shard_map.131.refs_0_), channel_id=1, source_target_pairs={{0,2},{1,3},{2,0},{3,1},{4,6},{5,7},{6,4},{7,5},{8,10},{9,11},{10,... | collective-permute-start | bytes 98312 | tf_op jit(solution)/shard_map/ppermute | solution.py:247
  14.2 1.4 %collective-permute-start.5 = (bf16[512,128]{1,0:T(8,128)(2,1)S(1)}, bf16[512,128]{1,0:T(8,128)(2,1)S(1)}, u32[]{:S(2)}, u32[]{:S(2)}) collective-permute-start(bf16[512,128]{1,0:T(8,128)(2,1)S(1)} %get-tuple-element.66), channel_id=1, source_target_pairs={{0,1},{1,0},{2,3},{3,2},{4,5},{5,4},{6,7},{7,6},{8,9},{9,8},{10,11... | collective-permute-start | bytes 393224 | tf_op jit(solution)/shard_map/ppermute | solution.py:247
  14.3 1.5 %collective-permute-start.4 = (f32[256,128]{1,0:T(8,128)S(1)}, f32[256,128]{1,0:T(8,128)S(1)}, u32[]{:S(2)}, u32[]{:S(2)}) collective-permute-start(f32[256,128]{1,0:T(8,128)S(1)} %get-tuple-element.64.weights_ref), channel_id=1, source_target_pairs={{0,1},{1,0},{2,3},{3,2},{4,5},{5,4},{6,7},{7,6},{8,9},{9,8},{10,11... | collective-permute-start | bytes 393224 | tf_op jit(solution)/shard_map/ppermute | solution.py:247
  15.9 4.7 %collective-permute-start.6 = (bf16[384,128]{1,0:T(8,128)(2,1)S(1)}, bf16[384,128]{1,0:T(8,128)(2,1)S(1)}, u32[]{:S(2)}, u32[]{:S(2)}) collective-permute-start(bf16[384,128]{1,0:T(8,128)(2,1)S(1)} %get-tuple-element.69), channel_id=1, source_target_pairs={{0,8},{1,3},{2,10},{3,1},{4,12},{5,7},{6,14},{7,5},{8,0},{9,11},{1... | collective-permute-start | bytes 294920 | tf_op jit(solution)/shard_map/ppermute | solution.py:247
  17.4 4.6 %collective-permute-start.7 = (bf16[384,128]{1,0:T(8,128)(2,1)S(1)}, bf16[384,128]{1,0:T(8,128)(2,1)S(1)}, u32[]{:S(2)}, u32[]{:S(2)}) collective-permute-start(bf16[384,128]{1,0:T(8,128)(2,1)S(1)} %get-tuple-element.70), channel_id=1, source_target_pairs={{0,8},{1,5},{2,10},{3,7},{4,12},{5,1},{6,14},{7,3},{8,0},{9,13},{1... | collective-permute-start | bytes 294920 | tf_op jit(solution)/shard_map/ppermute | solution.py:247
  18.0 5.1 %collective-permute-start.8 = (bf16[384,128]{1,0:T(8,128)(2,1)S(1)}, bf16[384,128]{1,0:T(8,128)(2,1)S(1)}, u32[]{:S(2)}, u32[]{:S(2)}) collective-permute-start(bf16[384,128]{1,0:T(8,128)(2,1)S(1)} %get-tuple-element.71), channel_id=1, source_target_pairs={{0,8},{1,7},{2,10},{3,5},{4,12},{5,3},{6,14},{7,1},{8,0},{9,15},{1... | collective-permute-start | bytes 294920 | tf_op jit(solution)/shard_map/ppermute | solution.py:247
  23.2 4.3 %collective-permute-start.11 = (bf16[256,128]{1,0:T(8,128)(2,1)S(1)}, bf16[256,128]{1,0:T(8,128)(2,1)S(1)}, u32[]{:S(2)}, u32[]{:S(2)}) collective-permute-start(bf16[256,128]{1,0:T(8,128)(2,1)S(1)} %get-tuple-element.72.refs_0_), channel_id=1, source_target_pairs={{0,2},{1,25},{2,0},{3,27},{4,6},{5,29},{6,4},{7,31},{8,10},{9,17},... | collective-permute-start | bytes 196616 | tf_op jit(solution)/shard_map/ppermute | solution.py:247
  23.3 4.9 %collective-permute-start.10 = (bf16[256,128]{1,0:T(8,128)(2,1)S(1)}, bf16[256,128]{1,0:T(8,128)(2,1)S(1)}, u32[]{:S(2)}, u32[]{:S(2)}) collective-permute-start(bf16[256,128]{1,0:T(8,128)(2,1)S(1)} %get-tuple-element.72.refs_0_), channel_id=1, source_target_pairs={{0,2},{1,17},{2,0},{3,19},{4,6},{5,21},{6,4},{7,23},{8,10},{9,25},... | collective-permute-start | bytes 196616 | tf_op jit(solution)/shard_map/ppermute | solution.py:247
  25.3 4.3 %collective-permute-start.9 = (bf16[256,128]{1,0:T(8,128)(2,1)S(1)}, bf16[256,128]{1,0:T(8,128)(2,1)S(1)}, u32[]{:S(2)}, u32[]{:S(2)}) collective-permute-start(bf16[256,128]{1,0:T(8,128)(2,1)S(1)} %get-tuple-element.72.refs_0_), channel_id=1, source_target_pairs={{0,2},{1,9},{2,0},{3,11},{4,6},{5,13},{6,4},{7,15},{8,10},{9,1},{1... | collective-permute-start | bytes 196616 | tf_op jit(solution)/shard_map/ppermute | solution.py:247
  25.3 1.7 %collective-permute-start.12 = (f32[64,128]{1,0:T(8,128)S(1)}, f32[64,128]{1,0:T(8,128)S(1)}, u32[]{:S(2)}, u32[]{:S(2)}) collective-permute-start(f32[64,128]{1,0:T(8,128)S(1)} %get-tuple-element.73), channel_id=1, source_target_pairs={{0,1},{1,0},{2,3},{3,2},{4,5},{5,4},{6,7},{7,6},{8,9},{9,8},{10,11... | collective-permute-start | bytes 98312 | tf_op jit(solution)/shard_map/ppermute | solution.py:247
  29.6 1.4 %collective-permute-start.13 = (f32[256,128]{1,0:T(8,128)S(1)}, f32[256,128]{1,0:T(8,128)S(1)}, u32[]{:S(2)}, u32[]{:S(2)}) collective-permute-start(f32[256,128]{1,0:T(8,128)S(1)} %shard_map.137.mine_ref), channel_id=1, source_target_pairs={{0,1},{1,0},{2,3},{3,2},{4,5},{5,4},{6,7},{7,6},{8,9},{9,8},{10,11... | collective-permute-start | bytes 393224 | tf_op jit(solution)/shard_map/ppermute | solution.py:247

commit v3 on v2

--- a/solution.py
+++ b/solution.py
@@ -63,10 +63,8 @@
     return copies
 
 
-def publish_body(count, *refs):
-    sources, (out_ref, *targets), sems = refs[:count], refs[count:-1], refs[-1]
-    pub, rows, *rest = load(list(zip(sources, targets)), sems)
-    pub_ref, features_ref = targets[:2]
+def publish_body(pub_hbm, features_hbm, out_ref, pub_ref, features_ref, sems):
+    pub, rows = load([(pub_hbm, pub_ref), (features_hbm, features_ref)], sems)
     pub_count = pub_ref.shape[1]
     square = (pub_count, pub_count)
     pub.wait()
@@ -76,8 +74,6 @@
     pick = jnp.where(row == column.astype(jnp.int32), 1.0, 0.0).astype(BF)
     rows.wait()
     out_ref[...] = dot(pick, features_ref[...]).astype(BF)
-    for copy in rest:
-        copy.wait()
 
 
 def pair_body(own_ref, other_ref, out_ref):
@@ -92,13 +88,14 @@
     dom_size,
     pub_ref,
     features_ref,
-    local_ref,
-    bound_ref,
-    w_self_ref,
-    pos_ref,
-    count_ref,
-    mask_ref,
-    cot_ref,
+    pos_hbm,
+    count_hbm,
+    mask_hbm,
+    bound_hbm,
+    cot_hbm,
+    w_self_hbm,
+    w_neigh_hbm,
+    local_hbm,
     place_ref,
     adj_ref,
     flip_ref,
@@ -106,9 +103,33 @@
     inv_ref,
     self_ref,
     chosen_ref,
+    w_self_ref,
+    w_neigh_ref,
+    local_ref,
+    pos_ref,
+    count_ref,
+    mask_ref,
+    bound_ref,
+    cot_ref,
+    sems,
 ):
+    copies = load(
+        [
+            (pos_hbm, pos_ref),
+            (count_hbm, count_ref),
+            (mask_hbm, mask_ref),
+            (bound_hbm, bound_ref),
+            (w_self_hbm, w_self_ref),
+            (cot_hbm, cot_ref),
+            (local_hbm, local_ref),
+            (w_neigh_hbm, w_neigh_ref),
+        ],
+        sems,
+    )
     pub_count = pub_ref.shape[1]
     place_ref[...] = one_hot(features_ref.shape[0], pub_ref[...])
+    for copy in copies:
+        copy.wait()
     features = features_ref[...]
     self_ref[...] = dot(features, w_self_ref[...])
     me = lax.axis_index("dom")
@@ -249,52 +270,49 @@
     def over_core(x):
         return exchange(x, 1, 1)
 
-    fetched = (
+    published, pub_rows, features = pl.pallas_call(
+        publish_body,
+        out_shape=[
+            jax.ShapeDtypeStruct((pub_count, width), BF),
+            jax.ShapeDtypeStruct(pub_rows.shape, jnp.int32),
+            jax.ShapeDtypeStruct(wide, BF),
+        ],
+        in_specs=[HBM] * 2,
+        out_specs=[VMEM] * 3,
+        scratch_shapes=[pltpu.SemaphoreType.DMA((2,))],
+        compiler_params=PARAMS,
+    )(in_hbm(pub_rows), in_hbm(features))
+    (pair,) = call(pair_body, [((2 * pub_count, width), BF)], published, over_core(published))
+    pairs = [pair] + [exchange(pair, 2 * z, 2 * z) for z in range(1, z_size)]
+
+    columns = dom_size * pub_count
+    mask = target_mask.reshape(1, row_count)
+    place, adj_rows, adj_flip, part, inverse, own_part, chosen, w_self, w_neigh, adj_local = pl.pallas_call(
+        functools.partial(prepare_body, dom_size),
+        out_shape=[
+            jax.ShapeDtypeStruct(s, d)
+            for s, d in [
+                ((row_count, pub_count), BF),
+                ((row_count, columns), BF),
+                ((columns, row_count), BF),
+                (wide, F32),
+                (wide, F32),
+                (wide, F32),
+                (wide, BF),
+                (w_self.shape, BF),
+                (w_neigh.shape, BF),
+                (adj_local.shape, BF),
+            ]
+        ],
+        in_specs=[VMEM] * 2 + [HBM] * 8,
+        out_specs=[VMEM] * 10,
+        scratch_shapes=[pltpu.VMEM(x.shape, x.dtype) for x in (recv_pos, recv_count, mask, adj_bound, cotangent)]
+        + [pltpu.SemaphoreType.DMA((8,))],
+        compiler_params=PARAMS,
+    )(
         pub_rows,
         features,
-        adj_local,
-        adj_bound,
-        w_self,
-        w_neigh,
-        recv_pos,
-        recv_count,
-        target_mask.reshape(1, row_count),
-        cotangent,
-    )
-    published, *fetched = pl.pallas_call(
-        functools.partial(publish_body, len(fetched)),
-        out_shape=[jax.ShapeDtypeStruct((pub_count, width), BF)]
-        + [jax.ShapeDtypeStruct(x.shape, x.dtype) for x in fetched],
-        in_specs=[HBM] * len(fetched),
-        out_specs=[VMEM] * (1 + len(fetched)),
-        scratch_shapes=[pltpu.SemaphoreType.DMA((len(fetched),))],
-        compiler_params=PARAMS,
-    )(*(in_hbm(x) for x in fetched))
-    pub_rows, features, adj_local, adj_bound, w_self, w_neigh, recv_pos, recv_count, mask, cotangent = fetched
-    (pair,) = call(pair_body, [((2 * pub_count, width), BF)], published, over_core(published))
-    pairs = [pair] + [exchange(pair, 2 * z, 2 * z) for z in range(1, z_size)]
-
-    columns = dom_size * pub_count
-    place, adj_rows, adj_flip, part, inverse, own_part, chosen = call(
-        functools.partial(prepare_body, dom_size),
-        [
-            ((row_count, pub_count), BF),
-            ((row_count, columns), BF),
-            ((columns, row_count), BF),
-            (wide, F32),
-            (wide, F32),
-            (wide, F32),
-            (wide, BF),
-        ],
-        pub_rows,
-        features,
-        adj_local,
-        adj_bound,
-        w_self,
-        recv_pos,
-        recv_count,
-        mask,
-        cotangent,
+        *(in_hbm(x) for x in (recv_pos, recv_count, mask, adj_bound, cotangent, w_self, w_neigh, adj_local)),
     )
     square, both = (width, width), (2 * width, width)
     hidden, grad_pre, grad_agg, weights, grads, rounded = pl.pallas_call(

time: 31.8 us -> 31.5 us (level)
  waiting for transfers between devices: 12 us -> 10.6 us
  Pallas kernels: 5.49 us -> 6.49 us
    pallas_call x1 -> x2, Pallas kernels: 1.39 us -> 3.43 us  [the longest x1 2.33 us: local(): pl.pallas_call(functools.partial(prepare_body, dom_size), out_shape=[jax....]
    ppermute x14, waiting for transfers between devices: 12 us -> 10.6 us  [exchange(): lax.ppermute(x, ('group', 'dom'), [(a, a ^ (odd_step if a % 2 else even_s...]
    pallas_call x8 -> x7, Pallas kernels: 3.1 us -> 2.05 us  [call(): pl.pallas_call(body, out_shape=[jax.ShapeDtypeStruct(shape, dtype) for sh...]
  transfers between devices with their start and end apart: 14 -> 14, of which waited for: 13 -> 12; matrix products, arithmetic and copies ran while one was open for 0% -> 0% of each run, Pallas kernels for 7% -> 11%
where the time goes in v3:
time: 31.5 us; the launch traced here: 31.3 us
  starting transfers between devices  13.5 us (43%)
  waiting for transfers between devices  10.6 us (34%)
  Pallas kernels  6.49 us (21%)
  between operations  0.71 us (2%)
    ppermute x14, starting transfers between devices, exchange(): lax.ppermute(x, ('group', 'dom'), [(a, a ^ (odd_step if a % 2 else even_s...  13.5 us
    ppermute x14, waiting for transfers between devices, exchange(): lax.ppermute(x, ('group', 'dom'), [(a, a ^ (odd_step if a % 2 else even_s...  10.6 us
    pallas_call x1, Pallas kernels, local(): pl.pallas_call(functools.partial(prepare_body, dom_size), out_shape=[jax....  2.33 us
    pallas_call x7, Pallas kernels, call(): pl.pallas_call(body, out_shape=[jax.ShapeDtypeStruct(shape, dtype) for sh...  2.05 us
    pallas_call x1, Pallas kernels, local(): pl.pallas_call(publish_body, out_shape=[jax.ShapeDtypeStruct((pub_count,...  1.1 us
    pallas_call x1, Pallas kernels, local(): pl.pallas_call(functools.partial(layer_body, z_size), out_shape=[jax.Shap...  1.01 us
  transfers between devices with their start and end apart: 14, of which 12 were waited for; matrix products, arithmetic and copies ran while one was open for 0% of the time, Pallas kernels for 11%

profile of v3, /device:TPU:0, one launch (start us, length us, event | category | flops | bytes accessed | tf_op | source)
XLA Modules:
  0.0 31.3 jit_solution(9565688709472028198)
XLA Ops:
  0.6 1.1 %shard_map.129 = (bf16[64,128]{1,0:T(8,128)(2,1)S(1)}, s32[1,64]{1,0:T(1,128)S(1)}, bf16[512,128]{1,0:T(8,128)(2,1)S(1)}) custom-call(s32[1,64]{1,0:T(1,128)} %pub_hbm.1, bf16[512,128]{1,0:T(8,128)(2,1)} %features_hbm.1), custom_call_target="tpu_custom_call" | custom-call | tf_op jit(solution)/shard_map/pallas_call | solution.py:273
  1.7 0.5 %collective-permute-start = (bf16[64,128]{1,0:T(8,128)(2,1)S(1)}, bf16[64,128]{1,0:T(8,128)(2,1)S(1)}, u32[]{:S(2)}, u32[]{:S(2)}) collective-permute-start(bf16[64,128]{1,0:T(8,128)(2,1)S(1)} %get-tuple-element.49.own_ref), channel_id=1, source_target_pairs={{0,1},{1,0},{2,3},{3,2},{4,5},{5,4},{6,7},{7,6},{8,9},{9,8},{10,11... | collective-permute-start | bytes 49160 | tf_op jit(solution)/shard_map/ppermute | solution.py:268
  2.3 0.8 %collective-permute-done.other_ref = bf16[64,128]{1,0:T(8,128)(2,1)S(1)} collective-permute-done((bf16[64,128]{1,0:T(8,128)(2,1)S(1)}, bf16[64,128]{1,0:T(8,128)(2,1)S(1)}, u32[]{:S(2)}, u32[]{:S(2)}) %collective-permute-start) | collective-permute-done | bytes 16416 | tf_op jit(solution)/shard_map/ppermute | solution.py:268
  3.1 5.0 %collective-permute-start.3 = (bf16[128,128]{1,0:T(8,128)(2,1)S(1)}, bf16[128,128]{1,0:T(8,128)(2,1)S(1)}, u32[]{:S(2)}, u32[]{:S(2)}) collective-permute-start(bf16[128,128]{1,0:T(8,128)(2,1)S(1)} %shard_map.131.refs_0_), channel_id=1, source_target_pairs={{0,6},{1,7},{2,4},{3,5},{4,2},{5,3},{6,0},{7,1},{8,14},{9,15},{10,... | collective-permute-start | bytes 98312 | tf_op jit(solution)/shard_map/ppermute | solution.py:268
  8.1 0.0 collective-permute-start.2
  8.1 0.6 %collective-permute-start.1 = (bf16[128,128]{1,0:T(8,128)(2,1)S(1)}, bf16[128,128]{1,0:T(8,128)(2,1)S(1)}, u32[]{:S(2)}, u32[]{:S(2)}) collective-permute-start(bf16[128,128]{1,0:T(8,128)(2,1)S(1)} %shard_map.131.refs_0_), channel_id=1, source_target_pairs={{0,2},{1,3},{2,0},{3,1},{4,6},{5,7},{6,4},{7,5},{8,10},{9,11},{10,... | collective-permute-start | bytes 98312 | tf_op jit(solution)/shard_map/ppermute | solution.py:268
  8.8 2.3 %shard_map.130 = (bf16[512,64]{1,0:T(8,128)(2,1)S(1)}, bf16[512,512]{1,0:T(8,128)(2,1)S(1)}, bf16[512,512]{1,0:T(8,128)(2,1)S(1)}, f32[512,128]{1,0:T(8,128)S(1)...) custom-call(s32[1,64]{1,0:T(1,128)S(1)} %get-tuple-element.41.pub_re, ...), custom_call_target="tpu_custom_call" | custom-call | tf_op jit(solution)/shard_map/pallas_call | solution.py:290
  11.1 0.0 collective-permute-done.3.refs_3_
  11.1 1.8 %collective-permute-done.2.refs_2_ = bf16[128,128]{1,0:T(8,128)(2,1)S(1)} collective-permute-done((bf16[128,128]{1,0:T(8,128)(2,1)S(1)}, bf16[128,128]{1,0:T(8,128)(2,1)S(1)}, u32[]{:S(2)}, u32[]{:S(2)}) %collective-permute-start.2) | collective-permute-done | bytes 32800 | tf_op jit(solution)/shard_map/ppermute | solution.py:268
  12.9 0.0 collective-permute-done.1.refs_1_
  12.9 1.0 %shard_map.132 = (bf16[512,128]{1,0:T(8,128)(2,1)S(1)}, bf16[512,128]{1,0:T(8,128)(2,1)S(1)}, bf16[512,128]{1,0:T(8,128)(2,1)S(1)}, f32[256,128]{1,0:T(8,128)S(1...) custom-call(bf16[512,128]{1,0:T(8,128)(2,1)S(1)} %get-tuple-element.40.features_ref, ...), custom_call_target="tpu_custom_call" | custom-call | tf_op jit(solution)/shard_map/pallas_call | solution.py:318
  13.9 0.1 collective-permute-start.5
  14.0 0.5 %collective-permute-start.4 = (f32[256,128]{1,0:T(8,128)S(1)}, f32[256,128]{1,0:T(8,128)S(1)}, u32[]{:S(2)}, u32[]{:S(2)}) collective-permute-start(f32[256,128]{1,0:T(8,128)S(1)} %get-tuple-element.52.weights_ref), channel_id=1, source_target_pairs={{0,1},{1,0},{2,3},{3,2},{4,5},{5,4},{6,7},{7,6},{8,9},{9,8},{10,11... | collective-permute-start | bytes 393224 | tf_op jit(solution)/shard_map/ppermute | solution.py:268
  14.5 0.8 %collective-permute-done.5.got_g_ref = bf16[512,128]{1,0:T(8,128)(2,1)S(1)} collective-permute-done((bf16[512,128]{1,0:T(8,128)(2,1)S(1)}, bf16[512,128]{1,0:T(8,128)(2,1)S(1)}, u32[]{:S(2)}, u32[]{:S(2)}) %collective-permute-start.5) | collective-permute-done | bytes 131104 | tf_op jit(solution)/shard_map/ppermute | solution.py:268
  15.4 0.2 collective-permute-done.4.got_w_ref
  15.6 1.6 %collective-permute-start.6 = (bf16[384,128]{1,0:T(8,128)(2,1)S(1)}, bf16[384,128]{1,0:T(8,128)(2,1)S(1)}, u32[]{:S(2)}, u32[]{:S(2)}) collective-permute-start(bf16[384,128]{1,0:T(8,128)(2,1)S(1)} %get-tuple-element.57), channel_id=1, source_target_pairs={{0,8},{1,3},{2,10},{3,1},{4,12},{5,7},{6,14},{7,5},{8,0},{9,11},{1... | collective-permute-start | bytes 294920 | tf_op jit(solution)/shard_map/ppermute | solution.py:268
  17.1 0.5 %collective-permute-start.7 = (bf16[384,128]{1,0:T(8,128)(2,1)S(1)}, bf16[384,128]{1,0:T(8,128)(2,1)S(1)}, u32[]{:S(2)}, u32[]{:S(2)}) collective-permute-start(bf16[384,128]{1,0:T(8,128)(2,1)S(1)} %get-tuple-element.58), channel_id=1, source_target_pairs={{0,8},{1,5},{2,10},{3,7},{4,12},{5,1},{6,14},{7,3},{8,0},{9,13},{1... | collective-permute-start | bytes 294920 | tf_op jit(solution)/shard_map/ppermute | solution.py:268
  17.7 1.5 %collective-permute-start.8 = (bf16[384,128]{1,0:T(8,128)(2,1)S(1)}, bf16[384,128]{1,0:T(8,128)(2,1)S(1)}, u32[]{:S(2)}, u32[]{:S(2)}) collective-permute-start(bf16[384,128]{1,0:T(8,128)(2,1)S(1)} %get-tuple-element.59), channel_id=1, source_target_pairs={{0,8},{1,7},{2,10},{3,5},{4,12},{5,3},{6,14},{7,1},{8,0},{9,15},{1... | collective-permute-start | bytes 294920 | tf_op jit(solution)/shard_map/ppermute | solution.py:268
  19.2 1.1 %collective-permute-done.6.refs_0_ = bf16[384,128]{1,0:T(8,128)(2,1)S(1)} collective-permute-done((bf16[384,128]{1,0:T(8,128)(2,1)S(1)}, bf16[384,128]{1,0:T(8,128)(2,1)S(1)}, u32[]{:S(2)}, u32[]{:S(2)}) %collective-permute-start.6) | collective-permute-done | bytes 98336 | tf_op jit(solution)/shard_map/ppermute | solution.py:268
  20.3 1.5 %collective-permute-done.7.refs_1_ = bf16[384,128]{1,0:T(8,128)(2,1)S(1)} collective-permute-done((bf16[384,128]{1,0:T(8,128)(2,1)S(1)}, bf16[384,128]{1,0:T(8,128)(2,1)S(1)}, u32[]{:S(2)}, u32[]{:S(2)}) %collective-permute-start.7) | collective-permute-done | bytes 98336 | tf_op jit(solution)/shard_map/ppermute | solution.py:268
  21.8 1.1 %collective-permute-done.8.refs_2_ = bf16[384,128]{1,0:T(8,128)(2,1)S(1)} collective-permute-done((bf16[384,128]{1,0:T(8,128)(2,1)S(1)}, bf16[384,128]{1,0:T(8,128)(2,1)S(1)}, u32[]{:S(2)}, u32[]{:S(2)}) %collective-permute-start.8) | collective-permute-done | bytes 98336 | tf_op jit(solution)/shard_map/ppermute | solution.py:268
  22.8 0.1 shard_map.134
  22.9 0.1 collective-permute-start.11
  23.0 2.0 %collective-permute-start.10 = (bf16[256,128]{1,0:T(8,128)(2,1)S(1)}, bf16[256,128]{1,0:T(8,128)(2,1)S(1)}, u32[]{:S(2)}, u32[]{:S(2)}) collective-permute-start(bf16[256,128]{1,0:T(8,128)(2,1)S(1)} %get-tuple-element.60.refs_0_), channel_id=1, source_target_pairs={{0,2},{1,17},{2,0},{3,19},{4,6},{5,21},{6,4},{7,23},{8,10},{9,25},... | collective-permute-start | bytes 196616 | tf_op jit(solution)/shard_map/ppermute | solution.py:268
  25.0 0.1 collective-permute-start.9
  25.0 1.0 %collective-permute-start.12 = (f32[64,128]{1,0:T(8,128)S(1)}, f32[64,128]{1,0:T(8,128)S(1)}, u32[]{:S(2)}, u32[]{:S(2)}) collective-permute-start(f32[64,128]{1,0:T(8,128)S(1)} %get-tuple-element.61), channel_id=1, source_target_pairs={{0,1},{1,0},{2,3},{3,2},{4,5},{5,4},{6,7},{7,6},{8,9},{9,8},{10,11... | collective-permute-start | bytes 98312 | tf_op jit(solution)/shard_map/ppermute | solution.py:268
  26.0 0.4 %shard_map.135.local_grad_ref = f32[512,128]{1,0:T(8,128)S(1)} custom-call(bf16[512,512]{1,0:T(8,128)(2,1)S(1)} %get-tuple-element.62.local_ref, bf16[128,128]{1,0:T(8,128)(2,1)S(1)} %get-tuple-element.63.w_self_ref, bf16[512,128]{1,0:T(8,128)(2,1)S(1)} %get-tuple-element.64.pre_ref, bf16[512,128]{1,0:T(8,128)(2,1)S(1)} %get-tuple-element.65.agg_ref), custom_call_target="tpu_custom_call" | custom-call | tf_op jit(solution)/shard_map/pallas_call | solution.py:40
  26.4 0.5 %collective-permute-done.12.even_ref = f32[64,128]{1,0:T(8,128)S(1)} collective-permute-done((f32[64,128]{1,0:T(8,128)S(1)}, f32[64,128]{1,0:T(8,128)S(1)}, u32[]{:S(2)}, u32[]{:S(2)}) %collective-permute-start.12) | collective-permute-done | bytes 32800 | tf_op jit(solution)/shard_map/ppermute | solution.py:268
  26.9 0.3 %collective-permute-done.11.refs_3_ = bf16[256,128]{1,0:T(8,128)(2,1)S(1)} collective-permute-done((bf16[256,128]{1,0:T(8,128)(2,1)S(1)}, bf16[256,128]{1,0:T(8,128)(2,1)S(1)}, u32[]{:S(2)}, u32[]{:S(2)}) %collective-permute-start.11) | collective-permute-done | bytes 65568 | tf_op jit(solution)/shard_map/ppermute | solution.py:268
  27.2 0.7 %collective-permute-done.10.refs_2_ = bf16[256,128]{1,0:T(8,128)(2,1)S(1)} collective-permute-done((bf16[256,128]{1,0:T(8,128)(2,1)S(1)}, bf16[256,128]{1,0:T(8,128)(2,1)S(1)}, u32[]{:S(2)}, u32[]{:S(2)}) %collective-permute-start.10) | collective-permute-done | bytes 65568 | tf_op jit(solution)/shard_map/ppermute | solution.py:268
  27.9 1.3 %collective-permute-done.9.refs_1_ = bf16[256,128]{1,0:T(8,128)(2,1)S(1)} collective-permute-done((bf16[256,128]{1,0:T(8,128)(2,1)S(1)}, bf16[256,128]{1,0:T(8,128)(2,1)S(1)}, u32[]{:S(2)}, u32[]{:S(2)}) %collective-permute-start.9) | collective-permute-done | bytes 65568 | tf_op jit(solution)/shard_map/ppermute | solution.py:268
  29.3 0.1 collective-permute-start.13
  29.3 0.9 %shard_map.136 = (bf16[512,128]{1,0:T(8,128)(2,1)}, bf16[512,128]{1,0:T(8,128)(2,1)}) custom-call(bf16[512,128]{1,0:T(8,128)(2,1)S(1)} %get-tuple-element.50.hidden_ref, bf16[512,64]{1,0:T(8,128)(2,1)S(1)} %get-tuple-element.51.place_ref, f32[512,128]{1,0:T(8,128)S(1)} %shard_map.135.local_grad_ref, f32[64,128]{1,0:T(8,128)S(1)} %get-tuple-element.67.odd_ref, ...), custom_call_target="tpu_custom_call" | custom-call | tf_op jit(solution)/shard_map/pallas_call | solution.py:40
  30.2 0.5 %collective-permute-done.13.other_ref = f32[256,128]{1,0:T(8,128)S(1)} collective-permute-done((f32[256,128]{1,0:T(8,128)S(1)}, f32[256,128]{1,0:T(8,128)S(1)}, u32[]{:S(2)}, u32[]{:S(2)}) %collective-permute-start.13) | collective-permute-done | bytes 131104 | tf_op jit(solution)/shard_map/ppermute | solution.py:268
  30.7 0.7 %shard_map.138 = (f32[128,128]{1,0:T(8,128)}, f32[128,128]{1,0:T(8,128)}) custom-call(f32[256,128]{1,0:T(8,128)S(1)} %shard_map.137.mine_ref, f32[256,128]{1,0:T(8,128)S(1)} %collective-permute-done.13.other_ref), custom_call_target="tpu_custom_call" | custom-call | tf_op jit(solution)/shard_map/pallas_call | solution.py:40
  (3 shorter events, 0.1 us)
Async XLA Ops:
  1.7 1.4 %collective-permute-start = (bf16[64,128]{1,0:T(8,128)(2,1)S(1)}, bf16[64,128]{1,0:T(8,128)(2,1)S(1)}, u32[]{:S(2)}, u32[]{:S(2)}) collective-permute-start(bf16[64,128]{1,0:T(8,128)(2,1)S(1)} %get-tuple-element.49.own_ref), channel_id=1, source_target_pairs={{0,1},{1,0},{2,3},{3,2},{4,5},{5,4},{6,7},{7,6},{8,9},{9,8},{10,11... | collective-permute-start | bytes 49160 | tf_op jit(solution)/shard_map/ppermute | solution.py:268
  3.1 8.0 %collective-permute-start.3 = (bf16[128,128]{1,0:T(8,128)(2,1)S(1)}, bf16[128,128]{1,0:T(8,128)(2,1)S(1)}, u32[]{:S(2)}, u32[]{:S(2)}) collective-permute-start(bf16[128,128]{1,0:T(8,128)(2,1)S(1)} %shard_map.131.refs_0_), channel_id=1, source_target_pairs={{0,6},{1,7},{2,4},{3,5},{4,2},{5,3},{6,0},{7,1},{8,14},{9,15},{10,... | collective-permute-start | bytes 98312 | tf_op jit(solution)/shard_map/ppermute | solution.py:268
  8.1 4.8 %collective-permute-start.2 = (bf16[128,128]{1,0:T(8,128)(2,1)S(1)}, bf16[128,128]{1,0:T(8,128)(2,1)S(1)}, u32[]{:S(2)}, u32[]{:S(2)}) collective-permute-start(bf16[128,128]{1,0:T(8,128)(2,1)S(1)} %shard_map.131.refs_0_), channel_id=1, source_target_pairs={{0,4},{1,5},{2,6},{3,7},{4,0},{5,1},{6,2},{7,3},{8,12},{9,13},{10,... | collective-permute-start | bytes 98312 | tf_op jit(solution)/shard_map/ppermute | solution.py:268
  8.1 4.8 %collective-permute-start.1 = (bf16[128,128]{1,0:T(8,128)(2,1)S(1)}, bf16[128,128]{1,0:T(8,128)(2,1)S(1)}, u32[]{:S(2)}, u32[]{:S(2)}) collective-permute-start(bf16[128,128]{1,0:T(8,128)(2,1)S(1)} %shard_map.131.refs_0_), channel_id=1, source_target_pairs={{0,2},{1,3},{2,0},{3,1},{4,6},{5,7},{6,4},{7,5},{8,10},{9,11},{10,... | collective-permute-start | bytes 98312 | tf_op jit(solution)/shard_map/ppermute | solution.py:268
  13.9 1.4 %collective-permute-start.5 = (bf16[512,128]{1,0:T(8,128)(2,1)S(1)}, bf16[512,128]{1,0:T(8,128)(2,1)S(1)}, u32[]{:S(2)}, u32[]{:S(2)}) collective-permute-start(bf16[512,128]{1,0:T(8,128)(2,1)S(1)} %get-tuple-element.54), channel_id=1, source_target_pairs={{0,1},{1,0},{2,3},{3,2},{4,5},{5,4},{6,7},{7,6},{8,9},{9,8},{10,11... | collective-permute-start | bytes 393224 | tf_op jit(solution)/shard_map/ppermute | solution.py:268
  14.0 1.5 %collective-permute-start.4 = (f32[256,128]{1,0:T(8,128)S(1)}, f32[256,128]{1,0:T(8,128)S(1)}, u32[]{:S(2)}, u32[]{:S(2)}) collective-permute-start(f32[256,128]{1,0:T(8,128)S(1)} %get-tuple-element.52.weights_ref), channel_id=1, source_target_pairs={{0,1},{1,0},{2,3},{3,2},{4,5},{5,4},{6,7},{7,6},{8,9},{9,8},{10,11... | collective-permute-start | bytes 393224 | tf_op jit(solution)/shard_map/ppermute | solution.py:268
  15.6 4.7 %collective-permute-start.6 = (bf16[384,128]{1,0:T(8,128)(2,1)S(1)}, bf16[384,128]{1,0:T(8,128)(2,1)S(1)}, u32[]{:S(2)}, u32[]{:S(2)}) collective-permute-start(bf16[384,128]{1,0:T(8,128)(2,1)S(1)} %get-tuple-element.57), channel_id=1, source_target_pairs={{0,8},{1,3},{2,10},{3,1},{4,12},{5,7},{6,14},{7,5},{8,0},{9,11},{1... | collective-permute-start | bytes 294920 | tf_op jit(solution)/shard_map/ppermute | solution.py:268
  17.1 4.6 %collective-permute-start.7 = (bf16[384,128]{1,0:T(8,128)(2,1)S(1)}, bf16[384,128]{1,0:T(8,128)(2,1)S(1)}, u32[]{:S(2)}, u32[]{:S(2)}) collective-permute-start(bf16[384,128]{1,0:T(8,128)(2,1)S(1)} %get-tuple-element.58), channel_id=1, source_target_pairs={{0,8},{1,5},{2,10},{3,7},{4,12},{5,1},{6,14},{7,3},{8,0},{9,13},{1... | collective-permute-start | bytes 294920 | tf_op jit(solution)/shard_map/ppermute | solution.py:268
  17.7 5.1 %collective-permute-start.8 = (bf16[384,128]{1,0:T(8,128)(2,1)S(1)}, bf16[384,128]{1,0:T(8,128)(2,1)S(1)}, u32[]{:S(2)}, u32[]{:S(2)}) collective-permute-start(bf16[384,128]{1,0:T(8,128)(2,1)S(1)} %get-tuple-element.59), channel_id=1, source_target_pairs={{0,8},{1,7},{2,10},{3,5},{4,12},{5,3},{6,14},{7,1},{8,0},{9,15},{1... | collective-permute-start | bytes 294920 | tf_op jit(solution)/shard_map/ppermute | solution.py:268
  22.9 4.3 %collective-permute-start.11 = (bf16[256,128]{1,0:T(8,128)(2,1)S(1)}, bf16[256,128]{1,0:T(8,128)(2,1)S(1)}, u32[]{:S(2)}, u32[]{:S(2)}) collective-permute-start(bf16[256,128]{1,0:T(8,128)(2,1)S(1)} %get-tuple-element.60.refs_0_), channel_id=1, source_target_pairs={{0,2},{1,25},{2,0},{3,27},{4,6},{5,29},{6,4},{7,31},{8,10},{9,17},... | collective-permute-start | bytes 196616 | tf_op jit(solution)/shard_map/ppermute | solution.py:268
  23.0 4.9 %collective-permute-start.10 = (bf16[256,128]{1,0:T(8,128)(2,1)S(1)}, bf16[256,128]{1,0:T(8,128)(2,1)S(1)}, u32[]{:S(2)}, u32[]{:S(2)}) collective-permute-start(bf16[256,128]{1,0:T(8,128)(2,1)S(1)} %get-tuple-element.60.refs_0_), channel_id=1, source_target_pairs={{0,2},{1,17},{2,0},{3,19},{4,6},{5,21},{6,4},{7,23},{8,10},{9,25},... | collective-permute-start | bytes 196616 | tf_op jit(solution)/shard_map/ppermute | solution.py:268
  25.0 4.3 %collective-permute-start.9 = (bf16[256,128]{1,0:T(8,128)(2,1)S(1)}, bf16[256,128]{1,0:T(8,128)(2,1)S(1)}, u32[]{:S(2)}, u32[]{:S(2)}) collective-permute-start(bf16[256,128]{1,0:T(8,128)(2,1)S(1)} %get-tuple-element.60.refs_0_), channel_id=1, source_target_pairs={{0,2},{1,9},{2,0},{3,11},{4,6},{5,13},{6,4},{7,15},{8,10},{9,1},{1... | collective-permute-start | bytes 196616 | tf_op jit(solution)/shard_map/ppermute | solution.py:268
  25.0 1.8 %collective-permute-start.12 = (f32[64,128]{1,0:T(8,128)S(1)}, f32[64,128]{1,0:T(8,128)S(1)}, u32[]{:S(2)}, u32[]{:S(2)}) collective-permute-start(f32[64,128]{1,0:T(8,128)S(1)} %get-tuple-element.61), channel_id=1, source_target_pairs={{0,1},{1,0},{2,3},{3,2},{4,5},{5,4},{6,7},{7,6},{8,9},{9,8},{10,11... | collective-permute-start | bytes 98312 | tf_op jit(solution)/shard_map/ppermute | solution.py:268
  29.3 1.4 %collective-permute-start.13 = (f32[256,128]{1,0:T(8,128)S(1)}, f32[256,128]{1,0:T(8,128)S(1)}, u32[]{:S(2)}, u32[]{:S(2)}) collective-permute-start(f32[256,128]{1,0:T(8,128)S(1)} %shard_map.137.mine_ref), channel_id=1, source_target_pairs={{0,1},{1,0},{2,3},{3,2},{4,5},{5,4},{6,7},{7,6},{8,9},{9,8},{10,11... | collective-permute-start | bytes 393224 | tf_op jit(solution)/shard_map/ppermute | solution.py:268

commit v4 on v2

v4 whole, which is shorter than its diff:
```python
import functools
import math

import jax
import jax.numpy as jnp
from jax import lax
from jax.experimental import pallas as pl
from jax.experimental.pallas import tpu as pltpu
from jax.sharding import PartitionSpec as P

BF = jnp.bfloat16
F32 = jnp.float32
BLOCK, HITS = 128, 16
VMEM = pl.BlockSpec(memory_space=pltpu.VMEM)
HBM = pl.BlockSpec(memory_space=pltpu.HBM)
PARAMS = pltpu.CompilerParams(vmem_limit_bytes=48 * 1024 * 1024)


def dot(a, b):
    return jnp.dot(a, b, preferred_element_type=F32)


def dot_t(a, b):
    return lax.dot_general(a, b, (((0,), (0,)), ((), ())), preferred_element_type=F32)


def dot_nt(a, b):
    return lax.dot_general(a, b, (((1,), (1,)), ((), ())), preferred_element_type=F32)


def one_hot(rows, targets):
    row = lax.broadcasted_iota(jnp.int32, (rows, targets.shape[1]), 0)
    return jnp.where(row == targets, 1.0, 0.0).astype(BF)


def in_hbm(x):
    return pltpu.with_memory_space_constraint(x, pltpu.HBM)


def call(body, outs, *args):
    return pl.pallas_call(
        body,
        out_shape=[jax.ShapeDtypeStruct(shape, dtype) for shape, dtype in outs],
        in_specs=[VMEM] * len(args),
        out_specs=[VMEM] * len(outs),
        compiler_params=PARAMS,
    )(*args)


def odd_core():
    return lax.axis_index("dom") % 2 == 1


def tree_sum(parts):
    while len(parts) > 1:
        parts = [a + b for a, b in zip(parts[::2], parts[1::2])]
    return parts[0]


def load(pairs, sems):
    copies = [pltpu.make_async_copy(a, b, sems.at[i]) for i, (a, b) in enumerate(pairs)]
    for copy in copies:
        copy.start()
    return copies


def publish_body(count, *refs):
    sources, (out_ref, *targets), sems = refs[:count], refs[count:-1], refs[-1]
    pub, rows, *rest = load(list(zip(sources, targets)), sems)
    pub_ref, features_ref = targets[:2]
    pub_count = pub_ref.shape[1]
    square = (pub_count, pub_count)
    pub.wait()
    diagonal = lax.broadcasted_iota(jnp.int32, square, 0) == lax.broadcasted_iota(jnp.int32, square, 1)
    column = jnp.sum(jnp.where(diagonal, pub_ref[...].astype(F32), 0.0), axis=1, keepdims=True)
    row = lax.broadcasted_iota(jnp.int32, (pub_count, features_ref.shape[0]), 1)
    pick = jnp.where(row == column.astype(jnp.int32), 1.0, 0.0).astype(BF)
    rows.wait()
    out_ref[...] = dot(pick, features_ref[...]).astype(BF)
    for copy in rest:
        copy.wait()


def pair_body(own_ref, other_ref, out_ref):
    rows = own_ref.shape[0]
    odd = odd_core()
    own, other = own_ref[...], other_ref[...]
    out_ref[:rows, :] = jnp.where(odd, other, own)
    out_ref[rows:, :] = jnp.where(odd, own, other)


def move_columns(bound, target, chunk, c):
    return dot_nt(bound, one_hot(chunk, target - c * chunk)).astype(BF)


def prepare_body(
    dom_size,
    pub_ref,
    features_ref,
    mask_ref,
    pos_ref,
    count_ref,
    bound_ref,
    cot_ref,
    local_ref,
    place_ref,
    target_ref,
    pick_ref,
    near_ref,
    pack_ref,
):
    pub_count = pub_ref.shape[1]
    row_count, width = features_ref.shape
    place_ref[...] = one_hot(row_count, pub_ref[...])
    me = lax.axis_index("dom")
    chip = me - me % 2
    slots = pos_ref.shape[1]
    slot_rows = slots // dom_size
    lane = lax.broadcasted_iota(jnp.int32, (1, slots), 1)
    peer = lane // slot_rows
    limit = jnp.zeros((1, slots), jnp.int32)
    for j in range(dom_size):
        limit = jnp.where(peer == j, count_ref[0:1, j : j + 1], limit)
    in_use = lane % slot_rows < limit
    target = jnp.where(in_use, (peer ^ chip) * pub_count + pos_ref[...], -1)
    target_ref[...] = target
    blocks = row_count // BLOCK
    mask = jnp.concatenate(
        [
            jnp.broadcast_to(mask_ref[0:1, b * BLOCK : (b + 1) * BLOCK].astype(F32), (HITS, BLOCK))
            for b in range(blocks)
        ],
        axis=0,
    )
    before = lax.broadcasted_iota(jnp.int32, (BLOCK, BLOCK), 0) < lax.broadcasted_iota(jnp.int32, (BLOCK, BLOCK), 1)
    rank = dot(mask.astype(BF), jnp.where(before, 1.0, 0.0).astype(BF))
    row = lax.broadcasted_iota(jnp.int32, mask.shape, 0)
    hit = jnp.where(rank == (row % HITS).astype(F32), mask, 0.0)
    pick = jnp.concatenate([jnp.where(row // HITS == b, hit, 0.0) for b in range(blocks)], axis=1).astype(BF)
    pick_ref[...] = pick
    columns = dom_size * pub_count
    features = features_ref[...]
    near = dot(pick, local_ref[...]).astype(BF)
    near_ref[...] = near
    bound = dot(pick, bound_ref[...]).astype(BF)
    pack_ref[:, columns : columns + width] = dot(pick, features)
    pack_ref[:, columns + width : columns + 2 * width] = dot(pick, cot_ref[...])
    pack_ref[:, columns + 2 * width : columns + 3 * width] = dot(near, features)
    chunk = math.gcd(columns, 512)
    ones = jnp.ones((max(chunk, row_count), width), BF)

    def move(c, total):
        block = move_columns(bound, target, chunk, c)
        pack_ref[:, pl.ds(pl.multiple_of(c * chunk, chunk), chunk)] = block.astype(F32)
        return total + dot(block, ones[:chunk])

    sums = lax.fori_loop(0, columns // chunk, move, dot(near, ones[:row_count]))
    pack_ref[:, columns + 3 * width :] = 1.0 / (1.0 + sums)


def rows_body(*refs):
    pairs, out_ref = refs[:-1], refs[-1]
    count = pairs[0].shape[0]
    for z, pair in enumerate(pairs):
        out_ref[z * count : (z + 1) * count, :] = pair[...]


def target_body(
    w_self_ref,
    w_neigh_ref,
    pack_ref,
    got_pack_ref,
    rows_ref,
    pre_ref,
    agg_ref,
    own_ref,
    total_ref,
    *messages,
):
    count = rows_ref.shape[0] // (1 + len(messages))
    odd = odd_core()
    columns, width = rows_ref.shape
    own, other = pack_ref[...], got_pack_ref[...]
    pack = jnp.concatenate([jnp.where(odd, other, own), jnp.where(odd, own, other)], axis=0)
    adj = pack[:, :columns].astype(BF)
    features, cot, part, inv = (pack[:, columns + i * width : columns + (i + 1) * width] for i in range(4))
    features = features.astype(BF)
    aggregate = ((part + dot(adj, rows_ref[...])) * inv).astype(BF)
    preact = dot(features, w_self_ref[...]) + dot(aggregate, w_neigh_ref[...])
    sigma = jax.nn.sigmoid(preact)
    slope = sigma * (1.0 + preact * (1.0 - sigma))
    grad_pre = (cot * slope).astype(BF)
    grad_agg = (dot_nt(grad_pre, w_neigh_ref[...]) * inv).astype(BF)
    pre_ref[...] = grad_pre
    agg_ref[...] = grad_agg
    total = jnp.concatenate([dot_t(features, grad_pre), dot_t(aggregate, grad_pre)], axis=0).astype(BF)
    total_ref[...] = total
    grads = dot_t(adj, grad_agg)
    own_ref[...] = grads[:count]
    for z, message in zip(range(len(messages), 0, -1), messages):
        message[:count, :] = grads[z * count : (z + 1) * count].astype(BF)
        message[count:, :] = total


def rest_body(
    features_ref,
    local_ref,
    bound_ref,
    target_ref,
    w_self_ref,
    w_neigh_ref,
    rows_ref,
    pick_ref,
    near_ref,
    pre_ref,
    agg_ref,
    hidden_ref,
    out_ref,
):
    columns, width = rows_ref.shape
    features, near = features_ref[...], local_ref[...]
    chunk = math.gcd(columns, 512)
    ones = jnp.ones((max(chunk, near.shape[1]), width), BF)

    def move(c, totals):
        block = move_columns(bound_ref[...], target_ref[...], chunk, c)
        rows = rows_ref[pl.ds(pl.multiple_of(c * chunk, chunk), chunk), :]
        return totals[0] + dot(block, rows), totals[1] + dot(block, ones[:chunk])

    start = (dot(near, features), dot(near, ones[: near.shape[1]]))
    total, sums = lax.fori_loop(0, columns // chunk, move, start)
    aggregate = (total * (1.0 / (1.0 + sums))).astype(BF)
    preact = dot(features, w_self_ref[...]) + dot(aggregate, w_neigh_ref[...])
    hidden_ref[...] = (preact * jax.nn.sigmoid(preact)).astype(BF)
    odd = odd_core()
    half = pre_ref.shape[0] // 2
    grad_pre, grad_agg = pre_ref[...], agg_ref[...]
    grad_pre = jnp.where(odd, grad_pre[half:], grad_pre[:half])
    grad_agg = jnp.where(odd, grad_agg[half:], grad_agg[:half])
    spread = dot_t(pick_ref[...], grad_pre).astype(BF)
    out_ref[...] = dot_nt(spread, w_self_ref[...]) + dot_t(near_ref[...], grad_agg)


def column_body(scale, total_ref, own_ref, *refs):
    messages, (out_ref, even_ref, odd_ref) = refs[:-3], refs[-3:]
    rows = own_ref.shape[0]
    parts = [total_ref[...]] + [message[rows:, :] for message in messages]
    out_ref[...] = (tree_sum([part.astype(F32) for part in parts]) * scale).astype(BF)
    grads = own_ref[...]
    for message in messages:
        grads = grads + message[:rows, :].astype(F32)
    even_ref[...] = grads[: rows // 2]
    odd_ref[...] = grads[rows // 2 :]


def features_body(hidden_ref, place_ref, local_grad_ref, odd_ref, even_ref, hidden_out, out_ref):
    hidden_out[...] = hidden_ref[...]
    total = jnp.where(odd_core(), odd_ref[...], even_ref[...])
    place = place_ref[...]
    high = total.astype(BF)
    low = (total - high.astype(F32)).astype(BF)
    out_ref[...] = (local_grad_ref[...] + dot(place, high) + dot(place, low)).astype(BF)


def sum_body(*refs):
    refs[-1][...] = tree_sum([part[...].astype(F32) for part in refs[:-1]])


def order_body(mine_ref, other_ref, self_ref, neigh_ref):
    total = jnp.where(odd_core(), mine_ref[...], other_ref[...])
    width = self_ref.shape[0]
    self_ref[...] = total[:width]
    neigh_ref[...] = total[width:]


def local(
    features,
    adj_local,
    adj_bound,
    w_self,
    w_neigh,
    pub_rows,
    recv_pos,
    recv_count,
    target_mask,
    cotangent,
):
    dom_size, group_size = lax.axis_size("dom"), lax.axis_size("group")
    z_size = dom_size // 2
    row_count, width = features.shape
    pub_count = pub_rows.shape[1]
    wide = (row_count, width)
    devices = range(group_size * dom_size)

    def exchange(x, odd_step, even_step):
        return lax.ppermute(x, ("group", "dom"), [(a, a ^ (odd_step if a % 2 else even_step)) for a in devices])

    def over_core(x):
        return exchange(x, 1, 1)

    first = (
        pub_rows,
        features,
        target_mask.reshape(1, row_count),
        recv_pos,
        recv_count,
        adj_bound,
        cotangent,
        adj_local,
        w_self,
        w_neigh,
    )
    published, *first = pl.pallas_call(
        functools.partial(publish_body, len(first)),
        out_shape=[jax.ShapeDtypeStruct((pub_count, width), BF)]
        + [jax.ShapeDtypeStruct(x.shape, x.dtype) for x in first],
        in_specs=[HBM] * len(first),
        out_specs=[VMEM] * (1 + len(first)),
        scratch_shapes=[pltpu.SemaphoreType.DMA((len(first),))],
        compiler_params=PARAMS,
    )(*(in_hbm(x) for x in first))
    _, features, _, _, _, adj_bound, _, adj_local, w_self, w_neigh = first
    other = over_core(published)
    columns = dom_size * pub_count
    hits = row_count // BLOCK * HITS
    place, target, pick, near, pack = call(
        functools.partial(prepare_body, dom_size),
        [
            ((row_count, pub_count), BF),
            (recv_pos.shape, jnp.int32),
            ((hits, row_count), BF),
            ((hits, row_count), BF),
            ((hits, columns + 4 * width), F32),
        ],
        *first[:8],
    )
    other, pack = lax.optimization_barrier((other, pack))
    (pair,) = call(pair_body, [((2 * pub_count, width), BF)], published, other)
    pairs = [pair] + [exchange(pair, 2 * z, 2 * z) for z in range(1, z_size)]

    square, both = (width, width), (2 * width, width)
    message = ((2 * pub_count + 2 * width, width), BF)
    (rows,) = call(rows_body, [((columns, width), BF)], *pairs)
    grad_pre, grad_agg, own_g, chip_w, *messages = call(
        target_body,
        [((2 * hits, width), BF)] * 2 + [((2 * pub_count, width), F32), (both, BF)] + [message] * (z_size - 1),
        w_self,
        w_neigh,
        pack,
        over_core(pack),
        rows,
    )
    hidden, local_grad = call(
        rest_body,
        [(wide, BF), (wide, F32)],
        features,
        adj_local,
        adj_bound,
        target,
        w_self,
        w_neigh,
        rows,
        pick,
        near,
        grad_pre,
        grad_agg,
    )
    far = range(z_size - 1, 0, -1)
    arrived = [exchange(x, 2 * z, dom_size) for z, x in zip(far, messages)][::-1]
    *arrived, hidden, local_grad = lax.optimization_barrier((*arrived, hidden, local_grad))
    scale = 1.0 / math.sqrt(row_count * group_size * dom_size // 8)
    column_w, even_g, odd_g = call(
        functools.partial(column_body, scale),
        [(both, BF)] + [((pub_count, width), F32)] * 2,
        chip_w,
        own_g,
        *arrived,
    )
    others = [exchange(column_w, dom_size * k, 2) for k in range(1, group_size)]
    *others, even_g = lax.optimization_barrier((*others, over_core(even_g)))
    hidden, grad_features = call(features_body, [(wide, BF)] * 2, hidden, place, local_grad, odd_g, even_g)
    (mine,) = call(sum_body, [(both, F32)], column_w, *others)
    grad_self, grad_neigh = call(order_body, [(square, F32)] * 2, mine, over_core(mine))
    return hidden, grad_features, grad_self, grad_neigh


def solution(mesh):
    rows = P(("group", "dom"), None)
    in_specs = (rows, rows, rows, P(), P(), rows, rows, rows, P(("group", "dom")), rows)
    return jax.shard_map(
        local, mesh=mesh, in_specs=in_specs, out_specs=(rows, rows, P(), P()), check_vma=False
    )
```

time: 31.8 us -> 30 us (0.943)
  starting transfers between devices: 13.4 us -> 12.3 us
  waiting for transfers between devices: 12 us -> 11.3 us
    ppermute x14 -> x13, starting transfers between devices: 13.4 us -> 12.3 us  [exchange(): lax.ppermute(x, ('group', 'dom'), [(a, a ^ (odd_step if a % 2 else even_s...]
    pallas_call x8 -> x9, Pallas kernels: 3.1 us -> 4.1 us  [call(): pl.pallas_call(body, out_shape=[jax.ShapeDtypeStruct(shape, dtype) for sh...]
    pallas_call x2 -> x1, Pallas kernels: 2.39 us -> 1.42 us  [local(): pl.pallas_call(functools.partial(publish_body, len(first)), out_shape=[ja...]
    ppermute x14 -> x13, waiting for transfers between devices: 12 us -> 11.3 us  [exchange(): lax.ppermute(x, ('group', 'dom'), [(a, a ^ (odd_step if a % 2 else even_s...]
  transfers between devices with their start and end apart: 14 -> 13, of which waited for: 13 -> 10; matrix products, arithmetic and copies ran while one was open for 0% -> 0% of each run, Pallas kernels for 7% -> 9%
where the time goes in v4:
time: 30 us; the launch traced here: 29.8 us
  starting transfers between devices  12.3 us (41%)
  waiting for transfers between devices  11.3 us (38%)
  Pallas kernels  5.52 us (18%)
  between operations  0.71 us (2%)
    ppermute x13, starting transfers between devices, exchange(): lax.ppermute(x, ('group', 'dom'), [(a, a ^ (odd_step if a % 2 else even_s...  12.3 us
    ppermute x13, waiting for transfers between devices, exchange(): lax.ppermute(x, ('group', 'dom'), [(a, a ^ (odd_step if a % 2 else even_s...  11.3 us
    pallas_call x9, Pallas kernels, call(): pl.pallas_call(body, out_shape=[jax.ShapeDtypeStruct(shape, dtype) for sh...  4.1 us
    pallas_call x1, Pallas kernels, local(): pl.pallas_call(functools.partial(publish_body, len(first)), out_shape=[ja...  1.42 us
  transfers between devices with their start and end apart: 13, of which 10 were waited for; matrix products, arithmetic and copies ran while one was open for 0% of the time, Pallas kernels for 9%

profile of v4, /device:TPU:0, one launch (start us, length us, event | category | flops | bytes accessed | tf_op | source)
XLA Modules:
  0.0 29.8 jit_solution(4376482168499897475)
XLA Ops:
  0.6 1.4 %shard_map.129 = (bf16[64,128]{1,0:T(8,128)(2,1)S(1)}, s32[1,64]{1,0:T(1,128)S(1)}, bf16[512,128]{1,0:T(8,128)(2,1)S(1)}, s32[1,512]{1,0:T(1,128)S(1)}, s32[1,25...) custom-call(s32[1,64]{1,0:T(1,128)} %refs_0_.1, ...), custom_call_target="tpu_custom_call" | custom-call | tf_op jit(solution)/shard_map/pallas_call | solution.py:313
  2.1 0.5 %collective-permute-start = (bf16[64,128]{1,0:T(8,128)(2,1)S(1)}, bf16[64,128]{1,0:T(8,128)(2,1)S(1)}, u32[]{:S(2)}, u32[]{:S(2)}) collective-permute-start(bf16[64,128]{1,0:T(8,128)(2,1)S(1)} %get-tuple-element.49.own_ref), channel_id=1, source_target_pairs={{0,1},{1,0},{2,3},{3,2},{4,5},{5,4},{6,7},{7,6},{8,9},{9,8},{10,11... | collective-permute-start | bytes 49160 | tf_op jit(solution)/shard_map/ppermute | solution.py:296
  2.6 0.7 %shard_map.130 = (bf16[512,64]{1,0:T(8,128)(2,1)S(1)}, s32[1,256]{1,0:T(1,128)S(1)}, bf16[64,512]{1,0:T(8,128)(2,1)S(1)}, bf16[64,512]{1,0:T(8,128)(2,1)S(1)}, f32[64,1024]{1,0:T(8,128)S(1)}) custom-call(s32[1,64]{1,0:T(1,128)S(1)} %get-tuple-element.50.pub_ref, bf16[512,128]{1,0:T(8,128)(2,1)S(1)} %get-tuple-element.51.features_ref, ...), custom_call_target="tpu_custom_call" | custom-call | tf_op jit(solution)/shard_map/pallas_call | solution.py:41
  3.3 0.1 collective-permute-done.other_ref
  3.4 0.3 %collective-permute-start.1 = (f32[64,1024]{1,0:T(8,128)S(1)}, f32[64,1024]{1,0:T(8,128)S(1)}, u32[]{:S(2)}, u32[]{:S(2)}) collective-permute-start(f32[64,1024]{1,0:T(8,128)S(1)} %get-tuple-element.59.pack_ref), channel_id=1, source_target_pairs={{0,1},{1,0},{2,3},{3,2},{4,5},{5,4},{6,7},{7,6},{8,9},{9,8},{10,11... | collective-permute-start | bytes 786440 | tf_op jit(solution)/shard_map/ppermute | solution.py:296
  3.8 4.8 %collective-permute-start.4 = (bf16[128,128]{1,0:T(8,128)(2,1)S(1)}, bf16[128,128]{1,0:T(8,128)(2,1)S(1)}, u32[]{:S(2)}, u32[]{:S(2)}) collective-permute-start(bf16[128,128]{1,0:T(8,128)(2,1)S(1)} %shard_map.131.refs_0_), channel_id=1, source_target_pairs={{0,6},{1,7},{2,4},{3,5},{4,2},{5,3},{6,0},{7,1},{8,14},{9,15},{10,... | collective-permute-start | bytes 98312 | tf_op jit(solution)/shard_map/ppermute | solution.py:296
  8.6 0.0 collective-permute-start.3
  8.6 0.6 %collective-permute-start.2 = (bf16[128,128]{1,0:T(8,128)(2,1)S(1)}, bf16[128,128]{1,0:T(8,128)(2,1)S(1)}, u32[]{:S(2)}, u32[]{:S(2)}) collective-permute-start(bf16[128,128]{1,0:T(8,128)(2,1)S(1)} %shard_map.131.refs_0_), channel_id=1, source_target_pairs={{0,2},{1,3},{2,0},{3,1},{4,6},{5,7},{6,4},{7,5},{8,10},{9,11},{10,... | collective-permute-start | bytes 98312 | tf_op jit(solution)/shard_map/ppermute | solution.py:296
  9.2 1.4 %collective-permute-done.4.refs_3_ = bf16[128,128]{1,0:T(8,128)(2,1)S(1)} collective-permute-done((bf16[128,128]{1,0:T(8,128)(2,1)S(1)}, bf16[128,128]{1,0:T(8,128)(2,1)S(1)}, u32[]{:S(2)}, u32[]{:S(2)}) %collective-permute-start.4) | collective-permute-done | bytes 32800 | tf_op jit(solution)/shard_map/ppermute | solution.py:296
  10.6 2.8 %collective-permute-done.3.refs_2_ = bf16[128,128]{1,0:T(8,128)(2,1)S(1)} collective-permute-done((bf16[128,128]{1,0:T(8,128)(2,1)S(1)}, bf16[128,128]{1,0:T(8,128)(2,1)S(1)}, u32[]{:S(2)}, u32[]{:S(2)}) %collective-permute-start.3) | collective-permute-done | bytes 32800 | tf_op jit(solution)/shard_map/ppermute | solution.py:296
  13.4 0.0 collective-permute-done.2.refs_1_
  13.4 0.0 collective-permute-done.1.got_pack_ref
  13.4 0.6 %shard_map.133 = (bf16[128,128]{1,0:T(8,128)(2,1)S(1)}, bf16[128,128]{1,0:T(8,128)(2,1)S(1)}, f32[128,128]{1,0:T(8,128)S(1)}, bf16[256,128]{1,0:T(8,128)(2,1)S(1...) custom-call(bf16[128,128]{1,0:T(8,128)(2,1)S(1)} %get-tuple-element.47.w_self_ref, ...), custom_call_target="tpu_custom_call" | custom-call | tf_op jit(solution)/shard_map/pallas_call | solution.py:41
  14.1 1.6 %collective-permute-start.5 = (bf16[384,128]{1,0:T(8,128)(2,1)S(1)}, bf16[384,128]{1,0:T(8,128)(2,1)S(1)}, u32[]{:S(2)}, u32[]{:S(2)}) collective-permute-start(bf16[384,128]{1,0:T(8,128)(2,1)S(1)} %get-tuple-element.61), channel_id=1, source_target_pairs={{0,8},{1,3},{2,10},{3,1},{4,12},{5,7},{6,14},{7,5},{8,0},{9,11},{1... | collective-permute-start | bytes 294920 | tf_op jit(solution)/shard_map/ppermute | solution.py:296
  15.6 0.5 %collective-permute-start.6 = (bf16[384,128]{1,0:T(8,128)(2,1)S(1)}, bf16[384,128]{1,0:T(8,128)(2,1)S(1)}, u32[]{:S(2)}, u32[]{:S(2)}) collective-permute-start(bf16[384,128]{1,0:T(8,128)(2,1)S(1)} %get-tuple-element.62), channel_id=1, source_target_pairs={{0,8},{1,5},{2,10},{3,7},{4,12},{5,1},{6,14},{7,3},{8,0},{9,13},{1... | collective-permute-start | bytes 294920 | tf_op jit(solution)/shard_map/ppermute | solution.py:296
  16.2 1.5 %collective-permute-start.7 = (bf16[384,128]{1,0:T(8,128)(2,1)S(1)}, bf16[384,128]{1,0:T(8,128)(2,1)S(1)}, u32[]{:S(2)}, u32[]{:S(2)}) collective-permute-start(bf16[384,128]{1,0:T(8,128)(2,1)S(1)} %get-tuple-element.63), channel_id=1, source_target_pairs={{0,8},{1,7},{2,10},{3,5},{4,12},{5,3},{6,14},{7,1},{8,0},{9,15},{1... | collective-permute-start | bytes 294920 | tf_op jit(solution)/shard_map/ppermute | solution.py:296
  17.6 1.1 %shard_map.134 = (bf16[512,128]{1,0:T(8,128)(2,1)S(1)}, f32[512,128]{1,0:T(8,128)S(1)}) custom-call(bf16[512,128]{1,0:T(8,128)(2,1)S(1)} %get-tuple-element.51.features_ref, bf16[512,512]{1,0:T(8,128)(2,1)S(1)} %get-tuple-element.57.local_ref, bf16[512,256]{1,0:T(8,128)(2,1)S(1)} %get-tuple-element.55.bound_ref, s32[1,256]{1,0:T(1,128)S(1)} %get-tuple-element.64.target_ref, ...), custom_call_target="tpu_custom_call" | custom-call | tf_op jit(solution)/shard_map/pallas_call | solution.py:41
  18.8 0.0 collective-permute-done.5.refs_0_
  18.8 1.4 %collective-permute-done.6.refs_1_ = bf16[384,128]{1,0:T(8,128)(2,1)S(1)} collective-permute-done((bf16[384,128]{1,0:T(8,128)(2,1)S(1)}, bf16[384,128]{1,0:T(8,128)(2,1)S(1)}, u32[]{:S(2)}, u32[]{:S(2)}) %collective-permute-start.6) | collective-permute-done | bytes 98336 | tf_op jit(solution)/shard_map/ppermute | solution.py:296
  20.2 1.1 %collective-permute-done.7.refs_2_ = bf16[384,128]{1,0:T(8,128)(2,1)S(1)} collective-permute-done((bf16[384,128]{1,0:T(8,128)(2,1)S(1)}, bf16[384,128]{1,0:T(8,128)(2,1)S(1)}, u32[]{:S(2)}, u32[]{:S(2)}) %collective-permute-start.7) | collective-permute-done | bytes 98336 | tf_op jit(solution)/shard_map/ppermute | solution.py:296
  21.3 0.1 shard_map.135
  21.3 0.3 collective-permute-start.10
  21.6 1.8 %collective-permute-start.9 = (bf16[256,128]{1,0:T(8,128)(2,1)S(1)}, bf16[256,128]{1,0:T(8,128)(2,1)S(1)}, u32[]{:S(2)}, u32[]{:S(2)}) collective-permute-start(bf16[256,128]{1,0:T(8,128)(2,1)S(1)} %get-tuple-element.80.refs_0_), channel_id=1, source_target_pairs={{0,2},{1,17},{2,0},{3,19},{4,6},{5,21},{6,4},{7,23},{8,10},{9,25},... | collective-permute-start | bytes 196616 | tf_op jit(solution)/shard_map/ppermute | solution.py:296
  23.4 0.2 collective-permute-start.8
  23.7 0.0 collective-permute-start.11
  23.7 1.2 %collective-permute-done.11.even_ref = f32[64,128]{1,0:T(8,128)S(1)} collective-permute-done((f32[64,128]{1,0:T(8,128)S(1)}, f32[64,128]{1,0:T(8,128)S(1)}, u32[]{:S(2)}, u32[]{:S(2)}) %collective-permute-start.11) | collective-permute-done | bytes 32800 | tf_op jit(solution)/shard_map/ppermute | solution.py:296
  24.9 0.8 %collective-permute-done.10.refs_3_ = bf16[256,128]{1,0:T(8,128)(2,1)S(1)} collective-permute-done((bf16[256,128]{1,0:T(8,128)(2,1)S(1)}, bf16[256,128]{1,0:T(8,128)(2,1)S(1)}, u32[]{:S(2)}, u32[]{:S(2)}) %collective-permute-start.10) | collective-permute-done | bytes 65568 | tf_op jit(solution)/shard_map/ppermute | solution.py:296
  25.7 0.7 %collective-permute-done.9.refs_2_ = bf16[256,128]{1,0:T(8,128)(2,1)S(1)} collective-permute-done((bf16[256,128]{1,0:T(8,128)(2,1)S(1)}, bf16[256,128]{1,0:T(8,128)(2,1)S(1)}, u32[]{:S(2)}, u32[]{:S(2)}) %collective-permute-start.9) | collective-permute-done | bytes 65568 | tf_op jit(solution)/shard_map/ppermute | solution.py:296
  26.4 1.3 %collective-permute-done.8.refs_1_ = bf16[256,128]{1,0:T(8,128)(2,1)S(1)} collective-permute-done((bf16[256,128]{1,0:T(8,128)(2,1)S(1)}, bf16[256,128]{1,0:T(8,128)(2,1)S(1)}, u32[]{:S(2)}, u32[]{:S(2)}) %collective-permute-start.8) | collective-permute-done | bytes 65568 | tf_op jit(solution)/shard_map/ppermute | solution.py:296
  27.7 0.1 collective-permute-start.12
  27.8 0.9 %shard_map.136 = (bf16[512,128]{1,0:T(8,128)(2,1)}, bf16[512,128]{1,0:T(8,128)(2,1)}) custom-call(bf16[512,128]{1,0:T(8,128)(2,1)S(1)} %get-tuple-element.71.hidden_ref, bf16[512,64]{1,0:T(8,128)(2,1)S(1)} %get-tuple-element.72.place_ref, f32[512,128]{1,0:T(8,128)S(1)} %get-tuple-element.73.local_grad_ref, f32[64,128]{1,0:T(8,128)S(1)} %get-tuple-element.79.odd_ref, ...), custom_call_target="tpu_custom_call" | custom-call | tf_op jit(solution)/shard_map/pallas_call | solution.py:41
  28.7 0.5 %collective-permute-done.12.other_ref = f32[256,128]{1,0:T(8,128)S(1)} collective-permute-done((f32[256,128]{1,0:T(8,128)S(1)}, f32[256,128]{1,0:T(8,128)S(1)}, u32[]{:S(2)}, u32[]{:S(2)}) %collective-permute-start.12) | collective-permute-done | bytes 131104 | tf_op jit(solution)/shard_map/ppermute | solution.py:296
  29.2 0.7 %shard_map.138 = (f32[128,128]{1,0:T(8,128)}, f32[128,128]{1,0:T(8,128)}) custom-call(f32[256,128]{1,0:T(8,128)S(1)} %shard_map.137.mine_ref, f32[256,128]{1,0:T(8,128)S(1)} %collective-permute-done.12.other_ref), custom_call_target="tpu_custom_call" | custom-call | tf_op jit(solution)/shard_map/pallas_call | solution.py:41
  (3 shorter events, 0.1 us)
Async XLA Ops:
  2.1 1.4 %collective-permute-start = (bf16[64,128]{1,0:T(8,128)(2,1)S(1)}, bf16[64,128]{1,0:T(8,128)(2,1)S(1)}, u32[]{:S(2)}, u32[]{:S(2)}) collective-permute-start(bf16[64,128]{1,0:T(8,128)(2,1)S(1)} %get-tuple-element.49.own_ref), channel_id=1, source_target_pairs={{0,1},{1,0},{2,3},{3,2},{4,5},{5,4},{6,7},{7,6},{8,9},{9,8},{10,11... | collective-permute-start | bytes 49160 | tf_op jit(solution)/shard_map/ppermute | solution.py:296
  3.4 10.0 %collective-permute-start.1 = (f32[64,1024]{1,0:T(8,128)S(1)}, f32[64,1024]{1,0:T(8,128)S(1)}, u32[]{:S(2)}, u32[]{:S(2)}) collective-permute-start(f32[64,1024]{1,0:T(8,128)S(1)} %get-tuple-element.59.pack_ref), channel_id=1, source_target_pairs={{0,1},{1,0},{2,3},{3,2},{4,5},{5,4},{6,7},{7,6},{8,9},{9,8},{10,11... | collective-permute-start | bytes 786440 | tf_op jit(solution)/shard_map/ppermute | solution.py:296
  3.8 6.8 %collective-permute-start.4 = (bf16[128,128]{1,0:T(8,128)(2,1)S(1)}, bf16[128,128]{1,0:T(8,128)(2,1)S(1)}, u32[]{:S(2)}, u32[]{:S(2)}) collective-permute-start(bf16[128,128]{1,0:T(8,128)(2,1)S(1)} %shard_map.131.refs_0_), channel_id=1, source_target_pairs={{0,6},{1,7},{2,4},{3,5},{4,2},{5,3},{6,0},{7,1},{8,14},{9,15},{10,... | collective-permute-start | bytes 98312 | tf_op jit(solution)/shard_map/ppermute | solution.py:296
  8.6 4.8 %collective-permute-start.3 = (bf16[128,128]{1,0:T(8,128)(2,1)S(1)}, bf16[128,128]{1,0:T(8,128)(2,1)S(1)}, u32[]{:S(2)}, u32[]{:S(2)}) collective-permute-start(bf16[128,128]{1,0:T(8,128)(2,1)S(1)} %shard_map.131.refs_0_), channel_id=1, source_target_pairs={{0,4},{1,5},{2,6},{3,7},{4,0},{5,1},{6,2},{7,3},{8,12},{9,13},{10,... | collective-permute-start | bytes 98312 | tf_op jit(solution)/shard_map/ppermute | solution.py:296
  8.6 4.8 %collective-permute-start.2 = (bf16[128,128]{1,0:T(8,128)(2,1)S(1)}, bf16[128,128]{1,0:T(8,128)(2,1)S(1)}, u32[]{:S(2)}, u32[]{:S(2)}) collective-permute-start(bf16[128,128]{1,0:T(8,128)(2,1)S(1)} %shard_map.131.refs_0_), channel_id=1, source_target_pairs={{0,2},{1,3},{2,0},{3,1},{4,6},{5,7},{6,4},{7,5},{8,10},{9,11},{10,... | collective-permute-start | bytes 98312 | tf_op jit(solution)/shard_map/ppermute | solution.py:296
  14.1 4.7 %collective-permute-start.5 = (bf16[384,128]{1,0:T(8,128)(2,1)S(1)}, bf16[384,128]{1,0:T(8,128)(2,1)S(1)}, u32[]{:S(2)}, u32[]{:S(2)}) collective-permute-start(bf16[384,128]{1,0:T(8,128)(2,1)S(1)} %get-tuple-element.61), channel_id=1, source_target_pairs={{0,8},{1,3},{2,10},{3,1},{4,12},{5,7},{6,14},{7,5},{8,0},{9,11},{1... | collective-permute-start | bytes 294920 | tf_op jit(solution)/shard_map/ppermute | solution.py:296
  15.6 4.6 %collective-permute-start.6 = (bf16[384,128]{1,0:T(8,128)(2,1)S(1)}, bf16[384,128]{1,0:T(8,128)(2,1)S(1)}, u32[]{:S(2)}, u32[]{:S(2)}) collective-permute-start(bf16[384,128]{1,0:T(8,128)(2,1)S(1)} %get-tuple-element.62), channel_id=1, source_target_pairs={{0,8},{1,5},{2,10},{3,7},{4,12},{5,1},{6,14},{7,3},{8,0},{9,13},{1... | collective-permute-start | bytes 294920 | tf_op jit(solution)/shard_map/ppermute | solution.py:296
  16.2 5.1 %collective-permute-start.7 = (bf16[384,128]{1,0:T(8,128)(2,1)S(1)}, bf16[384,128]{1,0:T(8,128)(2,1)S(1)}, u32[]{:S(2)}, u32[]{:S(2)}) collective-permute-start(bf16[384,128]{1,0:T(8,128)(2,1)S(1)} %get-tuple-element.63), channel_id=1, source_target_pairs={{0,8},{1,7},{2,10},{3,5},{4,12},{5,3},{6,14},{7,1},{8,0},{9,15},{1... | collective-permute-start | bytes 294920 | tf_op jit(solution)/shard_map/ppermute | solution.py:296
  21.3 4.3 %collective-permute-start.10 = (bf16[256,128]{1,0:T(8,128)(2,1)S(1)}, bf16[256,128]{1,0:T(8,128)(2,1)S(1)}, u32[]{:S(2)}, u32[]{:S(2)}) collective-permute-start(bf16[256,128]{1,0:T(8,128)(2,1)S(1)} %get-tuple-element.80.refs_0_), channel_id=1, source_target_pairs={{0,2},{1,25},{2,0},{3,27},{4,6},{5,29},{6,4},{7,31},{8,10},{9,17},... | collective-permute-start | bytes 196616 | tf_op jit(solution)/shard_map/ppermute | solution.py:296
  21.6 4.7 %collective-permute-start.9 = (bf16[256,128]{1,0:T(8,128)(2,1)S(1)}, bf16[256,128]{1,0:T(8,128)(2,1)S(1)}, u32[]{:S(2)}, u32[]{:S(2)}) collective-permute-start(bf16[256,128]{1,0:T(8,128)(2,1)S(1)} %get-tuple-element.80.refs_0_), channel_id=1, source_target_pairs={{0,2},{1,17},{2,0},{3,19},{4,6},{5,21},{6,4},{7,23},{8,10},{9,25},... | collective-permute-start | bytes 196616 | tf_op jit(solution)/shard_map/ppermute | solution.py:296
  23.4 4.3 %collective-permute-start.8 = (bf16[256,128]{1,0:T(8,128)(2,1)S(1)}, bf16[256,128]{1,0:T(8,128)(2,1)S(1)}, u32[]{:S(2)}, u32[]{:S(2)}) collective-permute-start(bf16[256,128]{1,0:T(8,128)(2,1)S(1)} %get-tuple-element.80.refs_0_), channel_id=1, source_target_pairs={{0,2},{1,9},{2,0},{3,11},{4,6},{5,13},{6,4},{7,15},{8,10},{9,1},{1... | collective-permute-start | bytes 196616 | tf_op jit(solution)/shard_map/ppermute | solution.py:296
  23.7 1.2 %collective-permute-start.11 = (f32[64,128]{1,0:T(8,128)S(1)}, f32[64,128]{1,0:T(8,128)S(1)}, u32[]{:S(2)}, u32[]{:S(2)}) collective-permute-start(f32[64,128]{1,0:T(8,128)S(1)} %get-tuple-element.81), channel_id=1, source_target_pairs={{0,1},{1,0},{2,3},{3,2},{4,5},{5,4},{6,7},{7,6},{8,9},{9,8},{10,11... | collective-permute-start | bytes 98312 | tf_op jit(solution)/shard_map/ppermute | solution.py:296
  27.7 1.4 %collective-permute-start.12 = (f32[256,128]{1,0:T(8,128)S(1)}, f32[256,128]{1,0:T(8,128)S(1)}, u32[]{:S(2)}, u32[]{:S(2)}) collective-permute-start(f32[256,128]{1,0:T(8,128)S(1)} %shard_map.137.mine_ref), channel_id=1, source_target_pairs={{0,1},{1,0},{2,3},{3,2},{4,5},{5,4},{6,7},{7,6},{8,9},{9,8},{10,11... | collective-permute-start | bytes 393224 | tf_op jit(solution)/shard_map/ppermute | solution.py:296

commit v5 on v4

--- a/solution.py
+++ b/solution.py
@@ -376,7 +376,7 @@
         own_g,
         *arrived,
     )
-    others = [exchange(column_w, dom_size * k, 2) for k in range(1, group_size)]
+    others = [exchange(column_w, dom_size * k, 2 if k % 2 else dom_size) for k in range(1, group_size)]
     *others, even_g = lax.optimization_barrier((*others, over_core(even_g)))
     hidden, grad_features = call(features_body, [(wide, BF)] * 2, hidden, place, local_grad, odd_g, even_g)
     (mine,) = call(sum_body, [(both, F32)], column_w, *others)

time: 30 us -> 29.2 us (0.973)
  waiting for transfers between devices: 11.3 us -> 9.71 us
  starting transfers between devices: 12.3 us -> 13.1 us
    ppermute x13, waiting for transfers between devices: 11.3 us -> 9.71 us  [exchange(): lax.ppermute(x, ('group', 'dom'), [(a, a ^ (odd_step if a % 2 else even_s...]
    ppermute x13, starting transfers between devices: 12.3 us -> 13.1 us  [exchange(): lax.ppermute(x, ('group', 'dom'), [(a, a ^ (odd_step if a % 2 else even_s...]
  transfers between devices with their start and end apart: 13 -> 13, of which waited for: 10 -> 9; matrix products, arithmetic and copies ran while one was open for 0% -> 0% of each run, Pallas kernels for 9% -> 9%
where the time goes in v5:
time: 29.2 us; the launch traced here: 29.1 us
  starting transfers between devices  13.1 us (45%)
  waiting for transfers between devices  9.71 us (33%)
  Pallas kernels  5.52 us (19%)
  between operations  0.71 us (2%)
    ppermute x13, starting transfers between devices, exchange(): lax.ppermute(x, ('group', 'dom'), [(a, a ^ (odd_step if a % 2 else even_s...  13.1 us
    ppermute x13, waiting for transfers between devices, exchange(): lax.ppermute(x, ('group', 'dom'), [(a, a ^ (odd_step if a % 2 else even_s...  9.71 us
    pallas_call x9, Pallas kernels, call(): pl.pallas_call(body, out_shape=[jax.ShapeDtypeStruct(shape, dtype) for sh...  4.11 us
    pallas_call x1, Pallas kernels, local(): pl.pallas_call(functools.partial(publish_body, len(first)), out_shape=[ja...  1.42 us
  transfers between devices with their start and end apart: 13, of which 9 were waited for; matrix products, arithmetic and copies ran while one was open for 0% of the time, Pallas kernels for 9%

profile of v5, /device:TPU:0, one launch (start us, length us, event | category | flops | bytes accessed | tf_op | source)
XLA Modules:
  0.0 29.1 jit_solution(16706018049045782967)
XLA Ops:
  0.6 1.4 %shard_map.129 = (bf16[64,128]{1,0:T(8,128)(2,1)S(1)}, s32[1,64]{1,0:T(1,128)S(1)}, bf16[512,128]{1,0:T(8,128)(2,1)S(1)}, s32[1,512]{1,0:T(1,128)S(1)}, s32[1,25...) custom-call(s32[1,64]{1,0:T(1,128)} %refs_0_.1, ...), custom_call_target="tpu_custom_call" | custom-call | tf_op jit(solution)/shard_map/pallas_call | solution.py:313
  2.1 0.5 %collective-permute-start = (bf16[64,128]{1,0:T(8,128)(2,1)S(1)}, bf16[64,128]{1,0:T(8,128)(2,1)S(1)}, u32[]{:S(2)}, u32[]{:S(2)}) collective-permute-start(bf16[64,128]{1,0:T(8,128)(2,1)S(1)} %get-tuple-element.49.own_ref), channel_id=1, source_target_pairs={{0,1},{1,0},{2,3},{3,2},{4,5},{5,4},{6,7},{7,6},{8,9},{9,8},{10,11... | collective-permute-start | bytes 49160 | tf_op jit(solution)/shard_map/ppermute | solution.py:296
  2.6 0.7 %shard_map.130 = (bf16[512,64]{1,0:T(8,128)(2,1)S(1)}, s32[1,256]{1,0:T(1,128)S(1)}, bf16[64,512]{1,0:T(8,128)(2,1)S(1)}, bf16[64,512]{1,0:T(8,128)(2,1)S(1)}, f32[64,1024]{1,0:T(8,128)S(1)}) custom-call(s32[1,64]{1,0:T(1,128)S(1)} %get-tuple-element.50.pub_ref, bf16[512,128]{1,0:T(8,128)(2,1)S(1)} %get-tuple-element.51.features_ref, ...), custom_call_target="tpu_custom_call" | custom-call | tf_op jit(solution)/shard_map/pallas_call | solution.py:41
  3.3 0.1 collective-permute-done.other_ref
  3.4 0.3 %collective-permute-start.1 = (f32[64,1024]{1,0:T(8,128)S(1)}, f32[64,1024]{1,0:T(8,128)S(1)}, u32[]{:S(2)}, u32[]{:S(2)}) collective-permute-start(f32[64,1024]{1,0:T(8,128)S(1)} %get-tuple-element.59.pack_ref), channel_id=1, source_target_pairs={{0,1},{1,0},{2,3},{3,2},{4,5},{5,4},{6,7},{7,6},{8,9},{9,8},{10,11... | collective-permute-start | bytes 786440 | tf_op jit(solution)/shard_map/ppermute | solution.py:296
  3.8 4.8 %collective-permute-start.4 = (bf16[128,128]{1,0:T(8,128)(2,1)S(1)}, bf16[128,128]{1,0:T(8,128)(2,1)S(1)}, u32[]{:S(2)}, u32[]{:S(2)}) collective-permute-start(bf16[128,128]{1,0:T(8,128)(2,1)S(1)} %shard_map.131.refs_0_), channel_id=1, source_target_pairs={{0,6},{1,7},{2,4},{3,5},{4,2},{5,3},{6,0},{7,1},{8,14},{9,15},{10,... | collective-permute-start | bytes 98312 | tf_op jit(solution)/shard_map/ppermute | solution.py:296
  8.6 0.0 collective-permute-start.3
  8.6 0.6 %collective-permute-start.2 = (bf16[128,128]{1,0:T(8,128)(2,1)S(1)}, bf16[128,128]{1,0:T(8,128)(2,1)S(1)}, u32[]{:S(2)}, u32[]{:S(2)}) collective-permute-start(bf16[128,128]{1,0:T(8,128)(2,1)S(1)} %shard_map.131.refs_0_), channel_id=1, source_target_pairs={{0,2},{1,3},{2,0},{3,1},{4,6},{5,7},{6,4},{7,5},{8,10},{9,11},{10,... | collective-permute-start | bytes 98312 | tf_op jit(solution)/shard_map/ppermute | solution.py:296
  9.2 1.4 %collective-permute-done.4.refs_3_ = bf16[128,128]{1,0:T(8,128)(2,1)S(1)} collective-permute-done((bf16[128,128]{1,0:T(8,128)(2,1)S(1)}, bf16[128,128]{1,0:T(8,128)(2,1)S(1)}, u32[]{:S(2)}, u32[]{:S(2)}) %collective-permute-start.4) | collective-permute-done | bytes 32800 | tf_op jit(solution)/shard_map/ppermute | solution.py:296
  10.6 2.8 %collective-permute-done.3.refs_2_ = bf16[128,128]{1,0:T(8,128)(2,1)S(1)} collective-permute-done((bf16[128,128]{1,0:T(8,128)(2,1)S(1)}, bf16[128,128]{1,0:T(8,128)(2,1)S(1)}, u32[]{:S(2)}, u32[]{:S(2)}) %collective-permute-start.3) | collective-permute-done | bytes 32800 | tf_op jit(solution)/shard_map/ppermute | solution.py:296
  13.4 0.0 collective-permute-done.2.refs_1_
  13.4 0.0 collective-permute-done.1.got_pack_ref
  13.4 0.6 %shard_map.133 = (bf16[128,128]{1,0:T(8,128)(2,1)S(1)}, bf16[128,128]{1,0:T(8,128)(2,1)S(1)}, f32[128,128]{1,0:T(8,128)S(1)}, bf16[256,128]{1,0:T(8,128)(2,1)S(1...) custom-call(bf16[128,128]{1,0:T(8,128)(2,1)S(1)} %get-tuple-element.47.w_self_ref, ...), custom_call_target="tpu_custom_call" | custom-call | tf_op jit(solution)/shard_map/pallas_call | solution.py:41
  14.1 1.6 %collective-permute-start.5 = (bf16[384,128]{1,0:T(8,128)(2,1)S(1)}, bf16[384,128]{1,0:T(8,128)(2,1)S(1)}, u32[]{:S(2)}, u32[]{:S(2)}) collective-permute-start(bf16[384,128]{1,0:T(8,128)(2,1)S(1)} %get-tuple-element.61), channel_id=1, source_target_pairs={{0,8},{1,3},{2,10},{3,1},{4,12},{5,7},{6,14},{7,5},{8,0},{9,11},{1... | collective-permute-start | bytes 294920 | tf_op jit(solution)/shard_map/ppermute | solution.py:296
  15.6 0.5 %collective-permute-start.6 = (bf16[384,128]{1,0:T(8,128)(2,1)S(1)}, bf16[384,128]{1,0:T(8,128)(2,1)S(1)}, u32[]{:S(2)}, u32[]{:S(2)}) collective-permute-start(bf16[384,128]{1,0:T(8,128)(2,1)S(1)} %get-tuple-element.62), channel_id=1, source_target_pairs={{0,8},{1,5},{2,10},{3,7},{4,12},{5,1},{6,14},{7,3},{8,0},{9,13},{1... | collective-permute-start | bytes 294920 | tf_op jit(solution)/shard_map/ppermute | solution.py:296
  16.2 1.5 %collective-permute-start.7 = (bf16[384,128]{1,0:T(8,128)(2,1)S(1)}, bf16[384,128]{1,0:T(8,128)(2,1)S(1)}, u32[]{:S(2)}, u32[]{:S(2)}) collective-permute-start(bf16[384,128]{1,0:T(8,128)(2,1)S(1)} %get-tuple-element.63), channel_id=1, source_target_pairs={{0,8},{1,7},{2,10},{3,5},{4,12},{5,3},{6,14},{7,1},{8,0},{9,15},{1... | collective-permute-start | bytes 294920 | tf_op jit(solution)/shard_map/ppermute | solution.py:296
  17.6 1.1 %shard_map.134 = (bf16[512,128]{1,0:T(8,128)(2,1)S(1)}, f32[512,128]{1,0:T(8,128)S(1)}) custom-call(bf16[512,128]{1,0:T(8,128)(2,1)S(1)} %get-tuple-element.51.features_ref, bf16[512,512]{1,0:T(8,128)(2,1)S(1)} %get-tuple-element.57.local_ref, bf16[512,256]{1,0:T(8,128)(2,1)S(1)} %get-tuple-element.55.bound_ref, s32[1,256]{1,0:T(1,128)S(1)} %get-tuple-element.64.target_ref, ...), custom_call_target="tpu_custom_call" | custom-call | tf_op jit(solution)/shard_map/pallas_call | solution.py:41
  18.8 0.0 collective-permute-done.5.refs_0_
  18.8 1.4 %collective-permute-done.6.refs_1_ = bf16[384,128]{1,0:T(8,128)(2,1)S(1)} collective-permute-done((bf16[384,128]{1,0:T(8,128)(2,1)S(1)}, bf16[384,128]{1,0:T(8,128)(2,1)S(1)}, u32[]{:S(2)}, u32[]{:S(2)}) %collective-permute-start.6) | collective-permute-done | bytes 98336 | tf_op jit(solution)/shard_map/ppermute | solution.py:296
  20.2 1.1 %collective-permute-done.7.refs_2_ = bf16[384,128]{1,0:T(8,128)(2,1)S(1)} collective-permute-done((bf16[384,128]{1,0:T(8,128)(2,1)S(1)}, bf16[384,128]{1,0:T(8,128)(2,1)S(1)}, u32[]{:S(2)}, u32[]{:S(2)}) %collective-permute-start.7) | collective-permute-done | bytes 98336 | tf_op jit(solution)/shard_map/ppermute | solution.py:296
  21.3 0.1 shard_map.135
  21.3 0.3 %collective-permute-start.10 = (bf16[256,128]{1,0:T(8,128)(2,1)S(1)}, bf16[256,128]{1,0:T(8,128)(2,1)S(1)}, u32[]{:S(2)}, u32[]{:S(2)}) collective-permute-start(bf16[256,128]{1,0:T(8,128)(2,1)S(1)} %get-tuple-element.80.refs_0_), channel_id=1, source_target_pairs={{0,2},{1,25},{2,0},{3,27},{4,6},{5,29},{6,4},{7,31},{8,10},{9,17},... | collective-permute-start | bytes 196616 | tf_op jit(solution)/shard_map/ppermute | solution.py:296
  21.6 1.1 %collective-permute-start.9 = (bf16[256,128]{1,0:T(8,128)(2,1)S(1)}, bf16[256,128]{1,0:T(8,128)(2,1)S(1)}, u32[]{:S(2)}, u32[]{:S(2)}) collective-permute-start(bf16[256,128]{1,0:T(8,128)(2,1)S(1)} %get-tuple-element.80.refs_0_), channel_id=1, source_target_pairs={{0,8},{1,17},{2,10},{3,19},{4,12},{5,21},{6,14},{7,23},{8,0},{9,25... | collective-permute-start | bytes 196616 | tf_op jit(solution)/shard_map/ppermute | solution.py:296
  22.7 1.8 %collective-permute-start.8 = (bf16[256,128]{1,0:T(8,128)(2,1)S(1)}, bf16[256,128]{1,0:T(8,128)(2,1)S(1)}, u32[]{:S(2)}, u32[]{:S(2)}) collective-permute-start(bf16[256,128]{1,0:T(8,128)(2,1)S(1)} %get-tuple-element.80.refs_0_), channel_id=1, source_target_pairs={{0,2},{1,9},{2,0},{3,11},{4,6},{5,13},{6,4},{7,15},{8,10},{9,1},{1... | collective-permute-start | bytes 196616 | tf_op jit(solution)/shard_map/ppermute | solution.py:296
  24.5 0.0 collective-permute-start.11
  24.5 1.2 %collective-permute-done.11.even_ref = f32[64,128]{1,0:T(8,128)S(1)} collective-permute-done((f32[64,128]{1,0:T(8,128)S(1)}, f32[64,128]{1,0:T(8,128)S(1)}, u32[]{:S(2)}, u32[]{:S(2)}) %collective-permute-start.11) | collective-permute-done | bytes 32800 | tf_op jit(solution)/shard_map/ppermute | solution.py:296
  25.7 0.0 collective-permute-done.10.refs_3_
  25.7 0.6 %collective-permute-done.9.refs_2_ = bf16[256,128]{1,0:T(8,128)(2,1)S(1)} collective-permute-done((bf16[256,128]{1,0:T(8,128)(2,1)S(1)}, bf16[256,128]{1,0:T(8,128)(2,1)S(1)}, u32[]{:S(2)}, u32[]{:S(2)}) %collective-permute-start.9) | collective-permute-done | bytes 65568 | tf_op jit(solution)/shard_map/ppermute | solution.py:296
  26.3 0.7 %collective-permute-done.8.refs_1_ = bf16[256,128]{1,0:T(8,128)(2,1)S(1)} collective-permute-done((bf16[256,128]{1,0:T(8,128)(2,1)S(1)}, bf16[256,128]{1,0:T(8,128)(2,1)S(1)}, u32[]{:S(2)}, u32[]{:S(2)}) %collective-permute-start.8) | collective-permute-done | bytes 65568 | tf_op jit(solution)/shard_map/ppermute | solution.py:296
  27.0 0.1 collective-permute-start.12
  27.1 0.9 %shard_map.136 = (bf16[512,128]{1,0:T(8,128)(2,1)}, bf16[512,128]{1,0:T(8,128)(2,1)}) custom-call(bf16[512,128]{1,0:T(8,128)(2,1)S(1)} %get-tuple-element.71.hidden_ref, bf16[512,64]{1,0:T(8,128)(2,1)S(1)} %get-tuple-element.72.place_ref, f32[512,128]{1,0:T(8,128)S(1)} %get-tuple-element.73.local_grad_ref, f32[64,128]{1,0:T(8,128)S(1)} %get-tuple-element.79.odd_ref, ...), custom_call_target="tpu_custom_call" | custom-call | tf_op jit(solution)/shard_map/pallas_call | solution.py:41
  28.0 0.5 %collective-permute-done.12.other_ref = f32[256,128]{1,0:T(8,128)S(1)} collective-permute-done((f32[256,128]{1,0:T(8,128)S(1)}, f32[256,128]{1,0:T(8,128)S(1)}, u32[]{:S(2)}, u32[]{:S(2)}) %collective-permute-start.12) | collective-permute-done | bytes 131104 | tf_op jit(solution)/shard_map/ppermute | solution.py:296
  28.4 0.7 %shard_map.138 = (f32[128,128]{1,0:T(8,128)}, f32[128,128]{1,0:T(8,128)}) custom-call(f32[256,128]{1,0:T(8,128)S(1)} %shard_map.137.mine_ref, f32[256,128]{1,0:T(8,128)S(1)} %collective-permute-done.12.other_ref), custom_call_target="tpu_custom_call" | custom-call | tf_op jit(solution)/shard_map/pallas_call | solution.py:41
  (3 shorter events, 0.1 us)
Async XLA Ops:
  2.1 1.4 %collective-permute-start = (bf16[64,128]{1,0:T(8,128)(2,1)S(1)}, bf16[64,128]{1,0:T(8,128)(2,1)S(1)}, u32[]{:S(2)}, u32[]{:S(2)}) collective-permute-start(bf16[64,128]{1,0:T(8,128)(2,1)S(1)} %get-tuple-element.49.own_ref), channel_id=1, source_target_pairs={{0,1},{1,0},{2,3},{3,2},{4,5},{5,4},{6,7},{7,6},{8,9},{9,8},{10,11... | collective-permute-start | bytes 49160 | tf_op jit(solution)/shard_map/ppermute | solution.py:296
  3.4 10.0 %collective-permute-start.1 = (f32[64,1024]{1,0:T(8,128)S(1)}, f32[64,1024]{1,0:T(8,128)S(1)}, u32[]{:S(2)}, u32[]{:S(2)}) collective-permute-start(f32[64,1024]{1,0:T(8,128)S(1)} %get-tuple-element.59.pack_ref), channel_id=1, source_target_pairs={{0,1},{1,0},{2,3},{3,2},{4,5},{5,4},{6,7},{7,6},{8,9},{9,8},{10,11... | collective-permute-start | bytes 786440 | tf_op jit(solution)/shard_map/ppermute | solution.py:296
  3.8 6.8 %collective-permute-start.4 = (bf16[128,128]{1,0:T(8,128)(2,1)S(1)}, bf16[128,128]{1,0:T(8,128)(2,1)S(1)}, u32[]{:S(2)}, u32[]{:S(2)}) collective-permute-start(bf16[128,128]{1,0:T(8,128)(2,1)S(1)} %shard_map.131.refs_0_), channel_id=1, source_target_pairs={{0,6},{1,7},{2,4},{3,5},{4,2},{5,3},{6,0},{7,1},{8,14},{9,15},{10,... | collective-permute-start | bytes 98312 | tf_op jit(solution)/shard_map/ppermute | solution.py:296
  8.6 4.8 %collective-permute-start.3 = (bf16[128,128]{1,0:T(8,128)(2,1)S(1)}, bf16[128,128]{1,0:T(8,128)(2,1)S(1)}, u32[]{:S(2)}, u32[]{:S(2)}) collective-permute-start(bf16[128,128]{1,0:T(8,128)(2,1)S(1)} %shard_map.131.refs_0_), channel_id=1, source_target_pairs={{0,4},{1,5},{2,6},{3,7},{4,0},{5,1},{6,2},{7,3},{8,12},{9,13},{10,... | collective-permute-start | bytes 98312 | tf_op jit(solution)/shard_map/ppermute | solution.py:296
  8.6 4.8 %collective-permute-start.2 = (bf16[128,128]{1,0:T(8,128)(2,1)S(1)}, bf16[128,128]{1,0:T(8,128)(2,1)S(1)}, u32[]{:S(2)}, u32[]{:S(2)}) collective-permute-start(bf16[128,128]{1,0:T(8,128)(2,1)S(1)} %shard_map.131.refs_0_), channel_id=1, source_target_pairs={{0,2},{1,3},{2,0},{3,1},{4,6},{5,7},{6,4},{7,5},{8,10},{9,11},{10,... | collective-permute-start | bytes 98312 | tf_op jit(solution)/shard_map/ppermute | solution.py:296
  14.1 4.7 %collective-permute-start.5 = (bf16[384,128]{1,0:T(8,128)(2,1)S(1)}, bf16[384,128]{1,0:T(8,128)(2,1)S(1)}, u32[]{:S(2)}, u32[]{:S(2)}) collective-permute-start(bf16[384,128]{1,0:T(8,128)(2,1)S(1)} %get-tuple-element.61), channel_id=1, source_target_pairs={{0,8},{1,3},{2,10},{3,1},{4,12},{5,7},{6,14},{7,5},{8,0},{9,11},{1... | collective-permute-start | bytes 294920 | tf_op jit(solution)/shard_map/ppermute | solution.py:296
  15.6 4.6 %collective-permute-start.6 = (bf16[384,128]{1,0:T(8,128)(2,1)S(1)}, bf16[384,128]{1,0:T(8,128)(2,1)S(1)}, u32[]{:S(2)}, u32[]{:S(2)}) collective-permute-start(bf16[384,128]{1,0:T(8,128)(2,1)S(1)} %get-tuple-element.62), channel_id=1, source_target_pairs={{0,8},{1,5},{2,10},{3,7},{4,12},{5,1},{6,14},{7,3},{8,0},{9,13},{1... | collective-permute-start | bytes 294920 | tf_op jit(solution)/shard_map/ppermute | solution.py:296
  16.2 5.1 %collective-permute-start.7 = (bf16[384,128]{1,0:T(8,128)(2,1)S(1)}, bf16[384,128]{1,0:T(8,128)(2,1)S(1)}, u32[]{:S(2)}, u32[]{:S(2)}) collective-permute-start(bf16[384,128]{1,0:T(8,128)(2,1)S(1)} %get-tuple-element.63), channel_id=1, source_target_pairs={{0,8},{1,7},{2,10},{3,5},{4,12},{5,3},{6,14},{7,1},{8,0},{9,15},{1... | collective-permute-start | bytes 294920 | tf_op jit(solution)/shard_map/ppermute | solution.py:296
  21.3 4.4 %collective-permute-start.10 = (bf16[256,128]{1,0:T(8,128)(2,1)S(1)}, bf16[256,128]{1,0:T(8,128)(2,1)S(1)}, u32[]{:S(2)}, u32[]{:S(2)}) collective-permute-start(bf16[256,128]{1,0:T(8,128)(2,1)S(1)} %get-tuple-element.80.refs_0_), channel_id=1, source_target_pairs={{0,2},{1,25},{2,0},{3,27},{4,6},{5,29},{6,4},{7,31},{8,10},{9,17},... | collective-permute-start | bytes 196616 | tf_op jit(solution)/shard_map/ppermute | solution.py:296
  21.6 4.6 %collective-permute-start.9 = (bf16[256,128]{1,0:T(8,128)(2,1)S(1)}, bf16[256,128]{1,0:T(8,128)(2,1)S(1)}, u32[]{:S(2)}, u32[]{:S(2)}) collective-permute-start(bf16[256,128]{1,0:T(8,128)(2,1)S(1)} %get-tuple-element.80.refs_0_), channel_id=1, source_target_pairs={{0,8},{1,17},{2,10},{3,19},{4,12},{5,21},{6,14},{7,23},{8,0},{9,25... | collective-permute-start | bytes 196616 | tf_op jit(solution)/shard_map/ppermute | solution.py:296
  22.7 4.3 %collective-permute-start.8 = (bf16[256,128]{1,0:T(8,128)(2,1)S(1)}, bf16[256,128]{1,0:T(8,128)(2,1)S(1)}, u32[]{:S(2)}, u32[]{:S(2)}) collective-permute-start(bf16[256,128]{1,0:T(8,128)(2,1)S(1)} %get-tuple-element.80.refs_0_), channel_id=1, source_target_pairs={{0,2},{1,9},{2,0},{3,11},{4,6},{5,13},{6,4},{7,15},{8,10},{9,1},{1... | collective-permute-start | bytes 196616 | tf_op jit(solution)/shard_map/ppermute | solution.py:296
  24.5 1.2 %collective-permute-start.11 = (f32[64,128]{1,0:T(8,128)S(1)}, f32[64,128]{1,0:T(8,128)S(1)}, u32[]{:S(2)}, u32[]{:S(2)}) collective-permute-start(f32[64,128]{1,0:T(8,128)S(1)} %get-tuple-element.81), channel_id=1, source_target_pairs={{0,1},{1,0},{2,3},{3,2},{4,5},{5,4},{6,7},{7,6},{8,9},{9,8},{10,11... | collective-permute-start | bytes 98312 | tf_op jit(solution)/shard_map/ppermute | solution.py:296
  27.0 1.4 %collective-permute-start.12 = (f32[256,128]{1,0:T(8,128)S(1)}, f32[256,128]{1,0:T(8,128)S(1)}, u32[]{:S(2)}, u32[]{:S(2)}) collective-permute-start(f32[256,128]{1,0:T(8,128)S(1)} %shard_map.137.mine_ref), channel_id=1, source_target_pairs={{0,1},{1,0},{2,3},{3,2},{4,5},{5,4},{6,7},{7,6},{8,9},{9,8},{10,11... | collective-permute-start | bytes 393224 | tf_op jit(solution)/shard_map/ppermute | solution.py:296

commit v6 on v5

--- a/solution.py
+++ b/solution.py
@@ -336,7 +336,7 @@
     )
     other, pack = lax.optimization_barrier((other, pack))
     (pair,) = call(pair_body, [((2 * pub_count, width), BF)], published, other)
-    pairs = [pair] + [exchange(pair, 2 * z, 2 * z) for z in range(1, z_size)]
+    pairs = [pair] + [exchange(pair, 2 * z + 1, 2 * z + 1) for z in range(1, z_size)]
 
     square, both = (width, width), (2 * width, width)
     message = ((2 * pub_count + 2 * width, width), BF)

time: 29.2 us -> 28.8 us (0.986)
  no operation moved by 1% of the time
where the time goes in v6:
time: 28.8 us; the launch traced here: 28.7 us
  starting transfers between devices  13 us (45%)
  waiting for transfers between devices  9.5 us (33%)
  Pallas kernels  5.51 us (19%)
  between operations  0.71 us (2%)
    ppermute x13, starting transfers between devices, exchange(): lax.ppermute(x, ('group', 'dom'), [(a, a ^ (odd_step if a % 2 else even_s...  13 us
    ppermute x13, waiting for transfers between devices, exchange(): lax.ppermute(x, ('group', 'dom'), [(a, a ^ (odd_step if a % 2 else even_s...  9.5 us
    pallas_call x9, Pallas kernels, call(): pl.pallas_call(body, out_shape=[jax.ShapeDtypeStruct(shape, dtype) for sh...  4.09 us
    pallas_call x1, Pallas kernels, local(): pl.pallas_call(functools.partial(publish_body, len(first)), out_shape=[ja...  1.42 us
  transfers between devices with their start and end apart: 13, of which 9 were waited for; matrix products, arithmetic and copies ran while one was open for 0% of the time, Pallas kernels for 9%

profile of v6, /device:TPU:0, one launch (start us, length us, event | category | flops | bytes accessed | tf_op | source)
XLA Modules:
  0.0 28.7 jit_solution(14999724075220691099)
XLA Ops:
  0.6 1.4 %shard_map.129 = (bf16[64,128]{1,0:T(8,128)(2,1)S(1)}, s32[1,64]{1,0:T(1,128)S(1)}, bf16[512,128]{1,0:T(8,128)(2,1)S(1)}, s32[1,512]{1,0:T(1,128)S(1)}, s32[1,25...) custom-call(s32[1,64]{1,0:T(1,128)} %refs_0_.1, ...), custom_call_target="tpu_custom_call" | custom-call | tf_op jit(solution)/shard_map/pallas_call | solution.py:313
  2.1 0.5 %collective-permute-start = (bf16[64,128]{1,0:T(8,128)(2,1)S(1)}, bf16[64,128]{1,0:T(8,128)(2,1)S(1)}, u32[]{:S(2)}, u32[]{:S(2)}) collective-permute-start(bf16[64,128]{1,0:T(8,128)(2,1)S(1)} %get-tuple-element.49.own_ref), channel_id=1, source_target_pairs={{0,1},{1,0},{2,3},{3,2},{4,5},{5,4},{6,7},{7,6},{8,9},{9,8},{10,11... | collective-permute-start | bytes 49160 | tf_op jit(solution)/shard_map/ppermute | solution.py:296
  2.6 0.7 %shard_map.130 = (bf16[512,64]{1,0:T(8,128)(2,1)S(1)}, s32[1,256]{1,0:T(1,128)S(1)}, bf16[64,512]{1,0:T(8,128)(2,1)S(1)}, bf16[64,512]{1,0:T(8,128)(2,1)S(1)}, f32[64,1024]{1,0:T(8,128)S(1)}) custom-call(s32[1,64]{1,0:T(1,128)S(1)} %get-tuple-element.50.pub_ref, bf16[512,128]{1,0:T(8,128)(2,1)S(1)} %get-tuple-element.51.features_ref, ...), custom_call_target="tpu_custom_call" | custom-call | tf_op jit(solution)/shard_map/pallas_call | solution.py:41
  3.3 0.1 collective-permute-done.other_ref
  3.4 0.3 %collective-permute-start.1 = (f32[64,1024]{1,0:T(8,128)S(1)}, f32[64,1024]{1,0:T(8,128)S(1)}, u32[]{:S(2)}, u32[]{:S(2)}) collective-permute-start(f32[64,1024]{1,0:T(8,128)S(1)} %get-tuple-element.59.pack_ref), channel_id=1, source_target_pairs={{0,1},{1,0},{2,3},{3,2},{4,5},{5,4},{6,7},{7,6},{8,9},{9,8},{10,11... | collective-permute-start | bytes 786440 | tf_op jit(solution)/shard_map/ppermute | solution.py:296
  3.8 4.8 %collective-permute-start.4 = (bf16[128,128]{1,0:T(8,128)(2,1)S(1)}, bf16[128,128]{1,0:T(8,128)(2,1)S(1)}, u32[]{:S(2)}, u32[]{:S(2)}) collective-permute-start(bf16[128,128]{1,0:T(8,128)(2,1)S(1)} %shard_map.131.refs_0_), channel_id=1, source_target_pairs={{0,7},{1,6},{2,5},{3,4},{4,3},{5,2},{6,1},{7,0},{8,15},{9,14},{10,... | collective-permute-start | bytes 98312 | tf_op jit(solution)/shard_map/ppermute | solution.py:296
  8.6 0.0 collective-permute-start.3
  8.6 0.4 %collective-permute-start.2 = (bf16[128,128]{1,0:T(8,128)(2,1)S(1)}, bf16[128,128]{1,0:T(8,128)(2,1)S(1)}, u32[]{:S(2)}, u32[]{:S(2)}) collective-permute-start(bf16[128,128]{1,0:T(8,128)(2,1)S(1)} %shard_map.131.refs_0_), channel_id=1, source_target_pairs={{0,3},{1,2},{2,1},{3,0},{4,7},{5,6},{6,5},{7,4},{8,11},{9,10},{10,... | collective-permute-start | bytes 98312 | tf_op jit(solution)/shard_map/ppermute | solution.py:296
  9.0 1.3 %collective-permute-done.4.refs_3_ = bf16[128,128]{1,0:T(8,128)(2,1)S(1)} collective-permute-done((bf16[128,128]{1,0:T(8,128)(2,1)S(1)}, bf16[128,128]{1,0:T(8,128)(2,1)S(1)}, u32[]{:S(2)}, u32[]{:S(2)}) %collective-permute-start.4) | collective-permute-done | bytes 32800 | tf_op jit(solution)/shard_map/ppermute | solution.py:296
  10.3 2.5 %collective-permute-done.3.refs_2_ = bf16[128,128]{1,0:T(8,128)(2,1)S(1)} collective-permute-done((bf16[128,128]{1,0:T(8,128)(2,1)S(1)}, bf16[128,128]{1,0:T(8,128)(2,1)S(1)}, u32[]{:S(2)}, u32[]{:S(2)}) %collective-permute-start.3) | collective-permute-done | bytes 32800 | tf_op jit(solution)/shard_map/ppermute | solution.py:296
  12.8 0.0 collective-permute-done.2.refs_1_
  12.8 0.0 collective-permute-done.1.got_pack_ref
  12.8 0.6 %shard_map.133 = (bf16[128,128]{1,0:T(8,128)(2,1)S(1)}, bf16[128,128]{1,0:T(8,128)(2,1)S(1)}, f32[128,128]{1,0:T(8,128)S(1)}, bf16[256,128]{1,0:T(8,128)(2,1)S(1...) custom-call(bf16[128,128]{1,0:T(8,128)(2,1)S(1)} %get-tuple-element.47.w_self_ref, ...), custom_call_target="tpu_custom_call" | custom-call | tf_op jit(solution)/shard_map/pallas_call | solution.py:41
  13.4 1.6 %collective-permute-start.5 = (bf16[384,128]{1,0:T(8,128)(2,1)S(1)}, bf16[384,128]{1,0:T(8,128)(2,1)S(1)}, u32[]{:S(2)}, u32[]{:S(2)}) collective-permute-start(bf16[384,128]{1,0:T(8,128)(2,1)S(1)} %get-tuple-element.61), channel_id=1, source_target_pairs={{0,8},{1,3},{2,10},{3,1},{4,12},{5,7},{6,14},{7,5},{8,0},{9,11},{1... | collective-permute-start | bytes 294920 | tf_op jit(solution)/shard_map/ppermute | solution.py:296
  15.0 0.5 %collective-permute-start.6 = (bf16[384,128]{1,0:T(8,128)(2,1)S(1)}, bf16[384,128]{1,0:T(8,128)(2,1)S(1)}, u32[]{:S(2)}, u32[]{:S(2)}) collective-permute-start(bf16[384,128]{1,0:T(8,128)(2,1)S(1)} %get-tuple-element.62), channel_id=1, source_target_pairs={{0,8},{1,5},{2,10},{3,7},{4,12},{5,1},{6,14},{7,3},{8,0},{9,13},{1... | collective-permute-start | bytes 294920 | tf_op jit(solution)/shard_map/ppermute | solution.py:296
  15.5 1.5 %collective-permute-start.7 = (bf16[384,128]{1,0:T(8,128)(2,1)S(1)}, bf16[384,128]{1,0:T(8,128)(2,1)S(1)}, u32[]{:S(2)}, u32[]{:S(2)}) collective-permute-start(bf16[384,128]{1,0:T(8,128)(2,1)S(1)} %get-tuple-element.63), channel_id=1, source_target_pairs={{0,8},{1,7},{2,10},{3,5},{4,12},{5,3},{6,14},{7,1},{8,0},{9,15},{1... | collective-permute-start | bytes 294920 | tf_op jit(solution)/shard_map/ppermute | solution.py:296
  17.0 1.1 %shard_map.134 = (bf16[512,128]{1,0:T(8,128)(2,1)S(1)}, f32[512,128]{1,0:T(8,128)S(1)}) custom-call(bf16[512,128]{1,0:T(8,128)(2,1)S(1)} %get-tuple-element.51.features_ref, bf16[512,512]{1,0:T(8,128)(2,1)S(1)} %get-tuple-element.57.local_ref, bf16[512,256]{1,0:T(8,128)(2,1)S(1)} %get-tuple-element.55.bound_ref, s32[1,256]{1,0:T(1,128)S(1)} %get-tuple-element.64.target_ref, ...), custom_call_target="tpu_custom_call" | custom-call | tf_op jit(solution)/shard_map/pallas_call | solution.py:41
  18.2 0.0 collective-permute-done.5.refs_0_
  18.2 1.4 %collective-permute-done.6.refs_1_ = bf16[384,128]{1,0:T(8,128)(2,1)S(1)} collective-permute-done((bf16[384,128]{1,0:T(8,128)(2,1)S(1)}, bf16[384,128]{1,0:T(8,128)(2,1)S(1)}, u32[]{:S(2)}, u32[]{:S(2)}) %collective-permute-start.6) | collective-permute-done | bytes 98336 | tf_op jit(solution)/shard_map/ppermute | solution.py:296
  19.6 1.1 %collective-permute-done.7.refs_2_ = bf16[384,128]{1,0:T(8,128)(2,1)S(1)} collective-permute-done((bf16[384,128]{1,0:T(8,128)(2,1)S(1)}, bf16[384,128]{1,0:T(8,128)(2,1)S(1)}, u32[]{:S(2)}, u32[]{:S(2)}) %collective-permute-start.7) | collective-permute-done | bytes 98336 | tf_op jit(solution)/shard_map/ppermute | solution.py:296
  20.7 0.1 shard_map.135
  20.7 0.5 %collective-permute-start.10 = (bf16[256,128]{1,0:T(8,128)(2,1)S(1)}, bf16[256,128]{1,0:T(8,128)(2,1)S(1)}, u32[]{:S(2)}, u32[]{:S(2)}) collective-permute-start(bf16[256,128]{1,0:T(8,128)(2,1)S(1)} %get-tuple-element.80.refs_0_), channel_id=1, source_target_pairs={{0,2},{1,25},{2,0},{3,27},{4,6},{5,29},{6,4},{7,31},{8,10},{9,17},... | collective-permute-start | bytes 196616 | tf_op jit(solution)/shard_map/ppermute | solution.py:296
  21.2 1.1 %collective-permute-start.9 = (bf16[256,128]{1,0:T(8,128)(2,1)S(1)}, bf16[256,128]{1,0:T(8,128)(2,1)S(1)}, u32[]{:S(2)}, u32[]{:S(2)}) collective-permute-start(bf16[256,128]{1,0:T(8,128)(2,1)S(1)} %get-tuple-element.80.refs_0_), channel_id=1, source_target_pairs={{0,8},{1,17},{2,10},{3,19},{4,12},{5,21},{6,14},{7,23},{8,0},{9,25... | collective-permute-start | bytes 196616 | tf_op jit(solution)/shard_map/ppermute | solution.py:296
  22.3 1.6 %collective-permute-start.8 = (bf16[256,128]{1,0:T(8,128)(2,1)S(1)}, bf16[256,128]{1,0:T(8,128)(2,1)S(1)}, u32[]{:S(2)}, u32[]{:S(2)}) collective-permute-start(bf16[256,128]{1,0:T(8,128)(2,1)S(1)} %get-tuple-element.80.refs_0_), channel_id=1, source_target_pairs={{0,2},{1,9},{2,0},{3,11},{4,6},{5,13},{6,4},{7,15},{8,10},{9,1},{1... | collective-permute-start | bytes 196616 | tf_op jit(solution)/shard_map/ppermute | solution.py:296
  23.9 0.0 collective-permute-start.11
  23.9 1.2 %collective-permute-done.11.even_ref = f32[64,128]{1,0:T(8,128)S(1)} collective-permute-done((f32[64,128]{1,0:T(8,128)S(1)}, f32[64,128]{1,0:T(8,128)S(1)}, u32[]{:S(2)}, u32[]{:S(2)}) %collective-permute-start.11) | collective-permute-done | bytes 32800 | tf_op jit(solution)/shard_map/ppermute | solution.py:296
  25.1 0.0 collective-permute-done.10.refs_3_
  25.1 0.9 %collective-permute-done.9.refs_2_ = bf16[256,128]{1,0:T(8,128)(2,1)S(1)} collective-permute-done((bf16[256,128]{1,0:T(8,128)(2,1)S(1)}, bf16[256,128]{1,0:T(8,128)(2,1)S(1)}, u32[]{:S(2)}, u32[]{:S(2)}) %collective-permute-start.9) | collective-permute-done | bytes 65568 | tf_op jit(solution)/shard_map/ppermute | solution.py:296
  26.0 0.5 %collective-permute-done.8.refs_1_ = bf16[256,128]{1,0:T(8,128)(2,1)S(1)} collective-permute-done((bf16[256,128]{1,0:T(8,128)(2,1)S(1)}, bf16[256,128]{1,0:T(8,128)(2,1)S(1)}, u32[]{:S(2)}, u32[]{:S(2)}) %collective-permute-start.8) | collective-permute-done | bytes 65568 | tf_op jit(solution)/shard_map/ppermute | solution.py:296
  26.6 0.2 collective-permute-start.12
  26.8 0.9 %shard_map.136 = (bf16[512,128]{1,0:T(8,128)(2,1)}, bf16[512,128]{1,0:T(8,128)(2,1)}) custom-call(bf16[512,128]{1,0:T(8,128)(2,1)S(1)} %get-tuple-element.71.hidden_ref, bf16[512,64]{1,0:T(8,128)(2,1)S(1)} %get-tuple-element.72.place_ref, f32[512,128]{1,0:T(8,128)S(1)} %get-tuple-element.73.local_grad_ref, f32[64,128]{1,0:T(8,128)S(1)} %get-tuple-element.79.odd_ref, ...), custom_call_target="tpu_custom_call" | custom-call | tf_op jit(solution)/shard_map/pallas_call | solution.py:41
  27.6 0.4 %collective-permute-done.12.other_ref = f32[256,128]{1,0:T(8,128)S(1)} collective-permute-done((f32[256,128]{1,0:T(8,128)S(1)}, f32[256,128]{1,0:T(8,128)S(1)}, u32[]{:S(2)}, u32[]{:S(2)}) %collective-permute-start.12) | collective-permute-done | bytes 131104 | tf_op jit(solution)/shard_map/ppermute | solution.py:296
  28.0 0.7 %shard_map.138 = (f32[128,128]{1,0:T(8,128)}, f32[128,128]{1,0:T(8,128)}) custom-call(f32[256,128]{1,0:T(8,128)S(1)} %shard_map.137.mine_ref, f32[256,128]{1,0:T(8,128)S(1)} %collective-permute-done.12.other_ref), custom_call_target="tpu_custom_call" | custom-call | tf_op jit(solution)/shard_map/pallas_call | solution.py:41
  (3 shorter events, 0.1 us)
Async XLA Ops:
  2.1 1.4 %collective-permute-start = (bf16[64,128]{1,0:T(8,128)(2,1)S(1)}, bf16[64,128]{1,0:T(8,128)(2,1)S(1)}, u32[]{:S(2)}, u32[]{:S(2)}) collective-permute-start(bf16[64,128]{1,0:T(8,128)(2,1)S(1)} %get-tuple-element.49.own_ref), channel_id=1, source_target_pairs={{0,1},{1,0},{2,3},{3,2},{4,5},{5,4},{6,7},{7,6},{8,9},{9,8},{10,11... | collective-permute-start | bytes 49160 | tf_op jit(solution)/shard_map/ppermute | solution.py:296
  3.4 9.4 %collective-permute-start.1 = (f32[64,1024]{1,0:T(8,128)S(1)}, f32[64,1024]{1,0:T(8,128)S(1)}, u32[]{:S(2)}, u32[]{:S(2)}) collective-permute-start(f32[64,1024]{1,0:T(8,128)S(1)} %get-tuple-element.59.pack_ref), channel_id=1, source_target_pairs={{0,1},{1,0},{2,3},{3,2},{4,5},{5,4},{6,7},{7,6},{8,9},{9,8},{10,11... | collective-permute-start | bytes 786440 | tf_op jit(solution)/shard_map/ppermute | solution.py:296
  3.8 6.5 %collective-permute-start.4 = (bf16[128,128]{1,0:T(8,128)(2,1)S(1)}, bf16[128,128]{1,0:T(8,128)(2,1)S(1)}, u32[]{:S(2)}, u32[]{:S(2)}) collective-permute-start(bf16[128,128]{1,0:T(8,128)(2,1)S(1)} %shard_map.131.refs_0_), channel_id=1, source_target_pairs={{0,7},{1,6},{2,5},{3,4},{4,3},{5,2},{6,1},{7,0},{8,15},{9,14},{10,... | collective-permute-start | bytes 98312 | tf_op jit(solution)/shard_map/ppermute | solution.py:296
  8.6 4.2 %collective-permute-start.3 = (bf16[128,128]{1,0:T(8,128)(2,1)S(1)}, bf16[128,128]{1,0:T(8,128)(2,1)S(1)}, u32[]{:S(2)}, u32[]{:S(2)}) collective-permute-start(bf16[128,128]{1,0:T(8,128)(2,1)S(1)} %shard_map.131.refs_0_), channel_id=1, source_target_pairs={{0,5},{1,4},{2,7},{3,6},{4,1},{5,0},{6,3},{7,2},{8,13},{9,12},{10,... | collective-permute-start | bytes 98312 | tf_op jit(solution)/shard_map/ppermute | solution.py:296
  8.6 4.2 %collective-permute-start.2 = (bf16[128,128]{1,0:T(8,128)(2,1)S(1)}, bf16[128,128]{1,0:T(8,128)(2,1)S(1)}, u32[]{:S(2)}, u32[]{:S(2)}) collective-permute-start(bf16[128,128]{1,0:T(8,128)(2,1)S(1)} %shard_map.131.refs_0_), channel_id=1, source_target_pairs={{0,3},{1,2},{2,1},{3,0},{4,7},{5,6},{6,5},{7,4},{8,11},{9,10},{10,... | collective-permute-start | bytes 98312 | tf_op jit(solution)/shard_map/ppermute | solution.py:296
  13.4 4.7 %collective-permute-start.5 = (bf16[384,128]{1,0:T(8,128)(2,1)S(1)}, bf16[384,128]{1,0:T(8,128)(2,1)S(1)}, u32[]{:S(2)}, u32[]{:S(2)}) collective-permute-start(bf16[384,128]{1,0:T(8,128)(2,1)S(1)} %get-tuple-element.61), channel_id=1, source_target_pairs={{0,8},{1,3},{2,10},{3,1},{4,12},{5,7},{6,14},{7,5},{8,0},{9,11},{1... | collective-permute-start | bytes 294920 | tf_op jit(solution)/shard_map/ppermute | solution.py:296
  15.0 4.6 %collective-permute-start.6 = (bf16[384,128]{1,0:T(8,128)(2,1)S(1)}, bf16[384,128]{1,0:T(8,128)(2,1)S(1)}, u32[]{:S(2)}, u32[]{:S(2)}) collective-permute-start(bf16[384,128]{1,0:T(8,128)(2,1)S(1)} %get-tuple-element.62), channel_id=1, source_target_pairs={{0,8},{1,5},{2,10},{3,7},{4,12},{5,1},{6,14},{7,3},{8,0},{9,13},{1... | collective-permute-start | bytes 294920 | tf_op jit(solution)/shard_map/ppermute | solution.py:296
  15.5 5.1 %collective-permute-start.7 = (bf16[384,128]{1,0:T(8,128)(2,1)S(1)}, bf16[384,128]{1,0:T(8,128)(2,1)S(1)}, u32[]{:S(2)}, u32[]{:S(2)}) collective-permute-start(bf16[384,128]{1,0:T(8,128)(2,1)S(1)} %get-tuple-element.63), channel_id=1, source_target_pairs={{0,8},{1,7},{2,10},{3,5},{4,12},{5,3},{6,14},{7,1},{8,0},{9,15},{1... | collective-permute-start | bytes 294920 | tf_op jit(solution)/shard_map/ppermute | solution.py:296
  20.7 4.4 %collective-permute-start.10 = (bf16[256,128]{1,0:T(8,128)(2,1)S(1)}, bf16[256,128]{1,0:T(8,128)(2,1)S(1)}, u32[]{:S(2)}, u32[]{:S(2)}) collective-permute-start(bf16[256,128]{1,0:T(8,128)(2,1)S(1)} %get-tuple-element.80.refs_0_), channel_id=1, source_target_pairs={{0,2},{1,25},{2,0},{3,27},{4,6},{5,29},{6,4},{7,31},{8,10},{9,17},... | collective-permute-start | bytes 196616 | tf_op jit(solution)/shard_map/ppermute | solution.py:296
  21.2 4.8 %collective-permute-start.9 = (bf16[256,128]{1,0:T(8,128)(2,1)S(1)}, bf16[256,128]{1,0:T(8,128)(2,1)S(1)}, u32[]{:S(2)}, u32[]{:S(2)}) collective-permute-start(bf16[256,128]{1,0:T(8,128)(2,1)S(1)} %get-tuple-element.80.refs_0_), channel_id=1, source_target_pairs={{0,8},{1,17},{2,10},{3,19},{4,12},{5,21},{6,14},{7,23},{8,0},{9,25... | collective-permute-start | bytes 196616 | tf_op jit(solution)/shard_map/ppermute | solution.py:296
  22.3 4.3 %collective-permute-start.8 = (bf16[256,128]{1,0:T(8,128)(2,1)S(1)}, bf16[256,128]{1,0:T(8,128)(2,1)S(1)}, u32[]{:S(2)}, u32[]{:S(2)}) collective-permute-start(bf16[256,128]{1,0:T(8,128)(2,1)S(1)} %get-tuple-element.80.refs_0_), channel_id=1, source_target_pairs={{0,2},{1,9},{2,0},{3,11},{4,6},{5,13},{6,4},{7,15},{8,10},{9,1},{1... | collective-permute-start | bytes 196616 | tf_op jit(solution)/shard_map/ppermute | solution.py:296
  23.9 1.2 %collective-permute-start.11 = (f32[64,128]{1,0:T(8,128)S(1)}, f32[64,128]{1,0:T(8,128)S(1)}, u32[]{:S(2)}, u32[]{:S(2)}) collective-permute-start(f32[64,128]{1,0:T(8,128)S(1)} %get-tuple-element.81), channel_id=1, source_target_pairs={{0,1},{1,0},{2,3},{3,2},{4,5},{5,4},{6,7},{7,6},{8,9},{9,8},{10,11... | collective-permute-start | bytes 98312 | tf_op jit(solution)/shard_map/ppermute | solution.py:296
  26.6 1.4 %collective-permute-start.12 = (f32[256,128]{1,0:T(8,128)S(1)}, f32[256,128]{1,0:T(8,128)S(1)}, u32[]{:S(2)}, u32[]{:S(2)}) collective-permute-start(f32[256,128]{1,0:T(8,128)S(1)} %shard_map.137.mine_ref), channel_id=1, source_target_pairs={{0,1},{1,0},{2,3},{3,2},{4,5},{5,4},{6,7},{7,6},{8,9},{9,8},{10,11... | collective-permute-start | bytes 393224 | tf_op jit(solution)/shard_map/ppermute | solution.py:296

commit v7 on v6

--- a/solution.py
+++ b/solution.py
@@ -158,14 +158,29 @@
     pack_ref[:, columns + 3 * width :] = 1.0 / (1.0 + sums)
 
 
-def rows_body(*refs):
-    pairs, out_ref = refs[:-1], refs[-1]
-    count = pairs[0].shape[0]
-    for z, pair in enumerate(pairs):
-        out_ref[z * count : (z + 1) * count, :] = pair[...]
+def either(mine, others):
+    odd = odd_core()
+    pairs = [(a[...], b[...]) for a, b in zip(mine, others)]
+    return [jnp.where(odd, a, b) for a, b in pairs] + [jnp.where(odd, b, a) for a, b in pairs]
+
+
+def by_peer(peers, own, refs):
+    near, *far = peers
+    count = len(far) // 2
+    parts = dict(zip(far, either(refs[1 : 1 + count], refs[1 + count : 1 + 2 * count])))
+    parts |= {0: own, near: refs[0][...]}
+    return [parts[k] for k in sorted(parts)]
+
+
+def rows_body(peers, pair_ref, *refs):
+    refs, out_ref = refs[:-1], refs[-1]
+    count = pair_ref.shape[0]
+    for z, pair in enumerate(by_peer(peers, pair_ref[...], refs)):
+        out_ref[z * count : (z + 1) * count, :] = pair
 
 
 def target_body(
+    peers,
     w_self_ref,
     w_neigh_ref,
     pack_ref,
@@ -177,7 +192,7 @@
     total_ref,
     *messages,
 ):
-    count = rows_ref.shape[0] // (1 + len(messages))
+    count = rows_ref.shape[0] // (1 + len(peers))
     odd = odd_core()
     columns, width = rows_ref.shape
     own, other = pack_ref[...], got_pack_ref[...]
@@ -197,8 +212,12 @@
     total_ref[...] = total
     grads = dot_t(adj, grad_agg)
     own_ref[...] = grads[:count]
-    for z, message in zip(range(len(messages), 0, -1), messages):
-        message[:count, :] = grads[z * count : (z + 1) * count].astype(BF)
+    near, *far = peers
+    halves = len(far) // 2
+    blocks = [grads[z * count : (z + 1) * count] for z in range(1 + len(peers))]
+    blocks = [blocks[near]] + [jnp.where(odd, blocks[a], blocks[b]) for a, b in zip(far[:halves], far[halves:])]
+    for block, message in zip(blocks, messages):
+        message[:count, :] = block.astype(BF)
         message[count:, :] = total
 
 
@@ -241,36 +260,40 @@
     out_ref[...] = dot_nt(spread, w_self_ref[...]) + dot_t(near_ref[...], grad_agg)
 
 
-def column_body(scale, total_ref, own_ref, *refs):
-    messages, (out_ref, even_ref, odd_ref) = refs[:-3], refs[-3:]
+def column_body(peers, scale, total_ref, own_ref, *refs):
+    refs, (out_ref, grads_ref) = refs[:-2], refs[-2:]
     rows = own_ref.shape[0]
-    parts = [total_ref[...]] + [message[rows:, :] for message in messages]
-    out_ref[...] = (tree_sum([part.astype(F32) for part in parts]) * scale).astype(BF)
+    messages = by_peer(peers, None, refs)[1:]
+    total = tree_sum([part.astype(F32) for part in [total_ref[...]] + [x[rows:] for x in messages]])
+    out_ref[...] = (total * scale).astype(BF)
     grads = own_ref[...]
     for message in messages:
-        grads = grads + message[:rows, :].astype(F32)
-    even_ref[...] = grads[: rows // 2]
-    odd_ref[...] = grads[rows // 2 :]
-
-
-def features_body(hidden_ref, place_ref, local_grad_ref, odd_ref, even_ref, hidden_out, out_ref):
+        grads = grads + message[:rows].astype(F32)
+    grads_ref[...] = jnp.where(odd_core(), grads[rows // 2 :], grads[: rows // 2])
+
+
+def features_body(hidden_ref, place_ref, local_grad_ref, grads_ref, hidden_out, out_ref):
     hidden_out[...] = hidden_ref[...]
-    total = jnp.where(odd_core(), odd_ref[...], even_ref[...])
+    total = grads_ref[...]
     place = place_ref[...]
     high = total.astype(BF)
     low = (total - high.astype(F32)).astype(BF)
     out_ref[...] = (local_grad_ref[...] + dot(place, high) + dot(place, low)).astype(BF)
 
 
-def sum_body(*refs):
-    refs[-1][...] = tree_sum([part[...].astype(F32) for part in refs[:-1]])
-
-
-def order_body(mine_ref, other_ref, self_ref, neigh_ref):
-    total = jnp.where(odd_core(), mine_ref[...], other_ref[...])
+def order_body(peers, own_ref, *refs):
+    refs, (self_ref, neigh_ref) = refs[:-2], refs[-2:]
+    total = tree_sum([part.astype(F32) for part in by_peer(peers, own_ref[...], refs)])
     width = self_ref.shape[0]
     self_ref[...] = total[:width]
     neigh_ref[...] = total[width:]
+
+
+def split_peers(size, near=1, swap=False):
+    far = [k for k in range(size - 1, 0, -1) if k != near]
+    if swap:
+        return [near] + far[1::2] + far[::2]
+    return [near] + far[::2] + far[1::2]
 
 
 def local(
@@ -336,14 +359,23 @@
     )
     other, pack = lax.optimization_barrier((other, pack))
     (pair,) = call(pair_body, [((2 * pub_count, width), BF)], published, other)
-    pairs = [pair] + [exchange(pair, 2 * z + 1, 2 * z + 1) for z in range(1, z_size)]
-
+    def stage(near, far, peers, step, also=()):
+        first, *rest = peers
+        count = len(rest) // 2
+        got = [exchange(near, step * first + 1, step * first + 1)]
+        got += [exchange(x, step * a, step * b) for x, a, b in zip(far, rest[:count], rest[count:])]
+        if also:
+            got[-1], *also = lax.optimization_barrier((got[-1], *also))
+        return got + [over_core(x) for x in got[1:]], also
+
+    c_peers, z_peers, group_peers = split_peers(z_size, 1), split_peers(z_size, 3), split_peers(group_size, 2)
+    got, _ = stage(pair, [pair] * (len(c_peers) // 2), c_peers, 2)
     square, both = (width, width), (2 * width, width)
     message = ((2 * pub_count + 2 * width, width), BF)
-    (rows,) = call(rows_body, [((columns, width), BF)], *pairs)
+    (rows,) = call(functools.partial(rows_body, c_peers), [((columns, width), BF)], pair, *got)
     grad_pre, grad_agg, own_g, chip_w, *messages = call(
-        target_body,
-        [((2 * hits, width), BF)] * 2 + [((2 * pub_count, width), F32), (both, BF)] + [message] * (z_size - 1),
+        functools.partial(target_body, z_peers),
+        [((2 * hits, width), BF)] * 2 + [((2 * pub_count, width), F32), (both, BF)] + [message] * (1 + len(z_peers) // 2),
         w_self,
         w_neigh,
         pack,
@@ -365,22 +397,22 @@
         grad_pre,
         grad_agg,
     )
-    far = range(z_size - 1, 0, -1)
-    arrived = [exchange(x, 2 * z, dom_size) for z, x in zip(far, messages)][::-1]
-    *arrived, hidden, local_grad = lax.optimization_barrier((*arrived, hidden, local_grad))
+    got, (hidden, local_grad) = stage(messages[0], messages[1:], z_peers, 2, (hidden, local_grad))
     scale = 1.0 / math.sqrt(row_count * group_size * dom_size // 8)
-    column_w, even_g, odd_g = call(
-        functools.partial(column_body, scale),
-        [(both, BF)] + [((pub_count, width), F32)] * 2,
+    column_w, grads = call(
+        functools.partial(column_body, z_peers, scale),
+        [(both, BF), ((pub_count, width), F32)],
         chip_w,
         own_g,
-        *arrived,
-    )
-    others = [exchange(column_w, dom_size * k, 2 if k % 2 else dom_size) for k in range(1, group_size)]
-    *others, even_g = lax.optimization_barrier((*others, over_core(even_g)))
-    hidden, grad_features = call(features_body, [(wide, BF)] * 2, hidden, place, local_grad, odd_g, even_g)
-    (mine,) = call(sum_body, [(both, F32)], column_w, *others)
-    grad_self, grad_neigh = call(order_body, [(square, F32)] * 2, mine, over_core(mine))
+        *got,
+    )
+    features_out = call(features_body, [(wide, BF)] * 2, hidden, place, local_grad, grads)
+    got, (hidden, grad_features) = stage(
+        column_w, [column_w] * (len(group_peers) // 2), group_peers, dom_size, features_out
+    )
+    grad_self, grad_neigh = call(
+        functools.partial(order_body, group_peers), [(square, F32)] * 2, column_w, *got
+    )
     return hidden, grad_features, grad_self, grad_neigh
 
 

time: 28.8 us -> 27.7 us (0.962)
  waiting for transfers between devices: 9.5 us -> 8.28 us
    ppermute x13 -> x11, waiting for transfers between devices: 9.5 us -> 8.28 us  [exchange(): lax.ppermute(x, ('group', 'dom'), [(a, a ^ (odd_step if a % 2 else even_s...]
    ppermute x13 -> x11, starting transfers between devices: 13 us -> 13 us  [exchange(): lax.ppermute(x, ('group', 'dom'), [(a, a ^ (odd_step if a % 2 else even_s...]
    pallas_call x9 -> x8, Pallas kernels: 4.09 us -> 4.11 us  [call(): pl.pallas_call(body, out_shape=[jax.ShapeDtypeStruct(shape, dtype) for sh...]
  transfers between devices with their start and end apart: 13 -> 11, of which waited for: 9 -> 7; matrix products, arithmetic and copies ran while one was open for 0% -> 0% of each run, Pallas kernels for 9% -> 10%
where the time goes in v7:
time: 27.7 us; the launch traced here: 27.5 us
  starting transfers between devices  13 us (47%)
  waiting for transfers between devices  8.28 us (30%)
  Pallas kernels  5.53 us (20%)
  between operations  0.71 us (3%)
    ppermute x11, starting transfers between devices, exchange(): lax.ppermute(x, ('group', 'dom'), [(a, a ^ (odd_step if a % 2 else even_s...  13 us
    ppermute x11, waiting for transfers between devices, exchange(): lax.ppermute(x, ('group', 'dom'), [(a, a ^ (odd_step if a % 2 else even_s...  8.28 us
    pallas_call x8, Pallas kernels, call(): pl.pallas_call(body, out_shape=[jax.ShapeDtypeStruct(shape, dtype) for sh...  4.11 us
    pallas_call x1, Pallas kernels, local(): pl.pallas_call(functools.partial(publish_body, len(first)), out_shape=[ja...  1.42 us
  transfers between devices with their start and end apart: 11, of which 7 were waited for; matrix products, arithmetic and copies ran while one was open for 0% of the time, Pallas kernels for 10%

profile of v7, /device:TPU:0, one launch (start us, length us, event | category | flops | bytes accessed | tf_op | source)
XLA Modules:
  0.0 27.5 jit_solution(10372091113083874198)
XLA Ops:
  0.6 1.4 %shard_map.129 = (bf16[64,128]{1,0:T(8,128)(2,1)S(1)}, s32[1,64]{1,0:T(1,128)S(1)}, bf16[512,128]{1,0:T(8,128)(2,1)S(1)}, s32[1,512]{1,0:T(1,128)S(1)}, s32[1,25...) custom-call(s32[1,64]{1,0:T(1,128)} %refs_0_.1, ...), custom_call_target="tpu_custom_call" | custom-call | tf_op jit(solution)/shard_map/pallas_call | solution.py:336
  2.1 0.5 %collective-permute-start = (bf16[64,128]{1,0:T(8,128)(2,1)S(1)}, bf16[64,128]{1,0:T(8,128)(2,1)S(1)}, u32[]{:S(2)}, u32[]{:S(2)}) collective-permute-start(bf16[64,128]{1,0:T(8,128)(2,1)S(1)} %get-tuple-element.44.own_ref), channel_id=1, source_target_pairs={{0,1},{1,0},{2,3},{3,2},{4,5},{5,4},{6,7},{7,6},{8,9},{9,8},{10,11... | collective-permute-start | bytes 49160 | tf_op jit(solution)/shard_map/ppermute | solution.py:319
  2.6 0.7 %shard_map.130 = (bf16[512,64]{1,0:T(8,128)(2,1)S(1)}, s32[1,256]{1,0:T(1,128)S(1)}, bf16[64,512]{1,0:T(8,128)(2,1)S(1)}, bf16[64,512]{1,0:T(8,128)(2,1)S(1)}, f32[64,1024]{1,0:T(8,128)S(1)}) custom-call(s32[1,64]{1,0:T(1,128)S(1)} %get-tuple-element.45.pub_ref, bf16[512,128]{1,0:T(8,128)(2,1)S(1)} %get-tuple-element.46.features_ref, ...), custom_call_target="tpu_custom_call" | custom-call | tf_op jit(solution)/shard_map/pallas_call | solution.py:41
  3.3 0.1 collective-permute-done.other_ref
  3.4 0.3 %collective-permute-start.1 = (f32[64,1024]{1,0:T(8,128)S(1)}, f32[64,1024]{1,0:T(8,128)S(1)}, u32[]{:S(2)}, u32[]{:S(2)}) collective-permute-start(f32[64,1024]{1,0:T(8,128)S(1)} %get-tuple-element.54.pack_ref), channel_id=1, source_target_pairs={{0,1},{1,0},{2,3},{3,2},{4,5},{5,4},{6,7},{7,6},{8,9},{9,8},{10,11... | collective-permute-start | bytes 786440 | tf_op jit(solution)/shard_map/ppermute | solution.py:319
  3.8 3.8 %collective-permute-start.3 = (bf16[128,128]{1,0:T(8,128)(2,1)S(1)}, bf16[128,128]{1,0:T(8,128)(2,1)S(1)}, u32[]{:S(2)}, u32[]{:S(2)}) collective-permute-start(bf16[128,128]{1,0:T(8,128)(2,1)S(1)} %shard_map.131.pair_ref), channel_id=1, source_target_pairs={{0,4},{1,7},{2,6},{3,5},{4,0},{5,3},{6,2},{7,1},{8,12},{9,15},{10,... | collective-permute-start | bytes 98312 | tf_op jit(solution)/shard_map/ppermute | solution.py:319
  7.6 0.2 collective-permute-start.2
  7.8 1.8 %collective-permute-done.3.refs_1_ = bf16[128,128]{1,0:T(8,128)(2,1)S(1)} collective-permute-done((bf16[128,128]{1,0:T(8,128)(2,1)S(1)}, bf16[128,128]{1,0:T(8,128)(2,1)S(1)}, u32[]{:S(2)}, u32[]{:S(2)}) %collective-permute-start.3) | collective-permute-done | bytes 32800 | tf_op jit(solution)/shard_map/ppermute | solution.py:319
  9.7 0.3 %collective-permute-start.4 = (bf16[128,128]{1,0:T(8,128)(2,1)S(1)}, bf16[128,128]{1,0:T(8,128)(2,1)S(1)}, u32[]{:S(2)}, u32[]{:S(2)}) collective-permute-start(bf16[128,128]{1,0:T(8,128)(2,1)S(1)} %collective-permute-done.3.refs_1_), channel_id=1, source_target_pairs={{0,1},{1,0},{2,3},{3,2},{4,5},{5,4},{6,7},{7,6},{8,9},{9,8},{10,11... | collective-permute-start | bytes 98312 | tf_op jit(solution)/shard_map/ppermute | solution.py:319
  10.0 1.0 %collective-permute-done.2.refs_0_ = bf16[128,128]{1,0:T(8,128)(2,1)S(1)} collective-permute-done((bf16[128,128]{1,0:T(8,128)(2,1)S(1)}, bf16[128,128]{1,0:T(8,128)(2,1)S(1)}, u32[]{:S(2)}, u32[]{:S(2)}) %collective-permute-start.2) | collective-permute-done | bytes 32800 | tf_op jit(solution)/shard_map/ppermute | solution.py:319
  10.9 0.0 collective-permute-done.4.refs_2_
  11.0 0.0 collective-permute-done.1.got_pack_ref
  11.0 0.6 %shard_map.133 = (bf16[128,128]{1,0:T(8,128)(2,1)S(1)}, bf16[128,128]{1,0:T(8,128)(2,1)S(1)}, f32[128,128]{1,0:T(8,128)S(1)}, bf16[256,128]{1,0:T(8,128)(2,1)S(1...) custom-call(bf16[128,128]{1,0:T(8,128)(2,1)S(1)} %get-tuple-element.42.w_self_ref, ...), custom_call_target="tpu_custom_call" | custom-call | tf_op jit(solution)/shard_map/pallas_call | solution.py:41
  11.6 1.8 %collective-permute-start.6 = (bf16[384,128]{1,0:T(8,128)(2,1)S(1)}, bf16[384,128]{1,0:T(8,128)(2,1)S(1)}, u32[]{:S(2)}, u32[]{:S(2)}) collective-permute-start(bf16[384,128]{1,0:T(8,128)(2,1)S(1)} %get-tuple-element.59), channel_id=1, source_target_pairs={{0,2},{1,5},{2,0},{3,7},{4,6},{5,1},{6,4},{7,3},{8,10},{9,13},{10,... | collective-permute-start | bytes 294920 | tf_op jit(solution)/shard_map/ppermute | solution.py:319
  13.4 2.4 %collective-permute-start.5 = (bf16[384,128]{1,0:T(8,128)(2,1)S(1)}, bf16[384,128]{1,0:T(8,128)(2,1)S(1)}, u32[]{:S(2)}, u32[]{:S(2)}) collective-permute-start(bf16[384,128]{1,0:T(8,128)(2,1)S(1)} %get-tuple-element.58), channel_id=1, source_target_pairs={{0,7},{1,6},{2,5},{3,4},{4,3},{5,2},{6,1},{7,0},{8,15},{9,14},{10,... | collective-permute-start | bytes 294920 | tf_op jit(solution)/shard_map/ppermute | solution.py:319
  15.8 1.1 %shard_map.134 = (bf16[512,128]{1,0:T(8,128)(2,1)S(1)}, f32[512,128]{1,0:T(8,128)S(1)}) custom-call(bf16[512,128]{1,0:T(8,128)(2,1)S(1)} %get-tuple-element.46.features_ref, bf16[512,512]{1,0:T(8,128)(2,1)S(1)} %get-tuple-element.52.local_ref, bf16[512,256]{1,0:T(8,128)(2,1)S(1)} %get-tuple-element.50.bound_ref, s32[1,256]{1,0:T(1,128)S(1)} %get-tuple-element.60.target_ref, ...), custom_call_target="tpu_custom_call" | custom-call | tf_op jit(solution)/shard_map/pallas_call | solution.py:41
  16.9 0.0 collective-permute-done.6.refs_1_
  16.9 1.0 %collective-permute-start.7 = (bf16[384,128]{1,0:T(8,128)(2,1)S(1)}, bf16[384,128]{1,0:T(8,128)(2,1)S(1)}, u32[]{:S(2)}, u32[]{:S(2)}) collective-permute-start(bf16[384,128]{1,0:T(8,128)(2,1)S(1)} %collective-permute-done.6.refs_1_), channel_id=1, source_target_pairs={{0,1},{1,0},{2,3},{3,2},{4,5},{5,4},{6,7},{7,6},{8,9},{9,8},{10,11... | collective-permute-start | bytes 294920 | tf_op jit(solution)/shard_map/ppermute | solution.py:319
  17.9 2.9 %collective-permute-done.5.refs_0_ = bf16[384,128]{1,0:T(8,128)(2,1)S(1)} collective-permute-done((bf16[384,128]{1,0:T(8,128)(2,1)S(1)}, bf16[384,128]{1,0:T(8,128)(2,1)S(1)}, u32[]{:S(2)}, u32[]{:S(2)}) %collective-permute-start.5) | collective-permute-done | bytes 98336 | tf_op jit(solution)/shard_map/ppermute | solution.py:319
  20.8 0.0 collective-permute-done.7.refs_2_
  20.8 0.1 shard_map.135
  20.8 1.6 %collective-permute-start.8 = (bf16[256,128]{1,0:T(8,128)(2,1)S(1)}, bf16[256,128]{1,0:T(8,128)(2,1)S(1)}, u32[]{:S(2)}, u32[]{:S(2)}) collective-permute-start(bf16[256,128]{1,0:T(8,128)(2,1)S(1)} %get-tuple-element.68.own_ref), channel_id=1, source_target_pairs={{0,8},{1,25},{2,10},{3,27},{4,12},{5,29},{6,14},{7,31},{8,0},{9,17... | collective-permute-start | bytes 196616 | tf_op jit(solution)/shard_map/ppermute | solution.py:319
  22.4 1.1 %collective-permute-start.9 = (bf16[256,128]{1,0:T(8,128)(2,1)S(1)}, bf16[256,128]{1,0:T(8,128)(2,1)S(1)}, u32[]{:S(2)}, u32[]{:S(2)}) collective-permute-start(bf16[256,128]{1,0:T(8,128)(2,1)S(1)} %get-tuple-element.68.own_ref), channel_id=1, source_target_pairs={{0,17},{1,16},{2,19},{3,18},{4,21},{5,20},{6,23},{7,22},{8,25},{9,... | collective-permute-start | bytes 196616 | tf_op jit(solution)/shard_map/ppermute | solution.py:319
  23.5 0.9 %shard_map.136 = (bf16[512,128]{1,0:T(8,128)(2,1)}, bf16[512,128]{1,0:T(8,128)(2,1)}) custom-call(bf16[512,128]{1,0:T(8,128)(2,1)S(1)} %get-tuple-element.69.hidden_ref, bf16[512,64]{1,0:T(8,128)(2,1)S(1)} %get-tuple-element.70.place_ref, f32[512,128]{1,0:T(8,128)S(1)} %get-tuple-element.71.local_grad_ref, f32[64,128]{1,0:T(8,128)S(1)} %get-tuple-element.72.grads_ref), custom_call_target="tpu_custom_call" | custom-call | tf_op jit(solution)/shard_map/pallas_call | solution.py:41
  24.3 1.2 %collective-permute-done.8.refs_1_ = bf16[256,128]{1,0:T(8,128)(2,1)S(1)} collective-permute-done((bf16[256,128]{1,0:T(8,128)(2,1)S(1)}, bf16[256,128]{1,0:T(8,128)(2,1)S(1)}, u32[]{:S(2)}, u32[]{:S(2)}) %collective-permute-start.8) | collective-permute-done | bytes 65568 | tf_op jit(solution)/shard_map/ppermute | solution.py:319
  25.6 0.0 collective-permute-start.10
  25.6 0.6 %collective-permute-done.9.refs_0_ = bf16[256,128]{1,0:T(8,128)(2,1)S(1)} collective-permute-done((bf16[256,128]{1,0:T(8,128)(2,1)S(1)}, bf16[256,128]{1,0:T(8,128)(2,1)S(1)}, u32[]{:S(2)}, u32[]{:S(2)}) %collective-permute-start.9) | collective-permute-done | bytes 65568 | tf_op jit(solution)/shard_map/ppermute | solution.py:319
  26.2 0.7 %collective-permute-done.10.refs_2_ = bf16[256,128]{1,0:T(8,128)(2,1)S(1)} collective-permute-done((bf16[256,128]{1,0:T(8,128)(2,1)S(1)}, bf16[256,128]{1,0:T(8,128)(2,1)S(1)}, u32[]{:S(2)}, u32[]{:S(2)}) %collective-permute-start.10) | collective-permute-done | bytes 65568 | tf_op jit(solution)/shard_map/ppermute | solution.py:319
  26.8 0.7 %shard_map.137 = (f32[128,128]{1,0:T(8,128)}, f32[128,128]{1,0:T(8,128)}) custom-call(bf16[256,128]{1,0:T(8,128)(2,1)S(1)} %get-tuple-element.68.own_ref, bf16[256,128]{1,0:T(8,128)(2,1)S(1)} %collective-permute-done.9.refs_0_, bf16[256,128]{1,0:T(8,128)(2,1)S(1)} %collective-permute-done.8.refs_1_, bf16[256,128]{1,0:T(8,128)(2,1)S(1)} %collective-permute-done.10.refs_2_), custom_call_target="tpu_custom_call" | custom-call | tf_op jit(solution)/shard_map/pallas_call | solution.py:41
  (2 shorter events, 0.0 us)
Async XLA Ops:
  2.1 1.4 %collective-permute-start = (bf16[64,128]{1,0:T(8,128)(2,1)S(1)}, bf16[64,128]{1,0:T(8,128)(2,1)S(1)}, u32[]{:S(2)}, u32[]{:S(2)}) collective-permute-start(bf16[64,128]{1,0:T(8,128)(2,1)S(1)} %get-tuple-element.44.own_ref), channel_id=1, source_target_pairs={{0,1},{1,0},{2,3},{3,2},{4,5},{5,4},{6,7},{7,6},{8,9},{9,8},{10,11... | collective-permute-start | bytes 49160 | tf_op jit(solution)/shard_map/ppermute | solution.py:319
  3.4 7.5 %collective-permute-start.1 = (f32[64,1024]{1,0:T(8,128)S(1)}, f32[64,1024]{1,0:T(8,128)S(1)}, u32[]{:S(2)}, u32[]{:S(2)}) collective-permute-start(f32[64,1024]{1,0:T(8,128)S(1)} %get-tuple-element.54.pack_ref), channel_id=1, source_target_pairs={{0,1},{1,0},{2,3},{3,2},{4,5},{5,4},{6,7},{7,6},{8,9},{9,8},{10,11... | collective-permute-start | bytes 786440 | tf_op jit(solution)/shard_map/ppermute | solution.py:319
  3.8 5.9 %collective-permute-start.3 = (bf16[128,128]{1,0:T(8,128)(2,1)S(1)}, bf16[128,128]{1,0:T(8,128)(2,1)S(1)}, u32[]{:S(2)}, u32[]{:S(2)}) collective-permute-start(bf16[128,128]{1,0:T(8,128)(2,1)S(1)} %shard_map.131.pair_ref), channel_id=1, source_target_pairs={{0,4},{1,7},{2,6},{3,5},{4,0},{5,3},{6,2},{7,1},{8,12},{9,15},{10,... | collective-permute-start | bytes 98312 | tf_op jit(solution)/shard_map/ppermute | solution.py:319
  7.6 3.3 %collective-permute-start.2 = (bf16[128,128]{1,0:T(8,128)(2,1)S(1)}, bf16[128,128]{1,0:T(8,128)(2,1)S(1)}, u32[]{:S(2)}, u32[]{:S(2)}) collective-permute-start(bf16[128,128]{1,0:T(8,128)(2,1)S(1)} %shard_map.131.pair_ref), channel_id=1, source_target_pairs={{0,3},{1,2},{2,1},{3,0},{4,7},{5,6},{6,5},{7,4},{8,11},{9,10},{10,... | collective-permute-start | bytes 98312 | tf_op jit(solution)/shard_map/ppermute | solution.py:319
  9.7 1.3 %collective-permute-start.4 = (bf16[128,128]{1,0:T(8,128)(2,1)S(1)}, bf16[128,128]{1,0:T(8,128)(2,1)S(1)}, u32[]{:S(2)}, u32[]{:S(2)}) collective-permute-start(bf16[128,128]{1,0:T(8,128)(2,1)S(1)} %collective-permute-done.3.refs_1_), channel_id=1, source_target_pairs={{0,1},{1,0},{2,3},{3,2},{4,5},{5,4},{6,7},{7,6},{8,9},{9,8},{10,11... | collective-permute-start | bytes 98312 | tf_op jit(solution)/shard_map/ppermute | solution.py:319
  11.6 5.3 %collective-permute-start.6 = (bf16[384,128]{1,0:T(8,128)(2,1)S(1)}, bf16[384,128]{1,0:T(8,128)(2,1)S(1)}, u32[]{:S(2)}, u32[]{:S(2)}) collective-permute-start(bf16[384,128]{1,0:T(8,128)(2,1)S(1)} %get-tuple-element.59), channel_id=1, source_target_pairs={{0,2},{1,5},{2,0},{3,7},{4,6},{5,1},{6,4},{7,3},{8,10},{9,13},{10,... | collective-permute-start | bytes 294920 | tf_op jit(solution)/shard_map/ppermute | solution.py:319
  13.4 7.4 %collective-permute-start.5 = (bf16[384,128]{1,0:T(8,128)(2,1)S(1)}, bf16[384,128]{1,0:T(8,128)(2,1)S(1)}, u32[]{:S(2)}, u32[]{:S(2)}) collective-permute-start(bf16[384,128]{1,0:T(8,128)(2,1)S(1)} %get-tuple-element.58), channel_id=1, source_target_pairs={{0,7},{1,6},{2,5},{3,4},{4,3},{5,2},{6,1},{7,0},{8,15},{9,14},{10,... | collective-permute-start | bytes 294920 | tf_op jit(solution)/shard_map/ppermute | solution.py:319
  16.9 3.8 %collective-permute-start.7 = (bf16[384,128]{1,0:T(8,128)(2,1)S(1)}, bf16[384,128]{1,0:T(8,128)(2,1)S(1)}, u32[]{:S(2)}, u32[]{:S(2)}) collective-permute-start(bf16[384,128]{1,0:T(8,128)(2,1)S(1)} %collective-permute-done.6.refs_1_), channel_id=1, source_target_pairs={{0,1},{1,0},{2,3},{3,2},{4,5},{5,4},{6,7},{7,6},{8,9},{9,8},{10,11... | collective-permute-start | bytes 294920 | tf_op jit(solution)/shard_map/ppermute | solution.py:319
  20.8 4.8 %collective-permute-start.8 = (bf16[256,128]{1,0:T(8,128)(2,1)S(1)}, bf16[256,128]{1,0:T(8,128)(2,1)S(1)}, u32[]{:S(2)}, u32[]{:S(2)}) collective-permute-start(bf16[256,128]{1,0:T(8,128)(2,1)S(1)} %get-tuple-element.68.own_ref), channel_id=1, source_target_pairs={{0,8},{1,25},{2,10},{3,27},{4,12},{5,29},{6,14},{7,31},{8,0},{9,17... | collective-permute-start | bytes 196616 | tf_op jit(solution)/shard_map/ppermute | solution.py:319
  22.4 3.8 %collective-permute-start.9 = (bf16[256,128]{1,0:T(8,128)(2,1)S(1)}, bf16[256,128]{1,0:T(8,128)(2,1)S(1)}, u32[]{:S(2)}, u32[]{:S(2)}) collective-permute-start(bf16[256,128]{1,0:T(8,128)(2,1)S(1)} %get-tuple-element.68.own_ref), channel_id=1, source_target_pairs={{0,17},{1,16},{2,19},{3,18},{4,21},{5,20},{6,23},{7,22},{8,25},{9,... | collective-permute-start | bytes 196616 | tf_op jit(solution)/shard_map/ppermute | solution.py:319
  25.6 1.3 %collective-permute-start.10 = (bf16[256,128]{1,0:T(8,128)(2,1)S(1)}, bf16[256,128]{1,0:T(8,128)(2,1)S(1)}, u32[]{:S(2)}, u32[]{:S(2)}) collective-permute-start(bf16[256,128]{1,0:T(8,128)(2,1)S(1)} %collective-permute-done.8.refs_1_), channel_id=1, source_target_pairs={{0,1},{1,0},{2,3},{3,2},{4,5},{5,4},{6,7},{7,6},{8,9},{9,8},{10,11... | collective-permute-start | bytes 196616 | tf_op jit(solution)/shard_map/ppermute | solution.py:319

commit v8 on v7

--- a/solution.py
+++ b/solution.py
@@ -37,13 +37,14 @@
     return pltpu.with_memory_space_constraint(x, pltpu.HBM)
 
 
-def call(body, outs, *args):
+def call(body, outs, *args, flops=None):
     return pl.pallas_call(
         body,
         out_shape=[jax.ShapeDtypeStruct(shape, dtype) for shape, dtype in outs],
         in_specs=[VMEM] * len(args),
         out_specs=[VMEM] * len(outs),
         compiler_params=PARAMS,
+        cost_estimate=flops and pl.CostEstimate(flops=flops, bytes_accessed=0, transcendentals=0),
     )(*args)
 
 
@@ -215,10 +216,11 @@
     near, *far = peers
     halves = len(far) // 2
     blocks = [grads[z * count : (z + 1) * count] for z in range(1 + len(peers))]
-    blocks = [blocks[near]] + [jnp.where(odd, blocks[a], blocks[b]) for a, b in zip(far[:halves], far[halves:])]
+    to_other = jnp.where(odd, blocks[near][: count // 2], blocks[near][count // 2 :])
+    blocks = [to_other] + [jnp.where(odd, blocks[a], blocks[b]) for a, b in zip(far[:halves], far[halves:])]
     for block, message in zip(blocks, messages):
-        message[:count, :] = block.astype(BF)
-        message[count:, :] = total
+        message[: block.shape[0], :] = block.astype(BF)
+        message[block.shape[0] :, :] = total
 
 
 def rest_body(
@@ -260,16 +262,35 @@
     out_ref[...] = dot_nt(spread, w_self_ref[...]) + dot_t(near_ref[...], grad_agg)
 
 
-def column_body(peers, scale, total_ref, own_ref, *refs):
+def near_body(total_ref, own_ref, got_ref, sum_ref, grads_ref):
+    rows = own_ref.shape[0] // 2
+    odd = odd_core()
+    sum_ref[...] = total_ref[...].astype(F32) + got_ref[rows:, :].astype(F32)
+    own = jnp.where(odd, own_ref[rows:, :], own_ref[:rows, :])
+    grads_ref[...] = own + got_ref[:rows, :].astype(F32)
+
+
+def span(size, first):
+    out = [0]
+    for k in [first, *range(1, size)]:
+        if k not in out:
+            out += [j ^ k for j in out]
+    return out
+
+
+def column_body(peers, scale, sum_ref, near_ref, *refs):
     refs, (out_ref, grads_ref) = refs[:-2], refs[-2:]
-    rows = own_ref.shape[0]
-    messages = by_peer(peers, None, refs)[1:]
-    total = tree_sum([part.astype(F32) for part in [total_ref[...]] + [x[rows:] for x in messages]])
+    rows = near_ref.shape[0]
+    near, *far = peers
+    messages = dict(zip(far, either(refs[: len(far) // 2], refs[len(far) // 2 :])))
+    messages = [messages[k] for k in span(1 + len(peers), near)[2:]]
+    parts = [message[2 * rows :].astype(F32) for message in messages]
+    total = tree_sum([sum_ref[...]] + [x + y for x, y in zip(parts[::2], parts[1::2])])
     out_ref[...] = (total * scale).astype(BF)
-    grads = own_ref[...]
+    grads = near_ref[...]
     for message in messages:
-        grads = grads + message[:rows].astype(F32)
-    grads_ref[...] = jnp.where(odd_core(), grads[rows // 2 :], grads[: rows // 2])
+        grads = grads + jnp.where(odd_core(), message[rows : 2 * rows], message[:rows]).astype(F32)
+    grads_ref[...] = grads
 
 
 def features_body(hidden_ref, place_ref, local_grad_ref, grads_ref, hidden_out, out_ref):
@@ -375,7 +396,7 @@
     (rows,) = call(functools.partial(rows_body, c_peers), [((columns, width), BF)], pair, *got)
     grad_pre, grad_agg, own_g, chip_w, *messages = call(
         functools.partial(target_body, z_peers),
-        [((2 * hits, width), BF)] * 2 + [((2 * pub_count, width), F32), (both, BF)] + [message] * (1 + len(z_peers) // 2),
+        [((2 * hits, width), BF)] * 2 + [((2 * pub_count, width), F32), (both, BF)] + [((pub_count + 2 * width, width), BF)] + [message] * (len(z_peers) // 2),
         w_self,
         w_neigh,
         pack,
@@ -399,12 +420,15 @@
     )
     got, (hidden, local_grad) = stage(messages[0], messages[1:], z_peers, 2, (hidden, local_grad))
     scale = 1.0 / math.sqrt(row_count * group_size * dom_size // 8)
+    near_w, near_g = call(
+        near_body, [(both, F32), ((pub_count, width), F32)], chip_w, own_g, got[0], flops=2 * 10**9
+    )
     column_w, grads = call(
         functools.partial(column_body, z_peers, scale),
         [(both, BF), ((pub_count, width), F32)],
-        chip_w,
-        own_g,
-        *got,
+        near_w,
+        near_g,
+        *got[1:],
     )
     features_out = call(features_body, [(wide, BF)] * 2, hidden, place, local_grad, grads)
     got, (hidden, grad_features) = stage(

time: 27.7 us -> 27.3 us (0.986)
  waiting for transfers between devices: 8.28 us -> 7.93 us
    ppermute x11, waiting for transfers between devices: 8.28 us -> 7.93 us  [exchange(): lax.ppermute(x, ('group', 'dom'), [(a, a ^ (odd_step if a % 2 else even_s...]
    pallas_call x8 -> x9, Pallas kernels: 4.11 us -> 4.12 us  [call(): pl.pallas_call(body, out_shape=[jax.ShapeDtypeStruct(shape, dtype) for sh...]
where the time goes in v8:
time: 27.3 us; the launch traced here: 27.2 us
  starting transfers between devices  13 us (48%)
  waiting for transfers between devices  7.93 us (29%)
  Pallas kernels  5.53 us (20%)
  between operations  0.72 us (3%)
    ppermute x11, starting transfers between devices, exchange(): lax.ppermute(x, ('group', 'dom'), [(a, a ^ (odd_step if a % 2 else even_s...  13 us
    ppermute x11, waiting for transfers between devices, exchange(): lax.ppermute(x, ('group', 'dom'), [(a, a ^ (odd_step if a % 2 else even_s...  7.93 us
    pallas_call x9, Pallas kernels, call(): pl.pallas_call(body, out_shape=[jax.ShapeDtypeStruct(shape, dtype) for sh...  4.12 us
    pallas_call x1, Pallas kernels, local(): pl.pallas_call(functools.partial(publish_body, len(first)), out_shape=[ja...  1.42 us
  transfers between devices with their start and end apart: 11, of which 7 were waited for; matrix products, arithmetic and copies ran while one was open for 0% of the time, Pallas kernels for 10%

profile of v8, /device:TPU:0, one launch (start us, length us, event | category | flops | bytes accessed | tf_op | source)
XLA Modules:
  0.0 27.2 jit_solution(13015810756079528622)
XLA Ops:
  0.6 1.4 %shard_map.129 = (bf16[64,128]{1,0:T(8,128)(2,1)S(1)}, s32[1,64]{1,0:T(1,128)S(1)}, bf16[512,128]{1,0:T(8,128)(2,1)S(1)}, s32[1,512]{1,0:T(1,128)S(1)}, s32[1,25...) custom-call(s32[1,64]{1,0:T(1,128)} %refs_0_.1, ...), custom_call_target="tpu_custom_call" | custom-call | tf_op jit(solution)/shard_map/pallas_call | solution.py:357
  2.1 0.5 %collective-permute-start = (bf16[64,128]{1,0:T(8,128)(2,1)S(1)}, bf16[64,128]{1,0:T(8,128)(2,1)S(1)}, u32[]{:S(2)}, u32[]{:S(2)}) collective-permute-start(bf16[64,128]{1,0:T(8,128)(2,1)S(1)} %get-tuple-element.46.own_ref), channel_id=1, source_target_pairs={{0,1},{1,0},{2,3},{3,2},{4,5},{5,4},{6,7},{7,6},{8,9},{9,8},{10,11... | collective-permute-start | bytes 49160 | tf_op jit(solution)/shard_map/ppermute | solution.py:340
  2.6 0.7 %shard_map.130 = (bf16[512,64]{1,0:T(8,128)(2,1)S(1)}, s32[1,256]{1,0:T(1,128)S(1)}, bf16[64,512]{1,0:T(8,128)(2,1)S(1)}, bf16[64,512]{1,0:T(8,128)(2,1)S(1)}, f32[64,1024]{1,0:T(8,128)S(1)}) custom-call(s32[1,64]{1,0:T(1,128)S(1)} %get-tuple-element.47.pub_ref, bf16[512,128]{1,0:T(8,128)(2,1)S(1)} %get-tuple-element.48.features_ref, ...), custom_call_target="tpu_custom_call" | custom-call | tf_op jit(solution)/shard_map/pallas_call | solution.py:41
  3.3 0.1 collective-permute-done.other_ref
  3.4 0.3 %collective-permute-start.1 = (f32[64,1024]{1,0:T(8,128)S(1)}, f32[64,1024]{1,0:T(8,128)S(1)}, u32[]{:S(2)}, u32[]{:S(2)}) collective-permute-start(f32[64,1024]{1,0:T(8,128)S(1)} %get-tuple-element.56.pack_ref), channel_id=1, source_target_pairs={{0,1},{1,0},{2,3},{3,2},{4,5},{5,4},{6,7},{7,6},{8,9},{9,8},{10,11... | collective-permute-start | bytes 786440 | tf_op jit(solution)/shard_map/ppermute | solution.py:340
  3.8 3.8 %collective-permute-start.3 = (bf16[128,128]{1,0:T(8,128)(2,1)S(1)}, bf16[128,128]{1,0:T(8,128)(2,1)S(1)}, u32[]{:S(2)}, u32[]{:S(2)}) collective-permute-start(bf16[128,128]{1,0:T(8,128)(2,1)S(1)} %shard_map.131.pair_ref), channel_id=1, source_target_pairs={{0,4},{1,7},{2,6},{3,5},{4,0},{5,3},{6,2},{7,1},{8,12},{9,15},{10,... | collective-permute-start | bytes 98312 | tf_op jit(solution)/shard_map/ppermute | solution.py:340
  7.6 0.2 collective-permute-start.2
  7.8 1.8 %collective-permute-done.3.refs_1_ = bf16[128,128]{1,0:T(8,128)(2,1)S(1)} collective-permute-done((bf16[128,128]{1,0:T(8,128)(2,1)S(1)}, bf16[128,128]{1,0:T(8,128)(2,1)S(1)}, u32[]{:S(2)}, u32[]{:S(2)}) %collective-permute-start.3) | collective-permute-done | bytes 32800 | tf_op jit(solution)/shard_map/ppermute | solution.py:340
  9.7 0.3 %collective-permute-start.4 = (bf16[128,128]{1,0:T(8,128)(2,1)S(1)}, bf16[128,128]{1,0:T(8,128)(2,1)S(1)}, u32[]{:S(2)}, u32[]{:S(2)}) collective-permute-start(bf16[128,128]{1,0:T(8,128)(2,1)S(1)} %collective-permute-done.3.refs_1_), channel_id=1, source_target_pairs={{0,1},{1,0},{2,3},{3,2},{4,5},{5,4},{6,7},{7,6},{8,9},{9,8},{10,11... | collective-permute-start | bytes 98312 | tf_op jit(solution)/shard_map/ppermute | solution.py:340
  10.0 1.0 %collective-permute-done.2.refs_0_ = bf16[128,128]{1,0:T(8,128)(2,1)S(1)} collective-permute-done((bf16[128,128]{1,0:T(8,128)(2,1)S(1)}, bf16[128,128]{1,0:T(8,128)(2,1)S(1)}, u32[]{:S(2)}, u32[]{:S(2)}) %collective-permute-start.2) | collective-permute-done | bytes 32800 | tf_op jit(solution)/shard_map/ppermute | solution.py:340
  10.9 0.0 collective-permute-done.4.refs_2_
  11.0 0.0 collective-permute-done.1.got_pack_ref
  11.0 0.6 %shard_map.133 = (bf16[128,128]{1,0:T(8,128)(2,1)S(1)}, bf16[128,128]{1,0:T(8,128)(2,1)S(1)}, f32[128,128]{1,0:T(8,128)S(1)}, bf16[256,128]{1,0:T(8,128)(2,1)S(1...) custom-call(bf16[128,128]{1,0:T(8,128)(2,1)S(1)} %get-tuple-element.44.w_self_ref, ...), custom_call_target="tpu_custom_call" | custom-call | tf_op jit(solution)/shard_map/pallas_call | solution.py:41
  11.6 1.8 %collective-permute-start.6 = (bf16[384,128]{1,0:T(8,128)(2,1)S(1)}, bf16[384,128]{1,0:T(8,128)(2,1)S(1)}, u32[]{:S(2)}, u32[]{:S(2)}) collective-permute-start(bf16[384,128]{1,0:T(8,128)(2,1)S(1)} %get-tuple-element.63), channel_id=1, source_target_pairs={{0,2},{1,5},{2,0},{3,7},{4,6},{5,1},{6,4},{7,3},{8,10},{9,13},{10,... | collective-permute-start | bytes 294920 | tf_op jit(solution)/shard_map/ppermute | solution.py:340
  13.4 2.4 %collective-permute-start.5 = (bf16[320,128]{1,0:T(8,128)(2,1)S(1)}, bf16[320,128]{1,0:T(8,128)(2,1)S(1)}, u32[]{:S(2)}, u32[]{:S(2)}) collective-permute-start(bf16[320,128]{1,0:T(8,128)(2,1)S(1)} %get-tuple-element.60), channel_id=1, source_target_pairs={{0,7},{1,6},{2,5},{3,4},{4,3},{5,2},{6,1},{7,0},{8,15},{9,14},{10,... | collective-permute-start | bytes 245768 | tf_op jit(solution)/shard_map/ppermute | solution.py:340
  15.8 1.1 %shard_map.135 = (bf16[512,128]{1,0:T(8,128)(2,1)S(1)}, f32[512,128]{1,0:T(8,128)S(1)}) custom-call(bf16[512,128]{1,0:T(8,128)(2,1)S(1)} %get-tuple-element.48.features_ref, bf16[512,512]{1,0:T(8,128)(2,1)S(1)} %get-tuple-element.54.local_ref, bf16[512,256]{1,0:T(8,128)(2,1)S(1)} %get-tuple-element.52.bound_ref, s32[1,256]{1,0:T(1,128)S(1)} %get-tuple-element.64.target_ref, ...), custom_call_target="tpu_custom_call" | custom-call | tf_op jit(solution)/shard_map/pallas_call | solution.py:41
  16.9 0.0 collective-permute-done.6.refs_0_
  16.9 1.0 %collective-permute-start.7 = (bf16[384,128]{1,0:T(8,128)(2,1)S(1)}, bf16[384,128]{1,0:T(8,128)(2,1)S(1)}, u32[]{:S(2)}, u32[]{:S(2)}) collective-permute-start(bf16[384,128]{1,0:T(8,128)(2,1)S(1)} %collective-permute-done.6.refs_0_), channel_id=1, source_target_pairs={{0,1},{1,0},{2,3},{3,2},{4,5},{5,4},{6,7},{7,6},{8,9},{9,8},{10,11... | collective-permute-start | bytes 294920 | tf_op jit(solution)/shard_map/ppermute | solution.py:340
  17.9 2.5 %collective-permute-done.5.got_ref = bf16[320,128]{1,0:T(8,128)(2,1)S(1)} collective-permute-done((bf16[320,128]{1,0:T(8,128)(2,1)S(1)}, bf16[320,128]{1,0:T(8,128)(2,1)S(1)}, u32[]{:S(2)}, u32[]{:S(2)}) %collective-permute-start.5) | collective-permute-done | bytes 81952 | tf_op jit(solution)/shard_map/ppermute | solution.py:340
  20.4 0.0 collective-permute-done.7.refs_1_
  20.4 0.1 shard_map.136
  20.5 1.6 %collective-permute-start.8 = (bf16[256,128]{1,0:T(8,128)(2,1)S(1)}, bf16[256,128]{1,0:T(8,128)(2,1)S(1)}, u32[]{:S(2)}, u32[]{:S(2)}) collective-permute-start(bf16[256,128]{1,0:T(8,128)(2,1)S(1)} %get-tuple-element.72.own_ref), channel_id=1, source_target_pairs={{0,8},{1,25},{2,10},{3,27},{4,12},{5,29},{6,14},{7,31},{8,0},{9,17... | collective-permute-start | bytes 196616 | tf_op jit(solution)/shard_map/ppermute | solution.py:340
  22.1 1.1 %collective-permute-start.9 = (bf16[256,128]{1,0:T(8,128)(2,1)S(1)}, bf16[256,128]{1,0:T(8,128)(2,1)S(1)}, u32[]{:S(2)}, u32[]{:S(2)}) collective-permute-start(bf16[256,128]{1,0:T(8,128)(2,1)S(1)} %get-tuple-element.72.own_ref), channel_id=1, source_target_pairs={{0,17},{1,16},{2,19},{3,18},{4,21},{5,20},{6,23},{7,22},{8,25},{9,... | collective-permute-start | bytes 196616 | tf_op jit(solution)/shard_map/ppermute | solution.py:340
  23.1 0.9 %shard_map.137 = (bf16[512,128]{1,0:T(8,128)(2,1)}, bf16[512,128]{1,0:T(8,128)(2,1)}) custom-call(bf16[512,128]{1,0:T(8,128)(2,1)S(1)} %get-tuple-element.73.hidden_ref, bf16[512,64]{1,0:T(8,128)(2,1)S(1)} %get-tuple-element.74.place_ref, f32[512,128]{1,0:T(8,128)S(1)} %get-tuple-element.75.local_grad_ref, f32[64,128]{1,0:T(8,128)S(1)} %get-tuple-element.76.grads_ref), custom_call_target="tpu_custom_call" | custom-call | tf_op jit(solution)/shard_map/pallas_call | solution.py:41
  24.0 1.2 %collective-permute-done.8.refs_1_ = bf16[256,128]{1,0:T(8,128)(2,1)S(1)} collective-permute-done((bf16[256,128]{1,0:T(8,128)(2,1)S(1)}, bf16[256,128]{1,0:T(8,128)(2,1)S(1)}, u32[]{:S(2)}, u32[]{:S(2)}) %collective-permute-start.8) | collective-permute-done | bytes 65568 | tf_op jit(solution)/shard_map/ppermute | solution.py:340
  25.3 0.0 collective-permute-start.10
  25.3 0.6 %collective-permute-done.9.refs_0_ = bf16[256,128]{1,0:T(8,128)(2,1)S(1)} collective-permute-done((bf16[256,128]{1,0:T(8,128)(2,1)S(1)}, bf16[256,128]{1,0:T(8,128)(2,1)S(1)}, u32[]{:S(2)}, u32[]{:S(2)}) %collective-permute-start.9) | collective-permute-done | bytes 65568 | tf_op jit(solution)/shard_map/ppermute | solution.py:340
  25.9 0.7 %collective-permute-done.10.refs_2_ = bf16[256,128]{1,0:T(8,128)(2,1)S(1)} collective-permute-done((bf16[256,128]{1,0:T(8,128)(2,1)S(1)}, bf16[256,128]{1,0:T(8,128)(2,1)S(1)}, u32[]{:S(2)}, u32[]{:S(2)}) %collective-permute-start.10) | collective-permute-done | bytes 65568 | tf_op jit(solution)/shard_map/ppermute | solution.py:340
  26.5 0.7 %shard_map.138 = (f32[128,128]{1,0:T(8,128)}, f32[128,128]{1,0:T(8,128)}) custom-call(bf16[256,128]{1,0:T(8,128)(2,1)S(1)} %get-tuple-element.72.own_ref, bf16[256,128]{1,0:T(8,128)(2,1)S(1)} %collective-permute-done.9.refs_0_, bf16[256,128]{1,0:T(8,128)(2,1)S(1)} %collective-permute-done.8.refs_1_, bf16[256,128]{1,0:T(8,128)(2,1)S(1)} %collective-permute-done.10.refs_2_), custom_call_target="tpu_custom_call" | custom-call | tf_op jit(solution)/shard_map/pallas_call | solution.py:41
  (3 shorter events, 0.1 us)
Async XLA Ops:
  2.1 1.4 %collective-permute-start = (bf16[64,128]{1,0:T(8,128)(2,1)S(1)}, bf16[64,128]{1,0:T(8,128)(2,1)S(1)}, u32[]{:S(2)}, u32[]{:S(2)}) collective-permute-start(bf16[64,128]{1,0:T(8,128)(2,1)S(1)} %get-tuple-element.46.own_ref), channel_id=1, source_target_pairs={{0,1},{1,0},{2,3},{3,2},{4,5},{5,4},{6,7},{7,6},{8,9},{9,8},{10,11... | collective-permute-start | bytes 49160 | tf_op jit(solution)/shard_map/ppermute | solution.py:340
  3.4 7.5 %collective-permute-start.1 = (f32[64,1024]{1,0:T(8,128)S(1)}, f32[64,1024]{1,0:T(8,128)S(1)}, u32[]{:S(2)}, u32[]{:S(2)}) collective-permute-start(f32[64,1024]{1,0:T(8,128)S(1)} %get-tuple-element.56.pack_ref), channel_id=1, source_target_pairs={{0,1},{1,0},{2,3},{3,2},{4,5},{5,4},{6,7},{7,6},{8,9},{9,8},{10,11... | collective-permute-start | bytes 786440 | tf_op jit(solution)/shard_map/ppermute | solution.py:340
  3.8 5.9 %collective-permute-start.3 = (bf16[128,128]{1,0:T(8,128)(2,1)S(1)}, bf16[128,128]{1,0:T(8,128)(2,1)S(1)}, u32[]{:S(2)}, u32[]{:S(2)}) collective-permute-start(bf16[128,128]{1,0:T(8,128)(2,1)S(1)} %shard_map.131.pair_ref), channel_id=1, source_target_pairs={{0,4},{1,7},{2,6},{3,5},{4,0},{5,3},{6,2},{7,1},{8,12},{9,15},{10,... | collective-permute-start | bytes 98312 | tf_op jit(solution)/shard_map/ppermute | solution.py:340
  7.6 3.3 %collective-permute-start.2 = (bf16[128,128]{1,0:T(8,128)(2,1)S(1)}, bf16[128,128]{1,0:T(8,128)(2,1)S(1)}, u32[]{:S(2)}, u32[]{:S(2)}) collective-permute-start(bf16[128,128]{1,0:T(8,128)(2,1)S(1)} %shard_map.131.pair_ref), channel_id=1, source_target_pairs={{0,3},{1,2},{2,1},{3,0},{4,7},{5,6},{6,5},{7,4},{8,11},{9,10},{10,... | collective-permute-start | bytes 98312 | tf_op jit(solution)/shard_map/ppermute | solution.py:340
  9.7 1.3 %collective-permute-start.4 = (bf16[128,128]{1,0:T(8,128)(2,1)S(1)}, bf16[128,128]{1,0:T(8,128)(2,1)S(1)}, u32[]{:S(2)}, u32[]{:S(2)}) collective-permute-start(bf16[128,128]{1,0:T(8,128)(2,1)S(1)} %collective-permute-done.3.refs_1_), channel_id=1, source_target_pairs={{0,1},{1,0},{2,3},{3,2},{4,5},{5,4},{6,7},{7,6},{8,9},{9,8},{10,11... | collective-permute-start | bytes 98312 | tf_op jit(solution)/shard_map/ppermute | solution.py:340
  11.6 5.3 %collective-permute-start.6 = (bf16[384,128]{1,0:T(8,128)(2,1)S(1)}, bf16[384,128]{1,0:T(8,128)(2,1)S(1)}, u32[]{:S(2)}, u32[]{:S(2)}) collective-permute-start(bf16[384,128]{1,0:T(8,128)(2,1)S(1)} %get-tuple-element.63), channel_id=1, source_target_pairs={{0,2},{1,5},{2,0},{3,7},{4,6},{5,1},{6,4},{7,3},{8,10},{9,13},{10,... | collective-permute-start | bytes 294920 | tf_op jit(solution)/shard_map/ppermute | solution.py:340
  13.4 7.0 %collective-permute-start.5 = (bf16[320,128]{1,0:T(8,128)(2,1)S(1)}, bf16[320,128]{1,0:T(8,128)(2,1)S(1)}, u32[]{:S(2)}, u32[]{:S(2)}) collective-permute-start(bf16[320,128]{1,0:T(8,128)(2,1)S(1)} %get-tuple-element.60), channel_id=1, source_target_pairs={{0,7},{1,6},{2,5},{3,4},{4,3},{5,2},{6,1},{7,0},{8,15},{9,14},{10,... | collective-permute-start | bytes 245768 | tf_op jit(solution)/shard_map/ppermute | solution.py:340
  16.9 3.5 %collective-permute-start.7 = (bf16[384,128]{1,0:T(8,128)(2,1)S(1)}, bf16[384,128]{1,0:T(8,128)(2,1)S(1)}, u32[]{:S(2)}, u32[]{:S(2)}) collective-permute-start(bf16[384,128]{1,0:T(8,128)(2,1)S(1)} %collective-permute-done.6.refs_0_), channel_id=1, source_target_pairs={{0,1},{1,0},{2,3},{3,2},{4,5},{5,4},{6,7},{7,6},{8,9},{9,8},{10,11... | collective-permute-start | bytes 294920 | tf_op jit(solution)/shard_map/ppermute | solution.py:340
  20.5 4.8 %collective-permute-start.8 = (bf16[256,128]{1,0:T(8,128)(2,1)S(1)}, bf16[256,128]{1,0:T(8,128)(2,1)S(1)}, u32[]{:S(2)}, u32[]{:S(2)}) collective-permute-start(bf16[256,128]{1,0:T(8,128)(2,1)S(1)} %get-tuple-element.72.own_ref), channel_id=1, source_target_pairs={{0,8},{1,25},{2,10},{3,27},{4,12},{5,29},{6,14},{7,31},{8,0},{9,17... | collective-permute-start | bytes 196616 | tf_op jit(solution)/shard_map/ppermute | solution.py:340
  22.1 3.8 %collective-permute-start.9 = (bf16[256,128]{1,0:T(8,128)(2,1)S(1)}, bf16[256,128]{1,0:T(8,128)(2,1)S(1)}, u32[]{:S(2)}, u32[]{:S(2)}) collective-permute-start(bf16[256,128]{1,0:T(8,128)(2,1)S(1)} %get-tuple-element.72.own_ref), channel_id=1, source_target_pairs={{0,17},{1,16},{2,19},{3,18},{4,21},{5,20},{6,23},{7,22},{8,25},{9,... | collective-permute-start | bytes 196616 | tf_op jit(solution)/shard_map/ppermute | solution.py:340
  25.3 1.3 %collective-permute-start.10 = (bf16[256,128]{1,0:T(8,128)(2,1)S(1)}, bf16[256,128]{1,0:T(8,128)(2,1)S(1)}, u32[]{:S(2)}, u32[]{:S(2)}) collective-permute-start(bf16[256,128]{1,0:T(8,128)(2,1)S(1)} %collective-permute-done.8.refs_1_), channel_id=1, source_target_pairs={{0,1},{1,0},{2,3},{3,2},{4,5},{5,4},{6,7},{7,6},{8,9},{9,8},{10,11... | collective-permute-start | bytes 196616 | tf_op jit(solution)/shard_map/ppermute | solution.py:340

commit v9 on v8

--- a/solution.py
+++ b/solution.py
@@ -430,10 +430,8 @@
         near_g,
         *got[1:],
     )
-    features_out = call(features_body, [(wide, BF)] * 2, hidden, place, local_grad, grads)
-    got, (hidden, grad_features) = stage(
-        column_w, [column_w] * (len(group_peers) // 2), group_peers, dom_size, features_out
-    )
+    hidden, grad_features = call(features_body, [(wide, BF)] * 2, hidden, place, local_grad, grads)
+    got, _ = stage(column_w, [column_w] * (len(group_peers) // 2), group_peers, dom_size)
     grad_self, grad_neigh = call(
         functools.partial(order_body, group_peers), [(square, F32)] * 2, column_w, *got
     )

time: 27.3 us -> 27.3 us (level)
  transfers between devices with their start and end apart: 11 -> 11, of which waited for: 7 -> 6; matrix products, arithmetic and copies ran while one was open for 0% -> 0% of each run, Pallas kernels for 10% -> 10%
where the time goes in v9:
time: 27.3 us; the launch traced here: 27.2 us
  starting transfers between devices  13 us (48%)
  waiting for transfers between devices  7.93 us (29%)
  Pallas kernels  5.53 us (20%)
  between operations  0.72 us (3%)
    ppermute x11, starting transfers between devices, exchange(): lax.ppermute(x, ('group', 'dom'), [(a, a ^ (odd_step if a % 2 else even_s...  13 us
    ppermute x11, waiting for transfers between devices, exchange(): lax.ppermute(x, ('group', 'dom'), [(a, a ^ (odd_step if a % 2 else even_s...  7.93 us
    pallas_call x9, Pallas kernels, call(): pl.pallas_call(body, out_shape=[jax.ShapeDtypeStruct(shape, dtype) for sh...  4.12 us
    pallas_call x1, Pallas kernels, local(): pl.pallas_call(functools.partial(publish_body, len(first)), out_shape=[ja...  1.42 us
  transfers between devices with their start and end apart: 11, of which 6 were waited for; matrix products, arithmetic and copies ran while one was open for 0% of the time, Pallas kernels for 10%

profile of v9, /device:TPU:0, one launch (start us, length us, event | category | flops | bytes accessed | tf_op | source)
XLA Modules:
  0.0 27.2 jit_solution(16045493482880113288)
XLA Ops:
  0.6 1.4 %shard_map.129 = (bf16[64,128]{1,0:T(8,128)(2,1)S(1)}, s32[1,64]{1,0:T(1,128)S(1)}, bf16[512,128]{1,0:T(8,128)(2,1)S(1)}, s32[1,512]{1,0:T(1,128)S(1)}, s32[1,25...) custom-call(s32[1,64]{1,0:T(1,128)} %refs_0_.1, ...), custom_call_target="tpu_custom_call" | custom-call | tf_op jit(solution)/shard_map/pallas_call | solution.py:357
  2.1 0.5 %collective-permute-start = (bf16[64,128]{1,0:T(8,128)(2,1)S(1)}, bf16[64,128]{1,0:T(8,128)(2,1)S(1)}, u32[]{:S(2)}, u32[]{:S(2)}) collective-permute-start(bf16[64,128]{1,0:T(8,128)(2,1)S(1)} %get-tuple-element.43.own_ref), channel_id=1, source_target_pairs={{0,1},{1,0},{2,3},{3,2},{4,5},{5,4},{6,7},{7,6},{8,9},{9,8},{10,11... | collective-permute-start | bytes 49160 | tf_op jit(solution)/shard_map/ppermute | solution.py:340
  2.6 0.7 %shard_map.130 = (bf16[512,64]{1,0:T(8,128)(2,1)S(1)}, s32[1,256]{1,0:T(1,128)S(1)}, bf16[64,512]{1,0:T(8,128)(2,1)S(1)}, bf16[64,512]{1,0:T(8,128)(2,1)S(1)}, f32[64,1024]{1,0:T(8,128)S(1)}) custom-call(s32[1,64]{1,0:T(1,128)S(1)} %get-tuple-element.44.pub_ref, bf16[512,128]{1,0:T(8,128)(2,1)S(1)} %get-tuple-element.45.features_ref, ...), custom_call_target="tpu_custom_call" | custom-call | tf_op jit(solution)/shard_map/pallas_call | solution.py:41
  3.3 0.1 collective-permute-done.other_ref
  3.4 0.3 %collective-permute-start.1 = (f32[64,1024]{1,0:T(8,128)S(1)}, f32[64,1024]{1,0:T(8,128)S(1)}, u32[]{:S(2)}, u32[]{:S(2)}) collective-permute-start(f32[64,1024]{1,0:T(8,128)S(1)} %get-tuple-element.53.pack_ref), channel_id=1, source_target_pairs={{0,1},{1,0},{2,3},{3,2},{4,5},{5,4},{6,7},{7,6},{8,9},{9,8},{10,11... | collective-permute-start | bytes 786440 | tf_op jit(solution)/shard_map/ppermute | solution.py:340
  3.8 3.8 %collective-permute-start.3 = (bf16[128,128]{1,0:T(8,128)(2,1)S(1)}, bf16[128,128]{1,0:T(8,128)(2,1)S(1)}, u32[]{:S(2)}, u32[]{:S(2)}) collective-permute-start(bf16[128,128]{1,0:T(8,128)(2,1)S(1)} %shard_map.131.pair_ref), channel_id=1, source_target_pairs={{0,4},{1,7},{2,6},{3,5},{4,0},{5,3},{6,2},{7,1},{8,12},{9,15},{10,... | collective-permute-start | bytes 98312 | tf_op jit(solution)/shard_map/ppermute | solution.py:340
  7.6 0.2 collective-permute-start.2
  7.8 1.8 %collective-permute-done.3.refs_1_ = bf16[128,128]{1,0:T(8,128)(2,1)S(1)} collective-permute-done((bf16[128,128]{1,0:T(8,128)(2,1)S(1)}, bf16[128,128]{1,0:T(8,128)(2,1)S(1)}, u32[]{:S(2)}, u32[]{:S(2)}) %collective-permute-start.3) | collective-permute-done | bytes 32800 | tf_op jit(solution)/shard_map/ppermute | solution.py:340
  9.7 0.3 %collective-permute-start.4 = (bf16[128,128]{1,0:T(8,128)(2,1)S(1)}, bf16[128,128]{1,0:T(8,128)(2,1)S(1)}, u32[]{:S(2)}, u32[]{:S(2)}) collective-permute-start(bf16[128,128]{1,0:T(8,128)(2,1)S(1)} %collective-permute-done.3.refs_1_), channel_id=1, source_target_pairs={{0,1},{1,0},{2,3},{3,2},{4,5},{5,4},{6,7},{7,6},{8,9},{9,8},{10,11... | collective-permute-start | bytes 98312 | tf_op jit(solution)/shard_map/ppermute | solution.py:340
  10.0 1.0 %collective-permute-done.2.refs_0_ = bf16[128,128]{1,0:T(8,128)(2,1)S(1)} collective-permute-done((bf16[128,128]{1,0:T(8,128)(2,1)S(1)}, bf16[128,128]{1,0:T(8,128)(2,1)S(1)}, u32[]{:S(2)}, u32[]{:S(2)}) %collective-permute-start.2) | collective-permute-done | bytes 32800 | tf_op jit(solution)/shard_map/ppermute | solution.py:340
  10.9 0.0 collective-permute-done.4.refs_2_
  11.0 0.0 collective-permute-done.1.got_pack_ref
  11.0 0.6 %shard_map.133 = (bf16[128,128]{1,0:T(8,128)(2,1)S(1)}, bf16[128,128]{1,0:T(8,128)(2,1)S(1)}, f32[128,128]{1,0:T(8,128)S(1)}, bf16[256,128]{1,0:T(8,128)(2,1)S(1...) custom-call(bf16[128,128]{1,0:T(8,128)(2,1)S(1)} %get-tuple-element.41.w_self_ref, ...), custom_call_target="tpu_custom_call" | custom-call | tf_op jit(solution)/shard_map/pallas_call | solution.py:41
  11.6 1.8 %collective-permute-start.5 = (bf16[384,128]{1,0:T(8,128)(2,1)S(1)}, bf16[384,128]{1,0:T(8,128)(2,1)S(1)}, u32[]{:S(2)}, u32[]{:S(2)}) collective-permute-start(bf16[384,128]{1,0:T(8,128)(2,1)S(1)} %get-tuple-element.55), channel_id=1, source_target_pairs={{0,2},{1,5},{2,0},{3,7},{4,6},{5,1},{6,4},{7,3},{8,10},{9,13},{10,... | collective-permute-start | bytes 294920 | tf_op jit(solution)/shard_map/ppermute | solution.py:340
  13.4 2.4 %collective-permute-start.6 = (bf16[320,128]{1,0:T(8,128)(2,1)S(1)}, bf16[320,128]{1,0:T(8,128)(2,1)S(1)}, u32[]{:S(2)}, u32[]{:S(2)}) collective-permute-start(bf16[320,128]{1,0:T(8,128)(2,1)S(1)} %get-tuple-element.68), channel_id=1, source_target_pairs={{0,7},{1,6},{2,5},{3,4},{4,3},{5,2},{6,1},{7,0},{8,15},{9,14},{10,... | collective-permute-start | bytes 245768 | tf_op jit(solution)/shard_map/ppermute | solution.py:340
  15.8 1.1 %shard_map.134 = (bf16[512,128]{1,0:T(8,128)(2,1)S(1)}, f32[512,128]{1,0:T(8,128)S(1)}) custom-call(bf16[512,128]{1,0:T(8,128)(2,1)S(1)} %get-tuple-element.45.features_ref, bf16[512,512]{1,0:T(8,128)(2,1)S(1)} %get-tuple-element.51.local_ref, bf16[512,256]{1,0:T(8,128)(2,1)S(1)} %get-tuple-element.49.bound_ref, s32[1,256]{1,0:T(1,128)S(1)} %get-tuple-element.56.target_ref, ...), custom_call_target="tpu_custom_call" | custom-call | tf_op jit(solution)/shard_map/pallas_call | solution.py:41
  16.9 0.0 collective-permute-done.5.refs_0_
  16.9 1.0 %collective-permute-start.7 = (bf16[384,128]{1,0:T(8,128)(2,1)S(1)}, bf16[384,128]{1,0:T(8,128)(2,1)S(1)}, u32[]{:S(2)}, u32[]{:S(2)}) collective-permute-start(bf16[384,128]{1,0:T(8,128)(2,1)S(1)} %collective-permute-done.5.refs_0_), channel_id=1, source_target_pairs={{0,1},{1,0},{2,3},{3,2},{4,5},{5,4},{6,7},{7,6},{8,9},{9,8},{10,11... | collective-permute-start | bytes 294920 | tf_op jit(solution)/shard_map/ppermute | solution.py:340
  17.9 2.5 %collective-permute-done.6.got_ref = bf16[320,128]{1,0:T(8,128)(2,1)S(1)} collective-permute-done((bf16[320,128]{1,0:T(8,128)(2,1)S(1)}, bf16[320,128]{1,0:T(8,128)(2,1)S(1)}, u32[]{:S(2)}, u32[]{:S(2)}) %collective-permute-start.6) | collective-permute-done | bytes 81952 | tf_op jit(solution)/shard_map/ppermute | solution.py:340
  20.4 0.0 collective-permute-done.7.refs_1_
  20.4 0.1 shard_map.136
  20.5 1.6 %collective-permute-start.9 = (bf16[256,128]{1,0:T(8,128)(2,1)S(1)}, bf16[256,128]{1,0:T(8,128)(2,1)S(1)}, u32[]{:S(2)}, u32[]{:S(2)}) collective-permute-start(bf16[256,128]{1,0:T(8,128)(2,1)S(1)} %get-tuple-element.75.own_ref), channel_id=1, source_target_pairs={{0,8},{1,25},{2,10},{3,27},{4,12},{5,29},{6,14},{7,31},{8,0},{9,17... | collective-permute-start | bytes 196616 | tf_op jit(solution)/shard_map/ppermute | solution.py:340
  22.1 1.1 %collective-permute-start.8 = (bf16[256,128]{1,0:T(8,128)(2,1)S(1)}, bf16[256,128]{1,0:T(8,128)(2,1)S(1)}, u32[]{:S(2)}, u32[]{:S(2)}) collective-permute-start(bf16[256,128]{1,0:T(8,128)(2,1)S(1)} %get-tuple-element.75.own_ref), channel_id=1, source_target_pairs={{0,17},{1,16},{2,19},{3,18},{4,21},{5,20},{6,23},{7,22},{8,25},{9,... | collective-permute-start | bytes 196616 | tf_op jit(solution)/shard_map/ppermute | solution.py:340
  23.1 2.1 %collective-permute-done.9.refs_1_ = bf16[256,128]{1,0:T(8,128)(2,1)S(1)} collective-permute-done((bf16[256,128]{1,0:T(8,128)(2,1)S(1)}, bf16[256,128]{1,0:T(8,128)(2,1)S(1)}, u32[]{:S(2)}, u32[]{:S(2)}) %collective-permute-start.9) | collective-permute-done | bytes 65568 | tf_op jit(solution)/shard_map/ppermute | solution.py:340
  25.3 0.0 collective-permute-start.10
  25.3 0.9 %shard_map.137 = (bf16[512,128]{1,0:T(8,128)(2,1)}, bf16[512,128]{1,0:T(8,128)(2,1)}) custom-call(bf16[512,128]{1,0:T(8,128)(2,1)S(1)} %get-tuple-element.63.hidden_ref, bf16[512,64]{1,0:T(8,128)(2,1)S(1)} %get-tuple-element.64.place_ref, f32[512,128]{1,0:T(8,128)S(1)} %get-tuple-element.65.local_grad_ref, f32[64,128]{1,0:T(8,128)S(1)} %get-tuple-element.72.grads_ref), custom_call_target="tpu_custom_call" | custom-call | tf_op jit(solution)/shard_map/pallas_call | solution.py:41
  26.1 0.0 collective-permute-done.8.refs_0_
  26.1 0.4 %collective-permute-done.10.refs_2_ = bf16[256,128]{1,0:T(8,128)(2,1)S(1)} collective-permute-done((bf16[256,128]{1,0:T(8,128)(2,1)S(1)}, bf16[256,128]{1,0:T(8,128)(2,1)S(1)}, u32[]{:S(2)}, u32[]{:S(2)}) %collective-permute-start.10) | collective-permute-done | bytes 65568 | tf_op jit(solution)/shard_map/ppermute | solution.py:340
  26.5 0.7 %shard_map.138 = (f32[128,128]{1,0:T(8,128)}, f32[128,128]{1,0:T(8,128)}) custom-call(bf16[256,128]{1,0:T(8,128)(2,1)S(1)} %get-tuple-element.75.own_ref, bf16[256,128]{1,0:T(8,128)(2,1)S(1)} %collective-permute-done.8.refs_0_, bf16[256,128]{1,0:T(8,128)(2,1)S(1)} %collective-permute-done.9.refs_1_, bf16[256,128]{1,0:T(8,128)(2,1)S(1)} %collective-permute-done.10.refs_2_), custom_call_target="tpu_custom_call" | custom-call | tf_op jit(solution)/shard_map/pallas_call | solution.py:41
  (3 shorter events, 0.1 us)
Async XLA Ops:
  2.1 1.4 %collective-permute-start = (bf16[64,128]{1,0:T(8,128)(2,1)S(1)}, bf16[64,128]{1,0:T(8,128)(2,1)S(1)}, u32[]{:S(2)}, u32[]{:S(2)}) collective-permute-start(bf16[64,128]{1,0:T(8,128)(2,1)S(1)} %get-tuple-element.43.own_ref), channel_id=1, source_target_pairs={{0,1},{1,0},{2,3},{3,2},{4,5},{5,4},{6,7},{7,6},{8,9},{9,8},{10,11... | collective-permute-start | bytes 49160 | tf_op jit(solution)/shard_map/ppermute | solution.py:340
  3.4 7.5 %collective-permute-start.1 = (f32[64,1024]{1,0:T(8,128)S(1)}, f32[64,1024]{1,0:T(8,128)S(1)}, u32[]{:S(2)}, u32[]{:S(2)}) collective-permute-start(f32[64,1024]{1,0:T(8,128)S(1)} %get-tuple-element.53.pack_ref), channel_id=1, source_target_pairs={{0,1},{1,0},{2,3},{3,2},{4,5},{5,4},{6,7},{7,6},{8,9},{9,8},{10,11... | collective-permute-start | bytes 786440 | tf_op jit(solution)/shard_map/ppermute | solution.py:340
  3.8 5.9 %collective-permute-start.3 = (bf16[128,128]{1,0:T(8,128)(2,1)S(1)}, bf16[128,128]{1,0:T(8,128)(2,1)S(1)}, u32[]{:S(2)}, u32[]{:S(2)}) collective-permute-start(bf16[128,128]{1,0:T(8,128)(2,1)S(1)} %shard_map.131.pair_ref), channel_id=1, source_target_pairs={{0,4},{1,7},{2,6},{3,5},{4,0},{5,3},{6,2},{7,1},{8,12},{9,15},{10,... | collective-permute-start | bytes 98312 | tf_op jit(solution)/shard_map/ppermute | solution.py:340
  7.6 3.3 %collective-permute-start.2 = (bf16[128,128]{1,0:T(8,128)(2,1)S(1)}, bf16[128,128]{1,0:T(8,128)(2,1)S(1)}, u32[]{:S(2)}, u32[]{:S(2)}) collective-permute-start(bf16[128,128]{1,0:T(8,128)(2,1)S(1)} %shard_map.131.pair_ref), channel_id=1, source_target_pairs={{0,3},{1,2},{2,1},{3,0},{4,7},{5,6},{6,5},{7,4},{8,11},{9,10},{10,... | collective-permute-start | bytes 98312 | tf_op jit(solution)/shard_map/ppermute | solution.py:340
  9.7 1.3 %collective-permute-start.4 = (bf16[128,128]{1,0:T(8,128)(2,1)S(1)}, bf16[128,128]{1,0:T(8,128)(2,1)S(1)}, u32[]{:S(2)}, u32[]{:S(2)}) collective-permute-start(bf16[128,128]{1,0:T(8,128)(2,1)S(1)} %collective-permute-done.3.refs_1_), channel_id=1, source_target_pairs={{0,1},{1,0},{2,3},{3,2},{4,5},{5,4},{6,7},{7,6},{8,9},{9,8},{10,11... | collective-permute-start | bytes 98312 | tf_op jit(solution)/shard_map/ppermute | solution.py:340
  11.6 5.3 %collective-permute-start.5 = (bf16[384,128]{1,0:T(8,128)(2,1)S(1)}, bf16[384,128]{1,0:T(8,128)(2,1)S(1)}, u32[]{:S(2)}, u32[]{:S(2)}) collective-permute-start(bf16[384,128]{1,0:T(8,128)(2,1)S(1)} %get-tuple-element.55), channel_id=1, source_target_pairs={{0,2},{1,5},{2,0},{3,7},{4,6},{5,1},{6,4},{7,3},{8,10},{9,13},{10,... | collective-permute-start | bytes 294920 | tf_op jit(solution)/shard_map/ppermute | solution.py:340
  13.4 7.0 %collective-permute-start.6 = (bf16[320,128]{1,0:T(8,128)(2,1)S(1)}, bf16[320,128]{1,0:T(8,128)(2,1)S(1)}, u32[]{:S(2)}, u32[]{:S(2)}) collective-permute-start(bf16[320,128]{1,0:T(8,128)(2,1)S(1)} %get-tuple-element.68), channel_id=1, source_target_pairs={{0,7},{1,6},{2,5},{3,4},{4,3},{5,2},{6,1},{7,0},{8,15},{9,14},{10,... | collective-permute-start | bytes 245768 | tf_op jit(solution)/shard_map/ppermute | solution.py:340
  16.9 3.5 %collective-permute-start.7 = (bf16[384,128]{1,0:T(8,128)(2,1)S(1)}, bf16[384,128]{1,0:T(8,128)(2,1)S(1)}, u32[]{:S(2)}, u32[]{:S(2)}) collective-permute-start(bf16[384,128]{1,0:T(8,128)(2,1)S(1)} %collective-permute-done.5.refs_0_), channel_id=1, source_target_pairs={{0,1},{1,0},{2,3},{3,2},{4,5},{5,4},{6,7},{7,6},{8,9},{9,8},{10,11... | collective-permute-start | bytes 294920 | tf_op jit(solution)/shard_map/ppermute | solution.py:340
  20.5 4.8 %collective-permute-start.9 = (bf16[256,128]{1,0:T(8,128)(2,1)S(1)}, bf16[256,128]{1,0:T(8,128)(2,1)S(1)}, u32[]{:S(2)}, u32[]{:S(2)}) collective-permute-start(bf16[256,128]{1,0:T(8,128)(2,1)S(1)} %get-tuple-element.75.own_ref), channel_id=1, source_target_pairs={{0,8},{1,25},{2,10},{3,27},{4,12},{5,29},{6,14},{7,31},{8,0},{9,17... | collective-permute-start | bytes 196616 | tf_op jit(solution)/shard_map/ppermute | solution.py:340
  22.1 4.1 %collective-permute-start.8 = (bf16[256,128]{1,0:T(8,128)(2,1)S(1)}, bf16[256,128]{1,0:T(8,128)(2,1)S(1)}, u32[]{:S(2)}, u32[]{:S(2)}) collective-permute-start(bf16[256,128]{1,0:T(8,128)(2,1)S(1)} %get-tuple-element.75.own_ref), channel_id=1, source_target_pairs={{0,17},{1,16},{2,19},{3,18},{4,21},{5,20},{6,23},{7,22},{8,25},{9,... | collective-permute-start | bytes 196616 | tf_op jit(solution)/shard_map/ppermute | solution.py:340
  25.3 1.3 %collective-permute-start.10 = (bf16[256,128]{1,0:T(8,128)(2,1)S(1)}, bf16[256,128]{1,0:T(8,128)(2,1)S(1)}, u32[]{:S(2)}, u32[]{:S(2)}) collective-permute-start(bf16[256,128]{1,0:T(8,128)(2,1)S(1)} %collective-permute-done.9.refs_1_), channel_id=1, source_target_pairs={{0,1},{1,0},{2,3},{3,2},{4,5},{5,4},{6,7},{7,6},{8,9},{9,8},{10,11... | collective-permute-start | bytes 196616 | tf_op jit(solution)/shard_map/ppermute | solution.py:340
